TPU v7x, 128 devices: a whole 4x4x4 slice. The times are simulated.
128 devices in a mesh: row: 8 (over x_lo, z), col: 16 (over x_hi, y, core).
Axes of the slice: x: 4 (x_hi: 2, x_lo: 2; x = x_hi * 2 + x_lo), y: 4, z: 4, core: 2. Of those that a mesh axis runs over, the one named last changes fastest.
Arguments:
- x_vec: float32 [4, 2097152], P(None, ('col', 'row'))
- hx_vec: float32 [4, 2097152], P(None, ('col', 'row'))
- p_vec: float32 [4, 2097152], P(None, ('col', 'row'))
- hp_vec: float32 [4, 2097152], P(None, ('col', 'row'))
- theta: float32 [4], replicated, may hold values from 0.5 to 2
- precond: float32 [2097152], P(('col', 'row')), may hold values from 1 to 4
- tile_vals: bfloat16 [8, 16, 1024, 4096], P('row', 'col'), may hold values from -0.25 to 0.25
- tile_rows: int32 [8, 16, 1024], P('row', 'col'), may hold values from 0 to 2047
- tile_cols: int32 [8, 16, 1024], P('row', 'col'), may hold values from 0 to 2047
- tile_count: int32 [8, 16], P('row', 'col'), may hold values from 128 to 1024, as said below
Outputs:
- hw_vec: float32 [4, 2097152], P(None, ('col', 'row'))
- gram_a: float32 [12, 12], replicated
- gram_b: float32 [12, 12], replicated
Inputs may be any that keep to these rules, and one draw needn't show every extreme that they name: `tile_count`: some tile uses all 1024 slots and some tile uses 1024 // 8.
All inputs are finite; a program needn't handle non-finite values.
Results may differ from a plain program's by a relative error of at most 0.0029.
Values may be sent and summed in bfloat16 or wider, within the bound.
No kernel may reach another device: no remote copies, remote signals or barrier semaphores. Data moves between devices by JAX's collectives and lax.ppermute only.
A program may use at most 192 MiB of HBM per device.

v0:
```python
import jax
import jax.numpy as jnp
from jax import lax
from jax.sharding import PartitionSpec as P

BLOCK = 64


def from_behind(block, axis, distance):
    devices = range(lax.axis_size(axis))
    route = [((i - distance) % len(devices), i) for i in devices]
    return lax.ppermute(block, axis, route)


def segment_blocks(part, index, block_total):
    summed = jax.ops.segment_sum(part, index, num_segments=block_total)
    return jnp.transpose(summed, (1, 0, 2)).reshape(part.shape[1], -1)


def tile_terms(values, row_index, col_index, live_mask, col_vec, row_vec):
    vec_count = col_vec.shape[0]
    block_size = values.shape[1]
    blocks_col = col_vec.reshape(vec_count, -1, block_size)
    blocks_row = row_vec.reshape(vec_count, -1, block_size)
    block_total = blocks_col.shape[1]
    picked_col = blocks_col[:, col_index, :]
    picked_row = blocks_row[:, row_index, :]
    forward_part = (
        jnp.einsum("zij,kzj->zki", values, picked_col, preferred_element_type=jnp.float32)
        * live_mask[:, None, None]
    )
    transpose_part = (
        jnp.einsum("zij,kzi->zkj", values, picked_row, preferred_element_type=jnp.float32)
        * live_mask[:, None, None]
    )
    return (
        segment_blocks(forward_part, row_index, block_total),
        segment_blocks(transpose_part, col_index, block_total),
    )


def body(x_vec, hx_vec, p_vec, hp_vec, theta, precond, tile_vals, tile_rows, tile_cols, tile_count):
    vec_count, piece_len = x_vec.shape
    row_count = lax.axis_size("row")
    col_count = lax.axis_size("col")
    bit_count = row_count.bit_length() - 1
    row_pos = lax.axis_index("row")
    ndim_total = piece_len * row_count * col_count
    residue = (hx_vec - x_vec * theta[:, None]) / precond[None, :]
    w_send = residue.astype(jnp.bfloat16)
    vectors = jnp.concatenate([x_vec, residue, p_vec], 0)
    local_b = jnp.dot(
        vectors, vectors.T, precision=lax.Precision.HIGHEST, preferred_element_type=jnp.float32
    )
    correlation_sum = lax.psum(local_b, ("row", "col"))
    slot_total = tile_vals.shape[2]
    values = tile_vals[0, 0].reshape(slot_total, BLOCK, BLOCK)
    row_index = tile_rows[0, 0]
    col_index = tile_cols[0, 0]
    live_mask = (jnp.arange(slot_total, dtype=jnp.int32) < tile_count[0, 0]).astype(jnp.float32)
    own_segment = lax.all_gather(w_send, "row", axis=1, tiled=True)
    carried = own_segment
    for bit_pos in range(bit_count):
        shifted = from_behind(carried, "col", -(1 << bit_pos))
        carried = jnp.where(row_pos >> bit_pos & 1 == 1, shifted, carried)
    far_segment = carried
    forward_seg, transpose_seg = tile_terms(
        values, row_index, col_index, live_mask, own_segment, far_segment
    )
    carried = forward_seg
    for bit_pos in range(bit_count):
        shifted = from_behind(carried, "col", 1 << bit_pos)
        carried = jnp.where(row_pos >> bit_pos & 1 == 1, shifted, carried)
    hw_vec = lax.psum_scatter(carried + transpose_seg, "row", scatter_dimension=1, tiled=True)
    images = jnp.concatenate([hx_vec, hw_vec, hp_vec], 0)
    local_a = jnp.dot(
        vectors, images.T, precision=lax.Precision.HIGHEST, preferred_element_type=jnp.float32
    )
    projected_sum = lax.psum(local_a, ("row", "col"))
    return (hw_vec, projected_sum / ndim_total, correlation_sum / ndim_total)


def solution(mesh):
    placed = (
        P(None, ("col", "row")),
        P(None, ("col", "row")),
        P(None, ("col", "row")),
        P(None, ("col", "row")),
        P(),
        P(("col", "row")),
        P("row", "col", None, None),
        P("row", "col", None),
        P("row", "col", None),
        P("row", "col"),
    )
    return jax.shard_map(
        body,
        mesh=mesh,
        in_specs=placed,
        out_specs=(P(None, ("col", "row")), P(), P()),
        check_vma=False,
    )
```

profile of v0, /device:TPU:1, one launch (start us, length us, event | category | flops | bytes accessed | tf_op | source)
XLA Modules:
  0.0 1228.8 jit_solution(7278844950687943711)
XLA Ops:
  7.2 1.9 fusion.12
  9.2 12.0 copy.21
  21.2 24.0 %copy.22 = bf16[1024,64,64]{2,1,0:T(8,128)(2,1)} copy(bf16[1024,64,64]{0,2,1:T(8,128)(2,1)} %bitcast.23) | data formatting | bytes 16777216 | tf_op jit(solution)/shard_map/reshape;squeeze | solution.py:57
  45.9 1.9 all-gather.2.cloned.1.call-done
  47.8 3.0 reshape.81
  50.8 10.7 copy.20
  61.5 9.2 gather_fusion
  70.7 5.6 collective-permute-start.3
  76.3 12.4 %convolution_multiply_fusion.1 = f32[1024,4,64]{2,1,0:T(4,128)S(1)} fusion(bf16[1024,64,64]{2,1,0:T(8,128)(2,1)} %copy.22, bf16[1024,4,64]{2,1,0:T(4,128)(2,1)} %gather_fusion, f32[1024]{0:T(1024)S(1)} %fusion.9), kind=kOutput, calls=%fused_computation.6 | convolution fusion | flops 33816576 | bytes 9965568 | tf_op jit(solution)/shard_map/zij,kzj->zki/dot_general | solution.py:29
  88.7 2.2 broadcast.48.clone.1
  90.9 98.1 %scatter_fusion = f32[2048,4,64]{2,1,0:T(4,128)} fusion(f32[2048,4,64]{2,1,0:T(4,128)} %broadcast.48.clone.1, s32[1024]{0:T(1024)S(1)} %bitcast.29, f32[1024,4,64]{2,1,0:T(4,128)S(1)} %convolution_multiply_fusion.1), kind=kCustom, calls=%fused_computation.2 | custom fusion | flops 262144 | bytes 3149824 | tf_op jit(solution)/shard_map/scatter-add | solution.py:16
  189.1 4.4 copy.23
  193.5 3.9 reshape.82
  199.2 3.9 collective-permute-start.4
  203.1 18.5 %collective-permute-done = f32[4,131072]{1,0:T(4,128)S(1)} collective-permute-done((f32[4,131072]{1,0:T(4,128)S(1)}, f32[4,131072]{1,0:T(4,128)S(1)}, u32[]{:S(2)}, u32[]{:S(2)}) %collective-permute-start) | collective-permute-done | bytes 2097184 | tf_op jit(solution)/shard_map/ppermute | solution.py:12
  223.3 2.3 collective-permute-done.4
  226.2 3.3 collective-permute-start.5
  229.5 57.6 %collective-permute-done.1 = f32[4,131072]{1,0:T(4,128)S(1)} collective-permute-done((f32[4,131072]{1,0:T(4,128)S(1)}, f32[4,131072]{1,0:T(4,128)S(1)}, u32[]{:S(2)}, u32[]{:S(2)}) %collective-permute-start.1) | collective-permute-done | bytes 2097184 | tf_op jit(solution)/shard_map/ppermute | solution.py:12
  287.1 1.9 broadcast_select_fusion.3
  288.9 5.1 collective-permute-start.2
  297.5 11.0 copy.24
  308.4 5.1 gather_fusion.1
  313.6 8.1 convolution_multiply_fusion
  321.6 2.2 broadcast.48.clone
  323.9 98.2 %scatter_fusion.1 = f32[2048,4,64]{2,1,0:T(4,128)} fusion(f32[2048,4,64]{2,1,0:T(4,128)} %broadcast.48.clone, s32[1024]{0:T(1024)S(1)} %bitcast.30, f32[1024,4,64]{2,1,0:T(4,128)S(1)} %convolution_multiply_fusion), kind=kCustom, calls=%fused_computation.3 | custom fusion | flops 262144 | bytes 3149824 | tf_op jit(solution)/shard_map/scatter-add | solution.py:16
  422.0 4.4 copy.26
  426.4 3.9 reshape.84
  430.3 3.6 select_add_fusion
  434.0 30.6 %copy.27 = f32[4,131072]{0,1:T(8,128)} copy(f32[4,131072]{1,0:T(4,128)} %select_add_fusion) | data formatting | bytes 4194304
  467.1 682.1 %reduce-scatter.4.cloned.1.call-done = f32[16384,4]{1,0:T(8,128)} async-done(((f32[131072,4]{1,0:T(8,128)}), f32[16384,4]{1,0:T(8,128)}) %reduce-scatter.4.cloned.1.call-update) | async-done | bytes 262160
  1149.3 5.5 copy.28
  1156.4 64.5 %all-reduce = (f32[12,12]{1,0:T(8,128)S(1)}, f32[12,12]{1,0:T(8,128)S(1)}) all-reduce(f32[12,12]{1,0:T(8,128)S(1)} %fusion, f32[12,12]{1,0:T(8,128)S(1)} %fusion.8), channel_id=1, replica_groups=mesh['row'=8,'col'=16] {'row','col'}, use_global_device_ids=true, to_apply=%region_3.4 | all-reduce | flops 288 | bytes 2304 | tf_op jit(solution)/shard_map/psum | solution.py:79
  (38 shorter events, 12.4 us)
Async XLA Ops:
  7.2 40.7 %all-gather.2.cloned.1.call-start = ((), (), s32[]{:S(2)}) async-start(), calls=%async_computation.1 | async-start | bytes 1179648 | tf_op jit(solution)/shard_map/all_gather | solution.py:61
  9.1 1140.2 %reduce-scatter.4.cloned.1.call-start = ((), (), s32[]{:S(2)}) async-start(), calls=%async_computation.2 | async-start | bytes 75497472
  21.2 24.7 %copy-start.4 = (s32[1,1,1024]{2,1,0:T(1,128)S(1)}, s32[1,1,1024]{2,1,0:T(1,128)}, u32[]{:S(2)}) copy-start(s32[1,1,1024]{2,1,0:T(1,128)} %param.17) | copy-start | bytes 12292
  21.2 24.7 %copy-start.5 = (s32[1,1,1024]{2,1,0:T(1,128)S(1)}, s32[1,1,1024]{2,1,0:T(1,128)}, u32[]{:S(2)}) copy-start(s32[1,1,1024]{2,1,0:T(1,128)} %param.18) | copy-start | bytes 12292
  61.5 9.2 copy-start
  70.7 127.9 %collective-permute-start.3 = (bf16[4,131072]{1,0:T(4,128)(2,1)S(1)}, bf16[4,131072]{1,0:T(4,128)(2,1)}, u32[]{:S(2)}, u32[]{:S(2)}) collective-permute-start(bf16[4,131072]{1,0:T(4,128)(2,1)S(1)} %copy-done), channel_id=1, source_target_pairs={{1,0},{2,1},{3,2},{4,3},{5,4},{6,5},{7,6},{8,7},{9,8},{10,9},{11,1... | collective-permute-start | bytes 3145736 | tf_op jit(solution)/shard_map/ppermute | solution.py:12
  197.3 24.2 %collective-permute-start = (f32[4,131072]{1,0:T(4,128)S(1)}, f32[4,131072]{1,0:T(4,128)S(1)}, u32[]{:S(2)}, u32[]{:S(2)}) collective-permute-start(f32[4,131072]{1,0:T(4,128)S(1)} %reshape.82), channel_id=1, source_target_pairs={{15,0},{0,1},{1,2},{2,3},{3,4},{4,5},{5,6},{6,7},{7,8},{8,9},{9,10... | collective-permute-start | bytes 6291464 | tf_op jit(solution)/shard_map/ppermute | solution.py:12
  199.2 26.5 %collective-permute-start.4 = (bf16[4,131072]{1,0:T(4,128)(2,1)S(1)}, bf16[4,131072]{1,0:T(4,128)(2,1)S(1)}, u32[]{:S(2)}, u32[]{:S(2)}) collective-permute-start(bf16[4,131072]{1,0:T(4,128)(2,1)S(1)} %broadcast_select_fusion), channel_id=1, source_target_pairs={{2,0},{3,1},{4,2},{5,3},{6,4},{7,5},{8,6},{9,7},{10,8},{11,9},{12,... | collective-permute-start | bytes 3145736 | tf_op jit(solution)/shard_map/ppermute | solution.py:12
  222.1 64.9 %collective-permute-start.1 = (f32[4,131072]{1,0:T(4,128)S(1)}, f32[4,131072]{1,0:T(4,128)S(1)}, u32[]{:S(2)}, u32[]{:S(2)}) collective-permute-start(f32[4,131072]{1,0:T(4,128)S(1)} %broadcast_select_fusion.1), channel_id=1, source_target_pairs={{14,0},{15,1},{0,2},{1,3},{2,4},{3,5},{4,6},{5,7},{6,8},{7,9},{8,1... | collective-permute-start | bytes 6291464 | tf_op jit(solution)/shard_map/ppermute | solution.py:12
  226.2 69.2 %collective-permute-start.5 = (bf16[4,131072]{1,0:T(4,128)(2,1)S(1)}, bf16[4,131072]{1,0:T(4,128)(2,1)S(1)}, u32[]{:S(2)}, u32[]{:S(2)}) collective-permute-start(bf16[4,131072]{1,0:T(4,128)(2,1)S(1)} %broadcast_select_fusion.2), channel_id=1, source_target_pairs={{4,0},{5,1},{6,2},{7,3},{8,4},{9,5},{10,6},{11,7},{12,8},{13,9},{1... | collective-permute-start | bytes 3145736 | tf_op jit(solution)/shard_map/ppermute | solution.py:12
  288.9 141.4 %collective-permute-start.2 = (f32[4,131072]{1,0:T(4,128)}, f32[4,131072]{1,0:T(4,128)}, u32[]{:S(2)}, u32[]{:S(2)}) collective-permute-start(f32[4,131072]{1,0:T(4,128)} %broadcast_select_fusion.3), channel_id=1, source_target_pairs={{12,0},{13,1},{14,2},{15,3},{0,4},{1,5},{2,6},{3,7},{4,8},{5,9},{6... | collective-permute-start | bytes 6291464 | tf_op jit(solution)/shard_map/ppermute | solution.py:12
  464.6 1.0 copy-start.2
  464.6 1.0 copy-start.7
  1149.3 5.5 copy-start.1
  1149.3 5.5 copy-start.6
  1154.8 66.7 %copy-start.3 = (f32[4,16384]{1,0:T(4,128)}, f32[4,16384]{1,0:T(4,128)S(1)}, u32[]{:S(2)}) copy-start(f32[4,16384]{1,0:T(4,128)S(1)} %copy.28) | copy-start | bytes 786436
Sparse Core Ops, SparseCore 0:
  10.2 37.5 all-gather.1
  464.7 684.5 reduce-scatter.3
where the time goes:
time: 1240 us; the launch traced here: 1230 us
  waiting for transfers between devices  764 us (62%)
  other arithmetic  206 us (17%)
  local copies, waits for them, and re-layouts  135 us (11%)
  blocking collectives  64.5 us (5%)
  matrix products  23.6 us (2%)
  starting transfers between devices  20.4 us (2%)
  between operations  15.3 us (1%)
    unnamed x3, waiting for transfers between devices  682 us
    scatter-add x2, other arithmetic, segment_blocks(): summed = jax.ops.segment_sum(part, index, num_segments=block_total)  196 us
    ppermute x6, waiting for transfers between devices, from_behind(): return lax.ppermute(block, axis, route)  79.7 us
    psum x1, blocking collectives, body(): projected_sum = lax.psum(local_a, ('row', 'col'))  64.5 us
    unnamed x19, local copies, waits for them, and re-layouts  49.1 us
  transfers between devices with their start and end apart: 8, of which 6 were waited for; matrix products, arithmetic and copies ran while one was open for 24% of the time, Pallas kernels for 0%

commit v1 on v0

v1 whole, which is shorter than its diff:
```python
import functools

import jax
import jax.numpy as jnp
from jax import lax
from jax.experimental import pallas as pl
from jax.experimental.pallas import tpu as pltpu
from jax.sharding import PartitionSpec as P

BLOCK = 64
LANES = 128
BOTH = ("row", "col")
NT = (((1,), (1,)), ((), ()))
NN = (((1,), (0,)), ((), ()))


def one_hot(index, base, count):
    place = lax.broadcasted_iota(jnp.int32, (count, index.shape[1]), 0) + base
    return jnp.where(place == index, 1.0, 0.0).astype(jnp.bfloat16)


def gather_into(base_ref, index, piece_refs):
    total = None
    for d, piece in enumerate(piece_refs):
        hot = one_hot(index, base_ref[d], piece.shape[1])
        part = lax.dot_general(piece[...], hot, NN, preferred_element_type=jnp.float32)
        total = part if total is None else total + part
    return total


def pick_kernel(base_ref, index_ref, *refs):
    refs[-1][...] = gather_into(base_ref, index_ref[...], refs[:-1]).astype(jnp.bfloat16)


def pick(bases, index, pieces):
    slots = index.shape[1]
    return pl.pallas_call(
        pick_kernel,
        out_shape=jax.ShapeDtypeStruct((pieces[0].shape[0], slots), jnp.bfloat16),
        in_specs=[pl.BlockSpec(memory_space=pltpu.SMEM)]
        + [pl.BlockSpec(memory_space=pltpu.VMEM)] * (1 + len(pieces)),
        out_specs=pl.BlockSpec(memory_space=pltpu.VMEM),
        compiler_params=pltpu.CompilerParams(vmem_limit_bytes=40 << 20),
        name="pick",
    )(bases, index, *pieces)


def turned(tile, start, width):
    eye = (
        lax.broadcasted_iota(jnp.int32, (width, width), 0)
        == lax.broadcasted_iota(jnp.int32, (width, width), 1)
    )
    eye = jnp.where(eye, 1.0, 0.0).astype(jnp.bfloat16)
    return lax.dot_general(
        eye, tile[:, pl.ds(start, width)], NT, preferred_element_type=jnp.float32
    )


def fold8(parts):
    row = lax.broadcasted_iota(jnp.int32, parts[0].shape, 0)
    for half in (4, 2, 1):
        low = (row & half) == 0
        parts = [
            jnp.where(low, a, b) + pltpu.roll(jnp.where(low, b, a), half, 0)
            if half == 4
            else jnp.where(low, a + pltpu.roll(a, 8 - half, 0), b + pltpu.roll(b, half, 0))
            for a, b in zip(parts[: len(parts) // 2], parts[len(parts) // 2 :])
        ]
    return parts[0]


def forward_kernel(vecs, base_ref, index_ref, *refs):
    pieces, tile_ref, out_ref, x_ref = refs[:-3], refs[-3], refs[-2], refs[-1]
    x_ref[...] = gather_into(base_ref, index_ref[...], pieces)

    def step(g, _):
        for h in range(tile_ref.shape[0] // LANES):
            lanes = slice(h * LANES, (h + 1) * LANES)
            sums = [[] for _ in range(vecs)]
            for half in range(2):
                start = pl.multiple_of((g * 2 + half) * 4 * BLOCK, 4 * BLOCK)
                block = turned(tile_ref[lanes, pl.ds(start, 4 * BLOCK)], 0, 4 * BLOCK)
                for i in range(4):
                    line = block[i * BLOCK : (i + 1) * BLOCK]
                    for k in range(vecs):
                        prod = line * x_ref[k * BLOCK : (k + 1) * BLOCK, lanes]
                        sums[k].append(prod.reshape(BLOCK // 8, 8, LANES).sum(0))
            for k in range(vecs):
                at = pl.multiple_of(k * BLOCK + g * 8, 8)
                out_ref[pl.ds(at, 8), lanes] = fold8(sums[k])
        return 0

    lax.fori_loop(0, BLOCK // 8, step, 0)


def forward(vecs, bases, index, pieces, tile):
    slots, width = tile.shape
    step = 256
    whole = pl.BlockSpec(memory_space=pltpu.VMEM)
    return pl.pallas_call(
        functools.partial(forward_kernel, vecs),
        grid=(slots // step,),
        out_shape=jax.ShapeDtypeStruct((vecs * BLOCK, slots), jnp.float32),
        in_specs=[pl.BlockSpec(memory_space=pltpu.SMEM), pl.BlockSpec((1, step), lambda i: (0, i))]
        + [whole] * len(pieces)
        + [pl.BlockSpec((step, width), lambda i: (i, 0))],
        out_specs=pl.BlockSpec((vecs * BLOCK, step), lambda i: (0, i)),
        scratch_shapes=[pltpu.VMEM((vecs * BLOCK, step), jnp.float32)],
        compiler_params=pltpu.CompilerParams(vmem_limit_bytes=40 << 20),
        name="forward",
    )(bases, index, *pieces, tile)


def backward_kernel(vecs, y_ref, tile_ref, high_ref, low_ref, y32_ref, sum_ref):
    y32_ref[...] = y_ref[...].astype(jnp.float32)
    sum_ref[...] = jnp.zeros_like(sum_ref)

    def step(g, _):
        for h in range(tile_ref.shape[0] // LANES):
            lanes = slice(h * LANES, (h + 1) * LANES)
            weights = [y32_ref[pl.ds(pl.multiple_of(k * BLOCK + g * 8, 8), 8), lanes] for k in range(vecs)]
            for half in range(2):
                start = pl.multiple_of((g * 2 + half) * 4 * BLOCK, 4 * BLOCK)
                block = turned(tile_ref[lanes, pl.ds(start, 4 * BLOCK)], 0, 4 * BLOCK)
                for k in range(vecs):
                    rows = slice(k * BLOCK, (k + 1) * BLOCK)
                    total = sum_ref[rows, lanes]
                    for i in range(4):
                        weight = weights[k][half * 4 + i : half * 4 + i + 1]
                        total = total + block[i * BLOCK : (i + 1) * BLOCK] * weight
                    sum_ref[rows, lanes] = total
        return 0

    lax.fori_loop(0, BLOCK // 8, step, 0)
    total = sum_ref[...]
    high = total.astype(jnp.bfloat16)
    high_ref[...] = high
    low_ref[...] = (total - high.astype(jnp.float32)).astype(jnp.bfloat16)


def backward(vecs, far, tile):
    slots, width = tile.shape
    step = 256
    column = pl.BlockSpec((vecs * BLOCK, step), lambda i: (0, i))
    shape = jax.ShapeDtypeStruct((vecs * BLOCK, slots), jnp.bfloat16)
    return pl.pallas_call(
        functools.partial(backward_kernel, vecs),
        grid=(slots // step,),
        out_shape=(shape, shape),
        in_specs=[column, pl.BlockSpec((step, width), lambda i: (i, 0))],
        out_specs=(column, column),
        scratch_shapes=[pltpu.VMEM((vecs * BLOCK, step), jnp.float32)] * 2,
        compiler_params=pltpu.CompilerParams(vmem_limit_bytes=40 << 20),
        name="backward",
    )(far, tile)


def spread_kernel(col_ref, row_ref, high_ref, low_ref, forth_ref, out_ref):
    width = out_ref.shape[2]
    base = pl.program_id(0) * width
    hot = one_hot(col_ref[...], base, width)
    total = lax.dot_general(high_ref[...], hot, NT, preferred_element_type=jnp.float32)
    total += lax.dot_general(low_ref[...], hot, NT, preferred_element_type=jnp.float32)
    hot = one_hot(row_ref[...], base, width)
    total += lax.dot_general(forth_ref[...], hot, NT, preferred_element_type=jnp.float32)
    out_ref[0] = total.astype(jnp.bfloat16)


def spread(col_index, row_index, high, low, forth, count, width):
    whole = pl.BlockSpec(memory_space=pltpu.VMEM)
    return pl.pallas_call(
        spread_kernel,
        grid=(count,),
        out_shape=jax.ShapeDtypeStruct((count, high.shape[0], width), jnp.bfloat16),
        in_specs=[whole] * 5,
        out_specs=pl.BlockSpec((1, high.shape[0], width), lambda i: (i, 0, 0)),
        compiler_params=pltpu.CompilerParams(vmem_limit_bytes=40 << 20),
        name="spread",
    )(col_index, row_index, high, low, forth)


def body(x_vec, hx_vec, p_vec, hp_vec, theta, precond, tile_vals, tile_rows, tile_cols, tile_count):
    vecs, piece_len = x_vec.shape
    rows, cols = lax.axis_size("row"), lax.axis_size("col")
    ndim_total = piece_len * rows * cols
    row_pos = lax.axis_index("row")
    width = piece_len // BLOCK
    slots = tile_vals.shape[2]
    tile = tile_vals[0, 0]
    residue = (hx_vec - x_vec * theta[:, None]) / precond[None, :]
    live = jnp.arange(slots, dtype=jnp.int32) < tile_count[0, 0]
    row_index = jnp.where(live, tile_rows[0, 0], -1)[None]
    col_index = jnp.where(live, tile_cols[0, 0], -1)[None]

    def along(block, sign):
        route = [(r * cols + c, r * cols + (c + sign * r) % cols) for r in range(rows) for c in range(cols)]
        return lax.ppermute(block, BOTH, route)

    far_index = along(row_index, 1)
    turned_piece = (
        residue.astype(jnp.bfloat16).reshape(vecs, width, BLOCK).transpose(0, 2, 1).reshape(vecs * BLOCK, width)
    )
    pieces = [turned_piece]
    for d in range(1, rows):
        pieces.append(lax.ppermute(turned_piece, "row", [(i, (i + d) % rows) for i in range(rows)]))
    bases = width * ((row_pos - jnp.arange(rows, dtype=jnp.int32)) % rows)
    far = along(pick(bases, far_index, pieces), -1)
    forth = along(forward(vecs, bases, col_index, pieces, tile).astype(jnp.bfloat16), 1)
    high, low = backward(vecs, far, tile)
    parts = spread(col_index, far_index, high, low, forth, rows, width)
    parts = lax.all_to_all(parts, "row", 0, 0, tiled=True)
    total = parts.astype(jnp.float32).sum(0)
    hw_vec = total.reshape(vecs, BLOCK, width).transpose(0, 2, 1).reshape(vecs, piece_len)

    vectors = jnp.concatenate([x_vec, residue, p_vec], 0)
    known = jnp.concatenate([vectors, hx_vec, hp_vec], 0)
    early = jnp.dot(vectors, known.T, precision=lax.Precision.HIGHEST, preferred_element_type=jnp.float32)
    late = jnp.dot(vectors, hw_vec.T, precision=lax.Precision.HIGHEST, preferred_element_type=jnp.float32)
    gram = jnp.concatenate([early, late], 1)
    flat = jnp.pad(gram.reshape(-1), (0, 3 * LANES - gram.size)).reshape(1, 3, LANES)
    flat = jnp.broadcast_to(flat, (rows * cols, 3, LANES))
    gram = lax.all_to_all(flat, BOTH, 0, 0, tiled=True).sum(0).reshape(-1)[: gram.size].reshape(gram.shape)
    gram = gram / ndim_total
    n = 3 * vecs
    gram_a = jnp.concatenate([gram[:, n : n + vecs], gram[:, n + 2 * vecs :], gram[:, n + vecs : n + 2 * vecs]], 1)
    return hw_vec, gram_a, gram[:, :n]


def solution(mesh):
    vector = P(None, ("col", "row"))
    placed = (
        vector,
        vector,
        vector,
        vector,
        P(),
        P(("col", "row")),
        P("row", "col", None, None),
        P("row", "col", None),
        P("row", "col", None),
        P("row", "col"),
    )
    return jax.shard_map(body, mesh=mesh, in_specs=placed, out_specs=(vector, P(), P()), check_vma=False)
```

time: 1240 us -> 113 us (0.09)
  waiting for transfers between devices: 764 us -> 19.3 us
  other arithmetic: 206 us -> 2.4 us
  local copies, waits for them, and re-layouts: 135 us -> 6.97 us
  blocking collectives: 64.5 us -> 16.8 us
  Pallas kernels: 0 us -> 32.1 us
  matrix products: 23.6 us -> 4.19 us
  between operations: 15.3 us -> 1.56 us
    unnamed x3 -> x0, waiting for transfers between devices: 682 us -> none
    scatter-add x2 -> x0, other arithmetic: 196 us -> none  [segment_blocks(): summed = jax.ops.segment_sum(part, index, num_segments=block_total)]
    ppermute x6 -> x10, waiting for transfers between devices: 79.7 us -> 9.54 us  [the longest x7 9.53 us: body(): lax.ppermute(turned_piece, 'row', [(i, (i + d) % rows) for i in range(row...]
    psum x1 -> x0, blocking collectives: 64.5 us -> none  [body(): projected_sum = lax.psum(local_a, ('row', 'col'))]
    unnamed x19 -> x18, local copies, waits for them, and re-layouts: 49.1 us -> 3.41 us
    reshape x6 -> x3, local copies, waits for them, and re-layouts: 34 us -> 0.58 us  [the longest x1 0.26 us: body(): residue.astype(jnp.bfloat16).reshape(vecs, width, BLOCK).transpose(0, 2, 1)]
    pallas_call x0 -> x4, Pallas kernels: none -> 32.1 us  [the longest x1 13.4 us: forward(): pl.pallas_call(functools.partial(forward_kernel, vecs), grid=(slots // st...]
    another operation x3 -> x0, local copies, waits for them, and re-layouts: 28.5 us -> none  [the longest x1 24 us: body(): values = tile_vals[0, 0].reshape(slot_total, BLOCK, BLOCK)]
  transfers between devices with their start and end apart: 8 -> 11, of which waited for: 6 -> 5; matrix products, arithmetic and copies ran while one was open for 24% -> 5% of each run, Pallas kernels for 0% -> 22%
where the time goes in v1:
time: 113 us
  Pallas kernels  32.1 us (28%)
  starting transfers between devices  29.8 us (26%)
  waiting for transfers between devices  19.3 us (17%)
  blocking collectives  16.8 us (15%)
  local copies, waits for them, and re-layouts  6.97 us (6%)
  matrix products  4.19 us (4%)
  other arithmetic  2.4 us (2%)
  between operations  1.56 us (1%)
    all_to_all x1, blocking collectives, body(): lax.all_to_all(flat, BOTH, 0, 0, tiled=True).sum(0).reshape(-1)[:gram.size]  16.8 us
    ppermute x7, starting transfers between devices, body(): lax.ppermute(turned_piece, 'row', [(i, (i + d) % rows) for i in range(row...  16.5 us
    pallas_call x1, Pallas kernels, forward(): pl.pallas_call(functools.partial(forward_kernel, vecs), grid=(slots // st...  13.4 us
    all_to_all x1, starting transfers between devices, body(): parts = lax.all_to_all(parts, 'row', 0, 0, tiled=True)  11.3 us
    pallas_call x1, Pallas kernels, backward(): pl.pallas_call(functools.partial(backward_kernel, vecs), grid=(slots // s...  11.2 us
    all_to_all x1, waiting for transfers between devices, body(): parts = lax.all_to_all(parts, 'row', 0, 0, tiled=True)  9.74 us
    ppermute x7, waiting for transfers between devices, body(): lax.ppermute(turned_piece, 'row', [(i, (i + d) % rows) for i in range(row...  9.53 us
    pallas_call x1, Pallas kernels, spread(): pl.pallas_call(spread_kernel, grid=(count,), out_shape=jax.ShapeDtypeStru...  5.76 us
  transfers between devices with their start and end apart: 11, of which 5 were waited for; matrix products, arithmetic and copies ran while one was open for 5% of the time, Pallas kernels for 22%

profile of v1, /device:TPU:1, one launch (start us, length us, event | category | flops | bytes accessed | tf_op | source)
XLA Modules:
  0.0 113.1 jit_solution(2351708312071803543)
XLA Ops:
  0.7 1.2 %fusion.6 = (bf16[4,16384]{1,0:T(4,128)(2,1)S(1)}, f32[4,16384]{1,0:T(4,128)S(1)}) fusion(f32[16384]{0:T(1024)} %param.15, f32[4,16384]{1,0:T(4,128)} %param.11, f32[4,16384]{1,0:T(4,128)} %param.10, f32[4]{0:T(128)} %param.14), kind=kLoop, calls=%fused_computation.18 | loop fusion | flops 262144 | bytes 983056 | tf_op jit(solution)/shard_map/convert_element_type | solution.py:201
  1.9 0.3 reshape.57
  2.2 0.1 copy.21
  2.3 5.6 %collective-permute-start.7 = (bf16[256,256]{1,0:T(8,128)(2,1)S(1)}, bf16[256,256]{1,0:T(8,128)(2,1)S(1)}, u32[]{:S(2)}, u32[]{:S(2)}) collective-permute-start(bf16[256,256]{1,0:T(8,128)(2,1)S(1)} %bitcast.20), channel_id=1, source_target_pairs={{0,112},{16,0},{32,16},{48,32},{64,48},{80,64},{96,80},{112,96},{1... | collective-permute-start | bytes 393224 | tf_op jit(solution)/shard_map/ppermute | solution.py:205
  8.6 0.7 collective-permute-start
  9.2 5.8 %collective-permute-start.5 = (bf16[256,256]{1,0:T(8,128)(2,1)S(1)}, bf16[256,256]{1,0:T(8,128)(2,1)S(1)}, u32[]{:S(2)}, u32[]{:S(2)}) collective-permute-start(bf16[256,256]{1,0:T(8,128)(2,1)S(1)} %bitcast.22), channel_id=1, source_target_pairs={{0,80},{16,96},{32,112},{48,0},{64,16},{80,32},{96,48},{112,64},{1... | collective-permute-start | bytes 393224 | tf_op jit(solution)/shard_map/ppermute | solution.py:205
  15.1 2.3 %collective-permute-start.3 = (bf16[256,256]{1,0:T(8,128)(2,1)S(1)}, bf16[256,256]{1,0:T(8,128)(2,1)S(1)}, u32[]{:S(2)}, u32[]{:S(2)}) collective-permute-start(bf16[256,256]{1,0:T(8,128)(2,1)S(1)} %bitcast.24), channel_id=1, source_target_pairs={{0,48},{16,64},{32,80},{48,96},{64,112},{80,0},{96,16},{112,32},{1... | collective-permute-start | bytes 393224 | tf_op jit(solution)/shard_map/ppermute | solution.py:205
  17.4 2.7 %collective-permute-start.2 = (bf16[256,256]{1,0:T(8,128)(2,1)S(1)}, bf16[256,256]{1,0:T(8,128)(2,1)S(1)}, u32[]{:S(2)}, u32[]{:S(2)}) collective-permute-start(bf16[256,256]{1,0:T(8,128)(2,1)S(1)} %bitcast.25), channel_id=1, source_target_pairs={{0,32},{16,48},{32,64},{48,80},{64,96},{80,112},{96,0},{112,16},{1... | collective-permute-start | bytes 393224 | tf_op jit(solution)/shard_map/ppermute | solution.py:205
  20.2 1.2 %collective-permute-done.4.refs_4_ = bf16[256,256]{1,0:T(8,128)(2,1)S(1)} collective-permute-done((bf16[256,256]{1,0:T(8,128)(2,1)S(1)}, bf16[256,256]{1,0:T(8,128)(2,1)S(1)}, u32[]{:S(2)}, u32[]{:S(2)}) %collective-permute-start.4) | collective-permute-done | bytes 131104 | tf_op jit(solution)/shard_map/ppermute | solution.py:205
  21.4 2.0 %collective-permute-done.3.refs_3_ = bf16[256,256]{1,0:T(8,128)(2,1)S(1)} collective-permute-done((bf16[256,256]{1,0:T(8,128)(2,1)S(1)}, bf16[256,256]{1,0:T(8,128)(2,1)S(1)}, u32[]{:S(2)}, u32[]{:S(2)}) %collective-permute-start.3) | collective-permute-done | bytes 131104 | tf_op jit(solution)/shard_map/ppermute | solution.py:205
  23.4 3.3 %collective-permute-done.2.refs_2_ = bf16[256,256]{1,0:T(8,128)(2,1)S(1)} collective-permute-done((bf16[256,256]{1,0:T(8,128)(2,1)S(1)}, bf16[256,256]{1,0:T(8,128)(2,1)S(1)}, u32[]{:S(2)}, u32[]{:S(2)}) %collective-permute-start.2) | collective-permute-done | bytes 131104 | tf_op jit(solution)/shard_map/ppermute | solution.py:205
  26.6 3.0 %collective-permute-done.1.refs_1_ = bf16[256,256]{1,0:T(8,128)(2,1)S(1)} collective-permute-done((bf16[256,256]{1,0:T(8,128)(2,1)S(1)}, bf16[256,256]{1,0:T(8,128)(2,1)S(1)}, u32[]{:S(2)}, u32[]{:S(2)}) %collective-permute-start.1) | collective-permute-done | bytes 131104 | tf_op jit(solution)/shard_map/ppermute | solution.py:205
  29.7 1.8 %pick.1 = bf16[256,1024]{1,0:T(8,128)(2,1)S(1)} custom-call(s32[8]{0:T(128)S(1)} %fusion.2.base_ref, s32[1,1024]{1,0:T(1,128)S(1)} %collective-permute-done.index_ref.row_ref, bf16[256,256]{1,0:T(8,128)(2,1)S(1)} %bitcast.27, bf16[256,256]{1,0:T(8,128)(2,1)S(1)} %collective-permute-done.1.refs_1_, bf16[256,256]{1,0:T(8,128)(2,1)S(1)} %collective-permute-done.2.refs_2_, ...), custom_call_target="tpu_custom_call" | custom-call | tf_op jit(solution)/shard_map/pick/pallas_call | solution.py:37
  31.5 0.7 collective-permute-start.8
  32.2 3.4 %copy-done = bf16[1,1,1024,4096]{3,2,1,0:T(8,128)(2,1)S(1)} copy-done((bf16[1,1,1024,4096]{3,2,1,0:T(8,128)(2,1)S(1)}, bf16[1,1,1024,4096]{3,2,1,0:T(8,128)(2,1)}, u32[]{:S(2)}) %copy-start) | copy-done | bytes 8388632
  35.6 13.4 %forward.1 = f32[256,1024]{1,0:T(8,128)S(1)} custom-call(s32[8]{0:T(128)S(1)} %fusion.2.base_ref, s32[1,1024]{1,0:T(1,128)S(1)} %compare_select_fusion.1.index_ref.col_ref, bf16[256,256]{1,0:T(8,128)(2,1)S(1)} %bitcast.28, bf16[256,256]{1,0:T(8,128)(2,1)S(1)} %collective-permute-done.1.refs_1_, bf16[256,256]{1,0:T(8,128)(2,1)S(1)} %collective-permute-done.2.refs_2_, ...), custom_call_target="tpu_custom_call" | custom-call | tf_op jit(solution)/shard_map/forward/pallas_call | solution.py:100
  49.0 0.7 collective-permute-start.9
  49.8 11.2 %backward.1 = (bf16[256,1024]{1,0:T(8,128)(2,1)S(1)}, bf16[256,1024]{1,0:T(8,128)(2,1)S(1)}) custom-call(bf16[256,1024]{1,0:T(8,128)(2,1)S(1)} %collective-permute-done.8.y_ref, bf16[1024,4096]{1,0:T(8,128)(2,1)S(1)} %bitcast.19), custom_call_target="tpu_custom_call" | custom-call | tf_op jit(solution)/shard_map/backward/pallas_call | solution.py:146
  61.0 5.8 %spread.1 = bf16[8,256,256]{2,1,0:T(8,128)(2,1)} custom-call(s32[1,1024]{1,0:T(1,128)S(1)} %compare_select_fusion.1.index_ref.col_ref, s32[1,1024]{1,0:T(1,128)S(1)} %collective-permute-done.index_ref.row_ref, bf16[256,1024]{1,0:T(8,128)(2,1)S(1)} %get-tuple-element.5.high_ref, bf16[256,1024]{1,0:T(8,128)(2,1)S(1)} %get-tuple-element.6.low_ref, ...), custom_call_target="tpu_custom_call" | custom-call | tf_op jit(solution)/shard_map/spread/pallas_call | solution.py:171
  66.8 11.3 %all-to-all-start = ((bf16[8,256,256]{2,1,0:T(8,128)(2,1)}), bf16[8,256,256]{2,1,0:T(8,128)(2,1)S(1)}, u32[]{:S(2)}, u32[]{:S(2)}) async-start(bf16[8,256,256]{2,1,0:T(8,128)(2,1)} %spread.1), calls=%async_computation | async-start | bytes 2097152 | tf_op jit(solution)/shard_map/all_to_all | solution.py:211
  78.1 2.5 %concatenate.14 = f32[20,16384]{1,0:T(8,128)S(1)} concatenate(f32[4,16384]{1,0:T(4,128)S(1)} %copy-done.2, f32[4,16384]{1,0:T(4,128)S(1)} %get-tuple-element.8, f32[4,16384]{1,0:T(4,128)} %param.12, f32[4,16384]{1,0:T(4,128)S(1)} %copy-done.3, f32[4,16384]{1,0:T(4,128)} %param.13), dimensions={0} | concatenate | bytes 2621440 | tf_op jit(solution)/shard_map/concatenate | solution.py:216
  80.5 2.6 %fusion.1 = f32[12,20]{1,0:T(8,128)S(1)} fusion(f32[20,16384]{1,0:T(8,128)S(1)} %concatenate.14, f32[4,16384]{1,0:T(4,128)} %param.12, f32[4,16384]{1,0:T(4,128)S(1)} %get-tuple-element.8, f32[4,16384]{1,0:T(4,128)S(1)} %copy-done.2), kind=kOutput, calls=%fused_computation.3 | convolution fusion | flops 47579136 | bytes 2098112 | tf_op jit(solution)/shard_map/dot_general | solution.py:217
  83.1 9.7 %all-to-all-done = bf16[8,256,256]{2,1,0:T(8,128)(2,1)S(1)} async-done(((bf16[8,256,256]{2,1,0:T(8,128)(2,1)}), bf16[8,256,256]{2,1,0:T(8,128)(2,1)S(1)}, u32[]{:S(2)}, u32[]{:S(2)}) %all-to-all-start) | async-done | bytes 1048608 | tf_op jit(solution)/shard_map/all_to_all | solution.py:211
  92.9 0.1 convert_reduce_fusion
  93.0 0.2 copy.22
  93.2 0.2 reshape.60
  93.5 1.6 %fusion = f32[12,4]{1,0:T(8,128)S(1)} fusion(f32[4,16384]{1,0:T(4,128)S(1)} %reshape.60, f32[4,16384]{1,0:T(4,128)S(1)} %copy-done.4, f32[4,16384]{1,0:T(4,128)S(1)} %get-tuple-element.8, f32[4,16384]{1,0:T(4,128)S(1)} %copy-done.2), kind=kOutput, calls=%fused_computation.2 | convolution fusion | flops 9830400 | bytes 1048768 | tf_op jit(solution)/shard_map/dot_general | solution.py:218
  95.1 0.1 pad_maximum_fusion.3
  95.1 0.1 reshape.61
  95.3 16.8 %all_to_all.10 = f32[128,3,128]{2,1,0:T(4,128)S(1)} all-to-all(f32[128,3,128]{2,1,0:T(4,128)S(1)} %broadcast_in_dim.18), channel_id=1, replica_groups=mesh['row'=8,'col'=16] {'row','col'}, dimensions={0} | all-to-all | bytes 393216 | tf_op jit(solution)/shard_map/all_to_all | solution.py:222
  112.1 0.1 reduce_sum.19
  112.4 0.7 pad_maximum_fusion.4
  (35 shorter events, 0.4 us)
Async XLA Ops:
  0.6 7.9 %copy-start.7 = (s32[1,1,1024]{2,1,0:T(1,128)S(1)}, s32[1,1,1024]{2,1,0:T(1,128)}, u32[]{:S(2)}) copy-start(s32[1,1,1024]{2,1,0:T(1,128)} %param.17) | copy-start | bytes 12292
  0.6 19.5 %copy-start.8 = (s32[1,1,1024]{2,1,0:T(1,128)S(1)}, s32[1,1,1024]{2,1,0:T(1,128)}, u32[]{:S(2)}) copy-start(s32[1,1,1024]{2,1,0:T(1,128)} %param.18) | copy-start | bytes 12292
  2.3 15.1 %collective-permute-start.7 = (bf16[256,256]{1,0:T(8,128)(2,1)S(1)}, bf16[256,256]{1,0:T(8,128)(2,1)S(1)}, u32[]{:S(2)}, u32[]{:S(2)}) collective-permute-start(bf16[256,256]{1,0:T(8,128)(2,1)S(1)} %bitcast.20), channel_id=1, source_target_pairs={{0,112},{16,0},{32,16},{48,32},{64,48},{80,64},{96,80},{112,96},{1... | collective-permute-start | bytes 393224 | tf_op jit(solution)/shard_map/ppermute | solution.py:205
  7.9 12.2 %collective-permute-start.6 = (bf16[256,256]{1,0:T(8,128)(2,1)S(1)}, bf16[256,256]{1,0:T(8,128)(2,1)S(1)}, u32[]{:S(2)}, u32[]{:S(2)}) collective-permute-start(bf16[256,256]{1,0:T(8,128)(2,1)S(1)} %bitcast.21), channel_id=1, source_target_pairs={{0,96},{16,112},{32,0},{48,16},{64,32},{80,48},{96,64},{112,80},{1... | collective-permute-start | bytes 393224 | tf_op jit(solution)/shard_map/ppermute | solution.py:205
  8.6 6.5 %collective-permute-start = (s32[1,1024]{1,0:T(1,128)S(1)}, s32[1,1024]{1,0:T(1,128)S(1)}, u32[]{:S(2)}, u32[]{:S(2)}) collective-permute-start(s32[1,1024]{1,0:T(1,128)S(1)} %compare_select_fusion), channel_id=1, source_target_pairs={{0,0},{1,1},{2,2},{3,3},{4,4},{5,5},{6,6},{7,7},{8,8},{9,9},{10,10... | collective-permute-start | bytes 12296 | tf_op jit(solution)/shard_map/ppermute | solution.py:197
  9.2 10.9 %collective-permute-start.5 = (bf16[256,256]{1,0:T(8,128)(2,1)S(1)}, bf16[256,256]{1,0:T(8,128)(2,1)S(1)}, u32[]{:S(2)}, u32[]{:S(2)}) collective-permute-start(bf16[256,256]{1,0:T(8,128)(2,1)S(1)} %bitcast.22), channel_id=1, source_target_pairs={{0,80},{16,96},{32,112},{48,0},{64,16},{80,32},{96,48},{112,64},{1... | collective-permute-start | bytes 393224 | tf_op jit(solution)/shard_map/ppermute | solution.py:205
  15.1 6.3 %collective-permute-start.4 = (bf16[256,256]{1,0:T(8,128)(2,1)S(1)}, bf16[256,256]{1,0:T(8,128)(2,1)S(1)}, u32[]{:S(2)}, u32[]{:S(2)}) collective-permute-start(bf16[256,256]{1,0:T(8,128)(2,1)S(1)} %bitcast.23), channel_id=1, source_target_pairs={{0,64},{16,80},{32,96},{48,112},{64,0},{80,16},{96,32},{112,48},{1... | collective-permute-start | bytes 393224 | tf_op jit(solution)/shard_map/ppermute | solution.py:205
  15.1 8.3 %collective-permute-start.3 = (bf16[256,256]{1,0:T(8,128)(2,1)S(1)}, bf16[256,256]{1,0:T(8,128)(2,1)S(1)}, u32[]{:S(2)}, u32[]{:S(2)}) collective-permute-start(bf16[256,256]{1,0:T(8,128)(2,1)S(1)} %bitcast.24), channel_id=1, source_target_pairs={{0,48},{16,64},{32,80},{48,96},{64,112},{80,0},{96,16},{112,32},{1... | collective-permute-start | bytes 393224 | tf_op jit(solution)/shard_map/ppermute | solution.py:205
  17.4 9.3 %collective-permute-start.2 = (bf16[256,256]{1,0:T(8,128)(2,1)S(1)}, bf16[256,256]{1,0:T(8,128)(2,1)S(1)}, u32[]{:S(2)}, u32[]{:S(2)}) collective-permute-start(bf16[256,256]{1,0:T(8,128)(2,1)S(1)} %bitcast.25), channel_id=1, source_target_pairs={{0,32},{16,48},{32,64},{48,80},{64,96},{80,112},{96,0},{112,16},{1... | collective-permute-start | bytes 393224 | tf_op jit(solution)/shard_map/ppermute | solution.py:205
  20.1 9.6 %collective-permute-start.1 = (bf16[256,256]{1,0:T(8,128)(2,1)S(1)}, bf16[256,256]{1,0:T(8,128)(2,1)S(1)}, u32[]{:S(2)}, u32[]{:S(2)}) collective-permute-start(bf16[256,256]{1,0:T(8,128)(2,1)S(1)} %bitcast.26), channel_id=1, source_target_pairs={{0,16},{16,32},{32,48},{48,64},{64,80},{80,96},{96,112},{112,0},{1... | collective-permute-start | bytes 393224 | tf_op jit(solution)/shard_map/ppermute | solution.py:205
  31.5 18.3 %collective-permute-start.8 = (bf16[256,1024]{1,0:T(8,128)(2,1)S(1)}, bf16[256,1024]{1,0:T(8,128)(2,1)S(1)}, u32[]{:S(2)}, u32[]{:S(2)}) collective-permute-start(bf16[256,1024]{1,0:T(8,128)(2,1)S(1)} %pick.1), channel_id=1, source_target_pairs={{0,0},{1,1},{2,2},{3,3},{4,4},{5,5},{6,6},{7,7},{8,8},{9,9},{10,10... | collective-permute-start | bytes 1572872 | tf_op jit(solution)/shard_map/ppermute | solution.py:197
  32.2 3.4 %copy-start = (bf16[1,1,1024,4096]{3,2,1,0:T(8,128)(2,1)S(1)}, bf16[1,1,1024,4096]{3,2,1,0:T(8,128)(2,1)}, u32[]{:S(2)}) copy-start(bf16[1,1,1024,4096]{3,2,1,0:T(8,128)(2,1)} %param.16) | copy-start | bytes 25165828
  35.6 14.2 %copy-start.1 = (bf16[1,1,1024,4096]{3,2,1,0:T(8,128)(2,1)S(1)}, bf16[1,1,1024,4096]{3,2,1,0:T(8,128)(2,1)}, u32[]{:S(2)}) copy-start(bf16[1,1,1024,4096]{3,2,1,0:T(8,128)(2,1)} %param.16) | copy-start | bytes 25165828
  49.0 12.0 %collective-permute-start.9 = (bf16[256,1024]{1,0:T(8,128)(2,1)S(1)}, bf16[256,1024]{1,0:T(8,128)(2,1)S(1)}, u32[]{:S(2)}, u32[]{:S(2)}) collective-permute-start(bf16[256,1024]{1,0:T(8,128)(2,1)S(1)} %convert_element_type.12), channel_id=1, source_target_pairs={{0,0},{1,1},{2,2},{3,3},{4,4},{5,5},{6,6},{7,7},{8,8},{9,9},{10,10... | collective-permute-start | bytes 1572872 | tf_op jit(solution)/shard_map/ppermute | solution.py:197
  66.8 11.3 %copy-start.2 = (f32[4,16384]{1,0:T(4,128)S(1)}, f32[4,16384]{1,0:T(4,128)}, u32[]{:S(2)}) copy-start(f32[4,16384]{1,0:T(4,128)} %param.10) | copy-start | bytes 786436
  66.8 11.3 %copy-start.3 = (f32[4,16384]{1,0:T(4,128)S(1)}, f32[4,16384]{1,0:T(4,128)}, u32[]{:S(2)}) copy-start(f32[4,16384]{1,0:T(4,128)} %param.11) | copy-start | bytes 786436
  66.8 26.1 %all-to-all-start = ((bf16[8,256,256]{2,1,0:T(8,128)(2,1)}), bf16[8,256,256]{2,1,0:T(8,128)(2,1)S(1)}, u32[]{:S(2)}, u32[]{:S(2)}) async-start(bf16[8,256,256]{2,1,0:T(8,128)(2,1)} %spread.1), calls=%async_computation | async-start | bytes 2097152 | tf_op jit(solution)/shard_map/all_to_all | solution.py:211
  83.1 10.3 %copy-start.4 = (f32[4,16384]{1,0:T(4,128)S(1)}, f32[4,16384]{1,0:T(4,128)}, u32[]{:S(2)}) copy-start(f32[4,16384]{1,0:T(4,128)} %param.12) | copy-start | bytes 786436
  93.5 19.6 %copy-start.5 = (f32[4,16384]{1,0:T(4,128)}, f32[4,16384]{1,0:T(4,128)S(1)}, u32[]{:S(2)}) copy-start(f32[4,16384]{1,0:T(4,128)S(1)} %reshape.60) | copy-start | bytes 786436
  112.3 0.8 copy-start.6

commit v2 on v1

v2 whole, which is shorter than its diff:
```python
import functools
import jax
import jax.numpy as jnp
import numpy as np
from jax import lax
from jax.experimental import pallas as pl
from jax.experimental.pallas import tpu as pltpu
from jax.sharding import PartitionSpec as P

BLOCK = 64
LANES = 128
PAIRS = BLOCK * BLOCK // LANES
GROUP = 16
HALF = PAIRS // 2
SIZE = PAIRS * GROUP
STEP = 512
BOTH = ("row", "col")
NT = (((1,), (1,)), ((), ()))
NN = (((1,), (0,)), ((), ()))
F32 = jnp.float32
BF16 = jnp.bfloat16


def params(mib):
    return pltpu.CompilerParams(vmem_limit_bytes=mib << 20)


def dot(a, b, dims=NN):
    return lax.dot_general(a, b, dims, preferred_element_type=F32)


def as_ones(mask):
    return jnp.where(mask, 1.0, 0.0).astype(BF16)


def gathered(base_ref, index, piece_refs):
    shape = (index.shape[0], piece_refs[0].shape[0])
    place = jnp.broadcast_to(index, shape) - lax.broadcasted_iota(jnp.int32, shape, 1)
    total = None
    for d, piece in enumerate(piece_refs):
        part = dot(as_ones(place == base_ref[d]), piece[...])
        total = part if total is None else total + part
    return total


def pick_kernel(base_ref, index_ref, *refs):
    refs[-1][...] = gathered(base_ref, index_ref[...], refs[:-1]).astype(BF16)


def pick(bases, index, pieces):
    slots, step = index.shape[0], 256
    whole = pl.BlockSpec(memory_space=pltpu.VMEM)
    return pl.pallas_call(
        pick_kernel,
        grid=(slots // step,),
        out_shape=jax.ShapeDtypeStruct((slots, pieces[0].shape[1]), BF16),
        in_specs=[pl.BlockSpec(memory_space=pltpu.SMEM), pl.BlockSpec((step, 1), lambda i: (i, 0))]
        + [whole] * len(pieces),
        out_specs=pl.BlockSpec((step, pieces[0].shape[1]), lambda i: (i, 0)),
        compiler_params=params(12),
        name="pick",
    )(bases, index, *pieces)


def route_matrix(vecs):
    row = np.arange(2 * vecs * SIZE)[:, None]
    kind, pair = row // SIZE, row % SIZE // GROUP
    return jnp.asarray(np.arange(vecs * BLOCK) == kind // 2 * BLOCK + 2 * pair + kind % 2, BF16)


def own_mask(rows):
    shape = (rows, SIZE)
    return (
        lax.broadcasted_iota(jnp.int32, shape, 1) % GROUP == lax.broadcasted_iota(jnp.int32, shape, 0) % GROUP
    )


def stacked(tile_ref, at, half):
    parts = [tile_ref[at, c * LANES : (c + 1) * LANES] for c in range(half * HALF, (half + 1) * HALF)]
    return jnp.concatenate(parts, 0)


def forward_kernel(vecs, base_ref, index_ref, *refs):
    pieces, (route_ref, tile_ref, out_ref, x_ref, wide_ref) = refs[:-5], refs[-5:]
    x_ref[...] = gathered(base_ref, index_ref[...], pieces)
    first = lax.broadcasted_iota(jnp.int32, (GROUP, LANES), 1) < BLOCK
    own = own_mask(GROUP)
    span = HALF * GROUP

    def step(g, _):
        at = pl.ds(pl.multiple_of(g * GROUP, GROUP), GROUP)
        rows = []
        for p in range(vecs // 2):
            both = x_ref[at, p * LANES : (p + 1) * LANES]
            swapped = pltpu.roll(both, BLOCK, 1)
            rows += [
                jnp.where(first, both, 0.0),
                jnp.where(first, 0.0, swapped),
                jnp.where(first, swapped, 0.0),
                jnp.where(first, 0.0, both),
            ]
        left = jnp.concatenate(rows, 0).astype(BF16)
        for half in range(2):
            out = dot(left, stacked(tile_ref, at, half), NT)
            for s in range(2 * vecs):
                part = jnp.where(own[:, :span], out[s * GROUP : (s + 1) * GROUP], 0.0)
                wide_ref[at, s * SIZE + half * span : s * SIZE + (half + 1) * span] = part.astype(BF16)
        return 0

    lax.fori_loop(0, x_ref.shape[0] // GROUP, step, 0, unroll=8)
    out_ref[...] = dot(wide_ref[...], route_ref[...]).astype(BF16)


def forward(vecs, bases, index, pieces, route, tile):
    slots, size = tile.shape
    wide = vecs * BLOCK
    whole = pl.BlockSpec(memory_space=pltpu.VMEM)
    return pl.pallas_call(
        functools.partial(forward_kernel, vecs),
        grid=(slots // STEP,),
        out_shape=jax.ShapeDtypeStruct((slots, wide), BF16),
        in_specs=[pl.BlockSpec(memory_space=pltpu.SMEM), pl.BlockSpec((STEP, 1), lambda i: (i, 0))]
        + [whole] * (len(pieces) + 1)
        + [pl.BlockSpec((STEP, size), lambda i: (i, 0))],
        out_specs=pl.BlockSpec((STEP, wide), lambda i: (i, 0)),
        scratch_shapes=[pltpu.VMEM((STEP, wide), F32), pltpu.VMEM((STEP, 2 * vecs * SIZE), BF16)],
        compiler_params=params(28),
        name="forward",
    )(bases, index, *pieces, route, tile)


def backward_kernel(vecs, y_ref, route_ref, tile_ref, out_ref, wide_ref):
    own = own_mask(y_ref.shape[0])
    for s in range(2 * vecs):
        part = dot(y_ref[...], route_ref[s * SIZE : (s + 1) * SIZE, :], NT)
        wide_ref[:, s * SIZE : (s + 1) * SIZE] = jnp.where(own, part, 0.0).astype(BF16)
    first = lax.broadcasted_iota(jnp.int32, (GROUP, LANES), 1) < BLOCK
    span = HALF * GROUP

    def step(g, _):
        at = pl.ds(pl.multiple_of(g * GROUP, GROUP), GROUP)
        out = None
        for half in range(2):
            left = [
                wide_ref[at, s * SIZE + half * span : s * SIZE + (half + 1) * span] for s in range(2 * vecs)
            ]
            part = dot(jnp.concatenate(left, 0), stacked(tile_ref, at, half))
            out = part if out is None else out + part
        sums = []
        for k in range(vecs):
            even, odd = out[2 * k * GROUP : (2 * k + 1) * GROUP], out[(2 * k + 1) * GROUP : (2 * k + 2) * GROUP]
            part = jnp.where(first, even, odd)
            sums.append(part + pltpu.roll(part, BLOCK, 1))
        for p in range(vecs // 2):
            out_ref[at, p * LANES : (p + 1) * LANES] = jnp.where(first, sums[2 * p], sums[2 * p + 1]).astype(BF16)
        return 0

    lax.fori_loop(0, y_ref.shape[0] // GROUP, step, 0, unroll=8)


def backward(vecs, far, route, tile):
    slots, wide = far.shape
    block = pl.BlockSpec((STEP, wide), lambda i: (i, 0))
    return pl.pallas_call(
        functools.partial(backward_kernel, vecs),
        grid=(slots // STEP,),
        out_shape=jax.ShapeDtypeStruct((slots, wide), BF16),
        in_specs=[
            block,
            pl.BlockSpec(memory_space=pltpu.VMEM),
            pl.BlockSpec((STEP, tile.shape[1]), lambda i: (i, 0)),
        ],
        out_specs=block,
        scratch_shapes=[pltpu.VMEM((STEP, 2 * vecs * SIZE), BF16)],
        compiler_params=params(28),
        name="backward",
    )(far, route, tile)


def spread_kernel(col_ref, row_ref, back_ref, forth_ref, out_ref):
    count = out_ref.shape[1]
    place = lax.broadcasted_iota(jnp.int32, (count, col_ref.shape[1]), 0) + pl.program_id(0) * count
    total = dot(as_ones(place == col_ref[...]), back_ref[...])
    total += dot(as_ones(place == row_ref[...]), forth_ref[...])
    out_ref[0] = total.astype(BF16)


def spread(col_index, row_index, back, forth, count, width):
    whole = pl.BlockSpec(memory_space=pltpu.VMEM)
    return pl.pallas_call(
        spread_kernel,
        grid=(count,),
        out_shape=jax.ShapeDtypeStruct((count, width, back.shape[1]), BF16),
        in_specs=[whole] * 4,
        out_specs=pl.BlockSpec((1, width, back.shape[1]), lambda i: (i, 0, 0)),
        compiler_params=params(16),
        name="spread",
    )(col_index, row_index, back, forth)


def body(x_vec, hx_vec, p_vec, hp_vec, theta, precond, tile_vals, tile_rows, tile_cols, tile_count):
    vecs, piece_len = x_vec.shape
    rows, cols = lax.axis_size("row"), lax.axis_size("col")
    ring = rows // 2
    ndim_total = piece_len * rows * cols
    row_pos = lax.axis_index("row")
    width = piece_len // BLOCK
    slots = tile_vals.shape[2]
    tile = tile_vals[0, 0]
    route = route_matrix(vecs)
    residue = (hx_vec - x_vec * theta[:, None]) / precond[None, :]
    live = jnp.arange(slots, dtype=jnp.int32) < tile_count[0, 0]
    row_index = jnp.where(live, tile_rows[0, 0], -1)[None]
    col_index = jnp.where(live, tile_cols[0, 0], -1)[None]

    def along(block, sign):
        path = [(r * cols + c, r * cols + (c + sign * r) % cols) for r in range(rows) for c in range(cols)]
        return lax.ppermute(block, BOTH, path)

    def within(block, flip, turn):
        return lax.ppermute(
            block, "row", [(i, (i // ring ^ flip) * ring + (i % ring + turn) % ring) for i in range(rows)]
        )

    own = residue.astype(BF16).reshape(vecs, width, BLOCK).transpose(1, 0, 2).reshape(width, vecs * BLOCK)
    offsets = [(0, 0), (1, 0), (0, 1), (0, 3), (1, 1), (1, 3), (0, 2), (1, 2)]
    pieces = [own] + [within(own, *o) for o in offsets[1:]]
    flips = jnp.array([o[0] for o in offsets], jnp.int32)
    turns = jnp.array([o[1] for o in offsets], jnp.int32)
    bases = width * ((row_pos // ring ^ flips) * ring + (row_pos % ring - turns) % ring)
    far_index = along(row_index, 1)
    far = along(pick(bases, far_index.reshape(slots, 1), pieces), -1)
    forth = along(forward(vecs, bases, col_index.reshape(slots, 1), pieces, route, tile), 1)
    back = backward(vecs, far, route, tile)
    parts = spread(col_index, far_index, back, forth, rows, width)
    parts = lax.all_to_all(parts, "row", 0, 0, tiled=True)
    total = parts.astype(F32).sum(0)
    hw_vec = total.reshape(width, vecs, BLOCK).transpose(1, 0, 2).reshape(vecs, piece_len)

    vectors = jnp.concatenate([x_vec, residue, p_vec], 0)
    known = jnp.concatenate([vectors, hx_vec, hp_vec], 0)
    early = jnp.dot(vectors, known.T, precision=lax.Precision.HIGHEST, preferred_element_type=jnp.float32)
    late = jnp.dot(vectors, hw_vec.T, precision=lax.Precision.HIGHEST, preferred_element_type=jnp.float32)
    gram = jnp.concatenate([early, late], 1)
    flat = jnp.pad(gram.reshape(-1), (0, 3 * LANES - gram.size)).reshape(1, 3, LANES)
    flat = jnp.broadcast_to(flat, (rows * cols, 3, LANES))
    gram = lax.all_to_all(flat, BOTH, 0, 0, tiled=True).sum(0).reshape(-1)[: gram.size].reshape(gram.shape)
    gram = gram / ndim_total
    n = 3 * vecs
    gram_a = jnp.concatenate([gram[:, n : n + vecs], gram[:, n + 2 * vecs :], gram[:, n + vecs : n + 2 * vecs]], 1)
    return hw_vec, gram_a, gram[:, :n]


def solution(mesh):
    vector = P(None, ("col", "row"))
    placed = (
        vector,
        vector,
        vector,
        vector,
        P(),
        P(("col", "row")),
        P("row", "col", None, None),
        P("row", "col", None),
        P("row", "col", None),
        P("row", "col"),
    )
    return jax.shard_map(body, mesh=mesh, in_specs=placed, out_specs=(vector, P(), P()), check_vma=False)
```

time: 113 us -> 114 us (level)
  starting transfers between devices: 29.8 us -> 46.1 us
  Pallas kernels: 32.1 us -> 23.9 us
  waiting for transfers between devices: 19.3 us -> 12.7 us
  blocking collectives: 16.8 us -> 14.9 us
    all_to_all x1, starting transfers between devices: 11.3 us -> 22.7 us  [body(): parts = lax.all_to_all(parts, 'row', 0, 0, tiled=True)]
    pallas_call x3, Pallas kernels: 26.4 us -> 19.1 us  [the longest x1 9.18 us: forward(): pl.pallas_call(functools.partial(forward_kernel, vecs), grid=(slots // ST...]
    ppermute x10, waiting for transfers between devices: 9.54 us -> 3.02 us  [the longest x7 3.02 us: within(): lax.ppermute(block, 'row', [(i, (i // ring ^ flip) * ring + (i % ring + t...]
    ppermute x10, starting transfers between devices: 18.5 us -> 23.4 us  [the longest x7 21.3 us: within(): lax.ppermute(block, 'row', [(i, (i // ring ^ flip) * ring + (i % ring + t...]
    all_to_all x1, blocking collectives: 16.8 us -> 14.9 us  [body(): lax.all_to_all(flat, BOTH, 0, 0, tiled=True).sum(0).reshape(-1)[:gram.size]]
    unnamed x18 -> x26, local copies, waits for them, and re-layouts: 3.41 us -> 3.43 us
  transfers between devices with their start and end apart: 11 -> 11, of which waited for: 5 -> 3; matrix products, arithmetic and copies ran while one was open for 5% -> 5% of each run, Pallas kernels for 22% -> 14%
where the time goes in v2:
time: 114 us
  starting transfers between devices  46.1 us (40%)
  Pallas kernels  23.9 us (21%)
  blocking collectives  14.9 us (13%)
  waiting for transfers between devices  12.7 us (11%)
  local copies, waits for them, and re-layouts  7.65 us (7%)
  matrix products  4.09 us (4%)
  other arithmetic  3.09 us (3%)
  between operations  1.65 us (1%)
    all_to_all x1, starting transfers between devices, body(): parts = lax.all_to_all(parts, 'row', 0, 0, tiled=True)  22.7 us
    ppermute x7, starting transfers between devices, within(): lax.ppermute(block, 'row', [(i, (i // ring ^ flip) * ring + (i % ring + t...  21.3 us
    all_to_all x1, blocking collectives, body(): lax.all_to_all(flat, BOTH, 0, 0, tiled=True).sum(0).reshape(-1)[:gram.size]  14.9 us
    all_to_all x1, waiting for transfers between devices, body(): parts = lax.all_to_all(parts, 'row', 0, 0, tiled=True)  9.66 us
    pallas_call x1, Pallas kernels, forward(): pl.pallas_call(functools.partial(forward_kernel, vecs), grid=(slots // ST...  9.18 us
    pallas_call x1, Pallas kernels, backward(): pl.pallas_call(functools.partial(backward_kernel, vecs), grid=(slots // S...  6.67 us
    pallas_call x1, Pallas kernels, spread(): pl.pallas_call(spread_kernel, grid=(count,), out_shape=jax.ShapeDtypeStru...  4.82 us
    unnamed x26, local copies, waits for them, and re-layouts  3.43 us
  transfers between devices with their start and end apart: 11, of which 3 were waited for; matrix products, arithmetic and copies ran while one was open for 5% of the time, Pallas kernels for 14%

profile of v2, /device:TPU:1, one launch (start us, length us, event | category | flops | bytes accessed | tf_op | source)
XLA Modules:
  0.0 114.0 jit_solution(3208978544222577228)
XLA Ops:
  0.7 1.9 %fusion.8 = (bf16[4,16384]{1,0:T(4,128)(2,1)S(1)}, f32[4,16384]{1,0:T(4,128)}) fusion(f32[16384]{0:T(1024)} %param.18, f32[4,16384]{1,0:T(4,128)} %param.14, f32[4,16384]{1,0:T(4,128)} %param.13, f32[4]{0:T(128)} %param.17), kind=kLoop, calls=%fused_computation.21 | loop fusion | flops 262144 | bytes 983056 | tf_op jit(solution)/shard_map/convert_element_type | solution.py:225
  2.6 0.3 reshape.78
  2.9 0.1 copy.62
  3.1 2.1 %collective-permute-start.1 = (bf16[256,256]{1,0:T(8,128)(2,1)S(1)}, bf16[256,256]{1,0:T(8,128)(2,1)S(1)}, u32[]{:S(2)}, u32[]{:S(2)}) collective-permute-start(bf16[256,256]{1,0:T(8,128)(2,1)S(1)} %copy.71.refs_0_), channel_id=1, source_target_pairs={{0,64},{16,80},{32,96},{48,112},{64,0},{80,16},{96,32},{112,48},{1... | collective-permute-start | bytes 393224 | tf_op jit(solution)/shard_map/ppermute | solution.py:221
  5.2 1.6 %collective-permute-start.2 = (bf16[256,256]{1,0:T(8,128)(2,1)S(1)}, bf16[256,256]{1,0:T(8,128)(2,1)S(1)}, u32[]{:S(2)}, u32[]{:S(2)}) collective-permute-start(bf16[256,256]{1,0:T(8,128)(2,1)S(1)} %copy.71.refs_0_), channel_id=1, source_target_pairs={{0,16},{16,32},{32,48},{48,0},{64,80},{80,96},{96,112},{112,64},{1... | collective-permute-start | bytes 393224 | tf_op jit(solution)/shard_map/ppermute | solution.py:221
  6.9 2.1 %collective-permute-start.3 = (bf16[256,256]{1,0:T(8,128)(2,1)S(1)}, bf16[256,256]{1,0:T(8,128)(2,1)}, u32[]{:S(2)}, u32[]{:S(2)}) collective-permute-start(bf16[256,256]{1,0:T(8,128)(2,1)S(1)} %copy.71.refs_0_), channel_id=1, source_target_pairs={{0,48},{16,0},{32,16},{48,32},{64,112},{80,64},{96,80},{112,96},{1... | collective-permute-start | bytes 393224 | tf_op jit(solution)/shard_map/ppermute | solution.py:221
  9.7 0.7 collective-permute-start
  10.4 0.2 copy.72
  10.7 10.0 %collective-permute-start.5 = (bf16[256,256]{1,0:T(8,128)(2,1)S(1)}, bf16[256,256]{1,0:T(8,128)(2,1)}, u32[]{:S(2)}, u32[]{:S(2)}) collective-permute-start(bf16[256,256]{1,0:T(8,128)(2,1)S(1)} %copy.71.refs_0_), channel_id=1, source_target_pairs={{0,112},{16,64},{32,80},{48,96},{64,48},{80,0},{96,16},{112,32},{1... | collective-permute-start | bytes 393224 | tf_op jit(solution)/shard_map/ppermute | solution.py:221
  20.7 2.0 %collective-permute-start.6 = (bf16[256,256]{1,0:T(8,128)(2,1)S(1)}, bf16[256,256]{1,0:T(8,128)(2,1)}, u32[]{:S(2)}, u32[]{:S(2)}) collective-permute-start(bf16[256,256]{1,0:T(8,128)(2,1)S(1)} %copy.71.refs_0_), channel_id=1, source_target_pairs={{0,32},{16,48},{32,0},{48,16},{64,96},{80,112},{96,64},{112,80},{1... | collective-permute-start | bytes 393224 | tf_op jit(solution)/shard_map/ppermute | solution.py:221
  22.7 3.5 %collective-permute-start.7 = (bf16[256,256]{1,0:T(8,128)(2,1)S(1)}, bf16[256,256]{1,0:T(8,128)(2,1)}, u32[]{:S(2)}, u32[]{:S(2)}) collective-permute-start(bf16[256,256]{1,0:T(8,128)(2,1)S(1)} %copy.71.refs_0_), channel_id=1, source_target_pairs={{0,96},{16,112},{32,64},{48,80},{64,32},{80,48},{96,0},{112,16},{1... | collective-permute-start | bytes 393224 | tf_op jit(solution)/shard_map/ppermute | solution.py:221
  26.2 0.2 copy.70.index_ref
  26.6 2.9 %collective-permute-done.7.refs_7_ = bf16[256,256]{1,0:T(8,128)(2,1)} collective-permute-done((bf16[256,256]{1,0:T(8,128)(2,1)S(1)}, bf16[256,256]{1,0:T(8,128)(2,1)}, u32[]{:S(2)}, u32[]{:S(2)}) %collective-permute-start.7) | collective-permute-done | bytes 131104 | tf_op jit(solution)/shard_map/ppermute | solution.py:221
  29.4 3.2 %pick.1 = bf16[1024,256]{1,0:T(8,128)(2,1)S(1)} custom-call(s32[8]{0:T(128)S(1)} %fusion.5.base_ref, s32[1024,1]{1,0:T(8,128)S(1)} %copy.70.index_ref, bf16[256,256]{1,0:T(8,128)(2,1)S(1)} %copy.71.refs_0_, bf16[256,256]{1,0:T(8,128)(2,1)S(1)} %collective-permute-done.1.refs_1_, bf16[256,256]{1,0:T(8,128)(2,1)S(1)} %collective-permute-done.2.refs_2_, ...), custom_call_target="tpu_custom_call" | custom-call | tf_op jit(solution)/shard_map/pick/pallas_call | solution.py:53
  32.6 0.7 collective-permute-start.8
  33.4 3.4 %copy-done = bf16[1,1,1024,4096]{3,2,1,0:T(8,128)(2,1)S(1)} copy-done((bf16[1,1,1024,4096]{3,2,1,0:T(8,128)(2,1)S(1)}, bf16[1,1,1024,4096]{3,2,1,0:T(8,128)(2,1)}, u32[]{:S(2)}) %copy-start) | copy-done | bytes 8388632
  36.7 9.2 %forward.1 = bf16[1024,256]{1,0:T(8,128)(2,1)S(1)} custom-call(s32[8]{0:T(128)S(1)} %fusion.5.base_ref, s32[1024,1]{1,0:T(8,128)S(1)} %fusion.2.index_ref, bf16[256,256]{1,0:T(8,128)(2,1)S(1)} %copy.71.refs_0_, bf16[256,256]{1,0:T(8,128)(2,1)S(1)} %collective-permute-done.1.refs_1_, bf16[256,256]{1,0:T(8,128)(2,1)S(1)} %collective-permute-done.2.refs_2_, ...), custom_call_target="tpu_custom_call" | custom-call | tf_op jit(solution)/shard_map/forward/pallas_call | solution.py:118
  45.9 0.7 collective-permute-start.9
  46.7 6.7 %backward.1.back_ref = bf16[1024,256]{1,0:T(8,128)(2,1)S(1)} custom-call(bf16[1024,256]{1,0:T(8,128)(2,1)S(1)} %collective-permute-done.8.y_ref, bf16[4096,256]{1,0:T(8,128)(2,1)S(1)} %copy-done.2, bf16[1024,4096]{1,0:T(8,128)(2,1)S(1)} %bitcast.22), custom_call_target="tpu_custom_call" | custom-call | tf_op jit(solution)/shard_map/backward/pallas_call | solution.py:164
  53.4 4.8 %spread.1 = bf16[8,256,256]{2,1,0:T(8,128)(2,1)} custom-call(s32[1,1024]{1,0:T(1,128)S(1)} %compare_select_fusion.1.col_ref, s32[1,1024]{1,0:T(1,128)S(1)} %collective-permute-done.row_ref, bf16[1024,256]{1,0:T(8,128)(2,1)S(1)} %backward.1.back_ref, bf16[1024,256]{1,0:T(8,128)(2,1)S(1)} %collective-permute-done.9.forth_ref), custom_call_target="tpu_custom_call" | custom-call | tf_op jit(solution)/shard_map/spread/pallas_call | solution.py:190
  58.2 22.7 %all-to-all-start = ((bf16[8,256,256]{2,1,0:T(8,128)(2,1)}), bf16[8,256,256]{2,1,0:T(8,128)(2,1)S(1)}, u32[]{:S(2)}, u32[]{:S(2)}) async-start(bf16[8,256,256]{2,1,0:T(8,128)(2,1)} %spread.1), calls=%async_computation | async-start | bytes 2097152 | tf_op jit(solution)/shard_map/all_to_all | solution.py:236
  80.9 2.5 %concatenate.14 = f32[20,16384]{1,0:T(8,128)S(1)} concatenate(f32[4,16384]{1,0:T(4,128)S(1)} %copy-done.3, f32[4,16384]{1,0:T(4,128)S(1)} %copy-done.4, f32[4,16384]{1,0:T(4,128)} %param.15, f32[4,16384]{1,0:T(4,128)S(1)} %copy-done.5, f32[4,16384]{1,0:T(4,128)} %param.16), dimensions={0} | concatenate | bytes 2621440 | tf_op jit(solution)/shard_map/concatenate | solution.py:241
  83.4 2.6 %fusion.1 = f32[12,20]{1,0:T(8,128)S(1)} fusion(f32[20,16384]{1,0:T(8,128)S(1)} %concatenate.14, f32[4,16384]{1,0:T(4,128)} %param.15, f32[4,16384]{1,0:T(4,128)S(1)} %copy-done.4, f32[4,16384]{1,0:T(4,128)S(1)} %copy-done.3), kind=kOutput, calls=%fused_computation.3 | convolution fusion | flops 47579136 | bytes 2098112 | tf_op jit(solution)/shard_map/dot_general | solution.py:242
  86.0 9.7 %all-to-all-done = bf16[8,256,256]{2,1,0:T(8,128)(2,1)S(1)} async-done(((bf16[8,256,256]{2,1,0:T(8,128)(2,1)}), bf16[8,256,256]{2,1,0:T(8,128)(2,1)S(1)}, u32[]{:S(2)}, u32[]{:S(2)}) %all-to-all-start) | async-done | bytes 1048608 | tf_op jit(solution)/shard_map/all_to_all | solution.py:236
  95.6 0.1 convert_reduce_fusion
  95.8 0.1 copy.74
  95.9 0.2 copy.75
  96.1 0.2 reshape.81
  96.4 1.5 %fusion = f32[12,4]{1,0:T(8,128)S(1)} fusion(f32[4,16384]{1,0:T(4,128)S(1)} %reshape.81, f32[4,16384]{1,0:T(4,128)S(1)} %copy-done.6, f32[4,16384]{1,0:T(4,128)S(1)} %copy-done.4, f32[4,16384]{1,0:T(4,128)S(1)} %copy-done.3), kind=kOutput, calls=%fused_computation.2 | convolution fusion | flops 9830400 | bytes 1048768 | tf_op jit(solution)/shard_map/dot_general | solution.py:243
  98.1 14.9 %all_to_all.10 = f32[128,3,128]{2,1,0:T(4,128)S(1)} all-to-all(f32[128,3,128]{2,1,0:T(4,128)S(1)} %broadcast_in_dim.21), channel_id=1, replica_groups=mesh['row'=8,'col'=16] {'row','col'}, dimensions={0} | all-to-all | bytes 393216 | tf_op jit(solution)/shard_map/all_to_all | solution.py:247
  113.0 0.1 reduce_sum.19
  113.4 0.7 pad_maximum_fusion.4
  (47 shorter events, 0.8 us)
Async XLA Ops:
  0.6 9.0 %copy-start.10 = (s32[1,1,1024]{2,1,0:T(1,128)S(1)}, s32[1,1,1024]{2,1,0:T(1,128)}, u32[]{:S(2)}) copy-start(s32[1,1,1024]{2,1,0:T(1,128)} %param.20) | copy-start | bytes 12292
  0.6 9.7 %copy-start.9 = (s32[1,1,1024]{2,1,0:T(1,128)S(1)}, s32[1,1,1024]{2,1,0:T(1,128)}, u32[]{:S(2)}) copy-start(s32[1,1,1024]{2,1,0:T(1,128)} %param.21) | copy-start | bytes 12292
  2.6 23.6 %copy-start.11 = (s32[8]{0:T(128)S(1)}, s32[8]{0:T(128)}, u32[]{:S(2)}) copy-start(s32[8]{0:T(128)} %constant.58.clone) | copy-start | bytes 100
  2.6 23.6 %copy-start.12 = (s32[8]{0:T(128)S(1)}, s32[8]{0:T(128)}, u32[]{:S(2)}) copy-start(s32[8]{0:T(128)} %constant.66) | copy-start | bytes 100
  3.1 17.6 %collective-permute-start.1 = (bf16[256,256]{1,0:T(8,128)(2,1)S(1)}, bf16[256,256]{1,0:T(8,128)(2,1)S(1)}, u32[]{:S(2)}, u32[]{:S(2)}) collective-permute-start(bf16[256,256]{1,0:T(8,128)(2,1)S(1)} %copy.71.refs_0_), channel_id=1, source_target_pairs={{0,64},{16,80},{32,96},{48,112},{64,0},{80,16},{96,32},{112,48},{1... | collective-permute-start | bytes 393224 | tf_op jit(solution)/shard_map/ppermute | solution.py:221
  5.2 17.5 %collective-permute-start.2 = (bf16[256,256]{1,0:T(8,128)(2,1)S(1)}, bf16[256,256]{1,0:T(8,128)(2,1)S(1)}, u32[]{:S(2)}, u32[]{:S(2)}) collective-permute-start(bf16[256,256]{1,0:T(8,128)(2,1)S(1)} %copy.71.refs_0_), channel_id=1, source_target_pairs={{0,16},{16,32},{32,48},{48,0},{64,80},{80,96},{96,112},{112,64},{1... | collective-permute-start | bytes 393224 | tf_op jit(solution)/shard_map/ppermute | solution.py:221
  6.9 19.5 %collective-permute-start.3 = (bf16[256,256]{1,0:T(8,128)(2,1)S(1)}, bf16[256,256]{1,0:T(8,128)(2,1)}, u32[]{:S(2)}, u32[]{:S(2)}) collective-permute-start(bf16[256,256]{1,0:T(8,128)(2,1)S(1)} %copy.71.refs_0_), channel_id=1, source_target_pairs={{0,48},{16,0},{32,16},{48,32},{64,112},{80,64},{96,80},{112,96},{1... | collective-permute-start | bytes 393224 | tf_op jit(solution)/shard_map/ppermute | solution.py:221
  9.0 17.4 %collective-permute-start.4 = (bf16[256,256]{1,0:T(8,128)(2,1)S(1)}, bf16[256,256]{1,0:T(8,128)(2,1)}, u32[]{:S(2)}, u32[]{:S(2)}) collective-permute-start(bf16[256,256]{1,0:T(8,128)(2,1)S(1)} %copy.71.refs_0_), channel_id=1, source_target_pairs={{0,80},{16,96},{32,112},{48,64},{64,16},{80,32},{96,48},{112,0},{1... | collective-permute-start | bytes 393224 | tf_op jit(solution)/shard_map/ppermute | solution.py:221
  9.7 1.0 collective-permute-start
  10.6 22.7 %copy-start.2 = (bf16[4096,256]{1,0:T(8,128)(2,1)S(1)}, bf16[4096,256]{1,0:T(8,128)(2,1)}, u32[]{:S(2)}) copy-start(bf16[4096,256]{1,0:T(8,128)(2,1)} %constant.57.clone.route_ref.refs_8_) | copy-start | bytes 6291460
  10.7 15.7 %collective-permute-start.5 = (bf16[256,256]{1,0:T(8,128)(2,1)S(1)}, bf16[256,256]{1,0:T(8,128)(2,1)}, u32[]{:S(2)}, u32[]{:S(2)}) collective-permute-start(bf16[256,256]{1,0:T(8,128)(2,1)S(1)} %copy.71.refs_0_), channel_id=1, source_target_pairs={{0,112},{16,64},{32,80},{48,96},{64,48},{80,0},{96,16},{112,32},{1... | collective-permute-start | bytes 393224 | tf_op jit(solution)/shard_map/ppermute | solution.py:221
  20.7 5.9 %collective-permute-start.6 = (bf16[256,256]{1,0:T(8,128)(2,1)S(1)}, bf16[256,256]{1,0:T(8,128)(2,1)}, u32[]{:S(2)}, u32[]{:S(2)}) collective-permute-start(bf16[256,256]{1,0:T(8,128)(2,1)S(1)} %copy.71.refs_0_), channel_id=1, source_target_pairs={{0,32},{16,48},{32,0},{48,16},{64,96},{80,112},{96,64},{112,80},{1... | collective-permute-start | bytes 393224 | tf_op jit(solution)/shard_map/ppermute | solution.py:221
  22.7 6.7 %collective-permute-start.7 = (bf16[256,256]{1,0:T(8,128)(2,1)S(1)}, bf16[256,256]{1,0:T(8,128)(2,1)}, u32[]{:S(2)}, u32[]{:S(2)}) collective-permute-start(bf16[256,256]{1,0:T(8,128)(2,1)S(1)} %copy.71.refs_0_), channel_id=1, source_target_pairs={{0,96},{16,112},{32,64},{48,80},{64,32},{80,48},{96,0},{112,16},{1... | collective-permute-start | bytes 393224 | tf_op jit(solution)/shard_map/ppermute | solution.py:221
  32.6 14.0 %collective-permute-start.8 = (bf16[1024,256]{1,0:T(8,128)(2,1)S(1)}, bf16[1024,256]{1,0:T(8,128)(2,1)S(1)}, u32[]{:S(2)}, u32[]{:S(2)}) collective-permute-start(bf16[1024,256]{1,0:T(8,128)(2,1)S(1)} %pick.1), channel_id=1, source_target_pairs={{0,0},{1,1},{2,2},{3,3},{4,4},{5,5},{6,6},{7,7},{8,8},{9,9},{10,10... | collective-permute-start | bytes 1572872 | tf_op jit(solution)/shard_map/ppermute | solution.py:218
  33.4 3.4 %copy-start = (bf16[1,1,1024,4096]{3,2,1,0:T(8,128)(2,1)S(1)}, bf16[1,1,1024,4096]{3,2,1,0:T(8,128)(2,1)}, u32[]{:S(2)}) copy-start(bf16[1,1,1024,4096]{3,2,1,0:T(8,128)(2,1)} %param.19) | copy-start | bytes 25165828
  36.7 9.9 %copy-start.1 = (bf16[1,1,1024,4096]{3,2,1,0:T(8,128)(2,1)S(1)}, bf16[1,1,1024,4096]{3,2,1,0:T(8,128)(2,1)}, u32[]{:S(2)}) copy-start(bf16[1,1,1024,4096]{3,2,1,0:T(8,128)(2,1)} %param.19) | copy-start | bytes 25165828
  45.9 7.4 %collective-permute-start.9 = (bf16[1024,256]{1,0:T(8,128)(2,1)S(1)}, bf16[1024,256]{1,0:T(8,128)(2,1)S(1)}, u32[]{:S(2)}, u32[]{:S(2)}) collective-permute-start(bf16[1024,256]{1,0:T(8,128)(2,1)S(1)} %forward.1), channel_id=1, source_target_pairs={{0,0},{1,1},{2,2},{3,3},{4,4},{5,5},{6,6},{7,7},{8,8},{9,9},{10,10... | collective-permute-start | bytes 1572872 | tf_op jit(solution)/shard_map/ppermute | solution.py:218
  58.2 22.7 %copy-start.3 = (f32[4,16384]{1,0:T(4,128)S(1)}, f32[4,16384]{1,0:T(4,128)}, u32[]{:S(2)}) copy-start(f32[4,16384]{1,0:T(4,128)} %param.13) | copy-start | bytes 786436
  58.2 22.7 %copy-start.4 = (f32[4,16384]{1,0:T(4,128)S(1)}, f32[4,16384]{1,0:T(4,128)}, u32[]{:S(2)}) copy-start(f32[4,16384]{1,0:T(4,128)} %get-tuple-element.4) | copy-start | bytes 786436
  58.2 22.7 %copy-start.5 = (f32[4,16384]{1,0:T(4,128)S(1)}, f32[4,16384]{1,0:T(4,128)}, u32[]{:S(2)}) copy-start(f32[4,16384]{1,0:T(4,128)} %param.14) | copy-start | bytes 786436
  58.2 37.5 %all-to-all-start = ((bf16[8,256,256]{2,1,0:T(8,128)(2,1)}), bf16[8,256,256]{2,1,0:T(8,128)(2,1)S(1)}, u32[]{:S(2)}, u32[]{:S(2)}) async-start(bf16[8,256,256]{2,1,0:T(8,128)(2,1)} %spread.1), calls=%async_computation | async-start | bytes 2097152 | tf_op jit(solution)/shard_map/all_to_all | solution.py:236
  86.0 10.4 %copy-start.6 = (f32[4,16384]{1,0:T(4,128)S(1)}, f32[4,16384]{1,0:T(4,128)}, u32[]{:S(2)}) copy-start(f32[4,16384]{1,0:T(4,128)} %param.15) | copy-start | bytes 786436
  96.4 17.7 %copy-start.7 = (f32[4,16384]{1,0:T(4,128)}, f32[4,16384]{1,0:T(4,128)S(1)}, u32[]{:S(2)}) copy-start(f32[4,16384]{1,0:T(4,128)S(1)} %reshape.81) | copy-start | bytes 786436
  113.3 0.8 copy-start.8

commit v3 on v2

--- a/solution.py
+++ b/solution.py
@@ -34,11 +34,11 @@
 
 
 def gathered(base_ref, index, piece_refs):
-    shape = (index.shape[0], piece_refs[0].shape[0])
-    place = jnp.broadcast_to(index, shape) - lax.broadcasted_iota(jnp.int32, shape, 1)
+    shape = (piece_refs[0].shape[1], index.shape[1])
+    place = index - lax.broadcasted_iota(jnp.int32, shape, 0)
     total = None
     for d, piece in enumerate(piece_refs):
-        part = dot(as_ones(place == base_ref[d]), piece[...])
+        part = dot(piece[...], as_ones(place == base_ref[d]))
         total = part if total is None else total + part
     return total
 
@@ -48,16 +48,13 @@
 
 
 def pick(bases, index, pieces):
-    slots, step = index.shape[0], 256
     whole = pl.BlockSpec(memory_space=pltpu.VMEM)
     return pl.pallas_call(
         pick_kernel,
-        grid=(slots // step,),
-        out_shape=jax.ShapeDtypeStruct((slots, pieces[0].shape[1]), BF16),
-        in_specs=[pl.BlockSpec(memory_space=pltpu.SMEM), pl.BlockSpec((step, 1), lambda i: (i, 0))]
-        + [whole] * len(pieces),
-        out_specs=pl.BlockSpec((step, pieces[0].shape[1]), lambda i: (i, 0)),
-        compiler_params=params(12),
+        out_shape=jax.ShapeDtypeStruct((pieces[0].shape[0], index.shape[1]), BF16),
+        in_specs=[pl.BlockSpec(memory_space=pltpu.SMEM)] + [whole] * (1 + len(pieces)),
+        out_specs=whole,
+        compiler_params=params(16),
         name="pick",
     )(bases, index, *pieces)
 
@@ -80,15 +77,16 @@
     return jnp.concatenate(parts, 0)
 
 
-def forward_kernel(vecs, base_ref, index_ref, *refs):
+def forward_kernel(vecs, base, base_ref, index_ref, *refs):
     pieces, (route_ref, tile_ref, out_ref, x_ref, wide_ref) = refs[:-5], refs[-5:]
-    x_ref[...] = gathered(base_ref, index_ref[...], pieces)
+    x_ref[...] = gathered(base_ref, index_ref[...], pieces).T
     first = lax.broadcasted_iota(jnp.int32, (GROUP, LANES), 1) < BLOCK
     own = own_mask(GROUP)
     span = HALF * GROUP
 
     def step(g, _):
         at = pl.ds(pl.multiple_of(g * GROUP, GROUP), GROUP)
+        start = pl.ds(pl.multiple_of(base + g * GROUP, GROUP), GROUP)
         rows = []
         for p in range(vecs // 2):
             both = x_ref[at, p * LANES : (p + 1) * LANES]
@@ -101,7 +99,7 @@
             ]
         left = jnp.concatenate(rows, 0).astype(BF16)
         for half in range(2):
-            out = dot(left, stacked(tile_ref, at, half), NT)
+            out = dot(left, stacked(tile_ref, start, half), NT)
             for s in range(2 * vecs):
                 part = jnp.where(own[:, :span], out[s * GROUP : (s + 1) * GROUP], 0.0)
                 wide_ref[at, s * SIZE + half * span : s * SIZE + (half + 1) * span] = part.astype(BF16)
@@ -111,28 +109,27 @@
     out_ref[...] = dot(wide_ref[...], route_ref[...]).astype(BF16)
 
 
-def forward(vecs, bases, index, pieces, route, tile):
-    slots, size = tile.shape
+def forward(vecs, bases, index, pieces, route, tile, at):
     wide = vecs * BLOCK
     whole = pl.BlockSpec(memory_space=pltpu.VMEM)
     return pl.pallas_call(
-        functools.partial(forward_kernel, vecs),
-        grid=(slots // STEP,),
-        out_shape=jax.ShapeDtypeStruct((slots, wide), BF16),
-        in_specs=[pl.BlockSpec(memory_space=pltpu.SMEM), pl.BlockSpec((STEP, 1), lambda i: (i, 0))]
-        + [whole] * (len(pieces) + 1)
-        + [pl.BlockSpec((STEP, size), lambda i: (i, 0))],
-        out_specs=pl.BlockSpec((STEP, wide), lambda i: (i, 0)),
+        functools.partial(forward_kernel, vecs, at * STEP),
+        grid=(1,),
+        out_shape=jax.ShapeDtypeStruct((STEP, wide), BF16),
+        in_specs=[pl.BlockSpec(memory_space=pltpu.SMEM), pl.BlockSpec((1, STEP), lambda i: (0, at))]
+        + [whole] * (len(pieces) + 2),
+        out_specs=whole,
         scratch_shapes=[pltpu.VMEM((STEP, wide), F32), pltpu.VMEM((STEP, 2 * vecs * SIZE), BF16)],
-        compiler_params=params(28),
+        compiler_params=params(20),
         name="forward",
     )(bases, index, *pieces, route, tile)
 
 
 def backward_kernel(vecs, y_ref, route_ref, tile_ref, out_ref, wide_ref):
-    own = own_mask(y_ref.shape[0])
+    own = own_mask(out_ref.shape[0])
+    far = y_ref[...].astype(F32).T.astype(BF16)
     for s in range(2 * vecs):
-        part = dot(y_ref[...], route_ref[s * SIZE : (s + 1) * SIZE, :], NT)
+        part = dot(far, route_ref[s * SIZE : (s + 1) * SIZE, :], NT)
         wide_ref[:, s * SIZE : (s + 1) * SIZE] = jnp.where(own, part, 0.0).astype(BF16)
     first = lax.broadcasted_iota(jnp.int32, (GROUP, LANES), 1) < BLOCK
     span = HALF * GROUP
@@ -155,33 +152,31 @@
             out_ref[at, p * LANES : (p + 1) * LANES] = jnp.where(first, sums[2 * p], sums[2 * p + 1]).astype(BF16)
         return 0
 
-    lax.fori_loop(0, y_ref.shape[0] // GROUP, step, 0, unroll=8)
+    lax.fori_loop(0, out_ref.shape[0] // GROUP, step, 0, unroll=8)
 
 
 def backward(vecs, far, route, tile):
-    slots, wide = far.shape
-    block = pl.BlockSpec((STEP, wide), lambda i: (i, 0))
+    wide, slots = far.shape
+    whole = pl.BlockSpec(memory_space=pltpu.VMEM)
     return pl.pallas_call(
         functools.partial(backward_kernel, vecs),
-        grid=(slots // STEP,),
         out_shape=jax.ShapeDtypeStruct((slots, wide), BF16),
-        in_specs=[
-            block,
-            pl.BlockSpec(memory_space=pltpu.VMEM),
-            pl.BlockSpec((STEP, tile.shape[1]), lambda i: (i, 0)),
-        ],
-        out_specs=block,
-        scratch_shapes=[pltpu.VMEM((STEP, 2 * vecs * SIZE), BF16)],
-        compiler_params=params(28),
+        in_specs=[whole] * 3,
+        out_specs=whole,
+        scratch_shapes=[pltpu.VMEM((slots, 2 * vecs * SIZE), BF16)],
+        compiler_params=params(20),
         name="backward",
     )(far, route, tile)
 
 
-def spread_kernel(col_ref, row_ref, back_ref, forth_ref, out_ref):
+def spread_kernel(col_ref, row_ref, back_ref, *refs):
+    forth_refs, out_ref = refs[:-1], refs[-1]
     count = out_ref.shape[1]
     place = lax.broadcasted_iota(jnp.int32, (count, col_ref.shape[1]), 0) + pl.program_id(0) * count
     total = dot(as_ones(place == col_ref[...]), back_ref[...])
-    total += dot(as_ones(place == row_ref[...]), forth_ref[...])
+    hot = as_ones(place == row_ref[...])
+    for n, forth in enumerate(forth_refs):
+        total += dot(hot[:, n * STEP : (n + 1) * STEP], forth[...])
     out_ref[0] = total.astype(BF16)
 
 
@@ -191,11 +186,11 @@
         spread_kernel,
         grid=(count,),
         out_shape=jax.ShapeDtypeStruct((count, width, back.shape[1]), BF16),
-        in_specs=[whole] * 4,
+        in_specs=[whole] * (3 + len(forth)),
         out_specs=pl.BlockSpec((1, width, back.shape[1]), lambda i: (i, 0, 0)),
         compiler_params=params(16),
         name="spread",
-    )(col_index, row_index, back, forth)
+    )(col_index, row_index, back, *forth)
 
 
 def body(x_vec, hx_vec, p_vec, hp_vec, theta, precond, tile_vals, tile_rows, tile_cols, tile_count):
@@ -222,15 +217,17 @@
             block, "row", [(i, (i // ring ^ flip) * ring + (i % ring + turn) % ring) for i in range(rows)]
         )
 
-    own = residue.astype(BF16).reshape(vecs, width, BLOCK).transpose(1, 0, 2).reshape(width, vecs * BLOCK)
+    own = residue.astype(BF16).reshape(vecs, width, BLOCK).transpose(0, 2, 1).reshape(vecs * BLOCK, width)
     offsets = [(0, 0), (1, 0), (0, 1), (0, 3), (1, 1), (1, 3), (0, 2), (1, 2)]
     pieces = [own] + [within(own, *o) for o in offsets[1:]]
     flips = jnp.array([o[0] for o in offsets], jnp.int32)
     turns = jnp.array([o[1] for o in offsets], jnp.int32)
     bases = width * ((row_pos // ring ^ flips) * ring + (row_pos % ring - turns) % ring)
-    far_index = along(row_index, 1)
-    far = along(pick(bases, far_index.reshape(slots, 1), pieces), -1)
-    forth = along(forward(vecs, bases, col_index.reshape(slots, 1), pieces, route, tile), 1)
+    far_index = along(lax.optimization_barrier((row_index, pieces[3]))[0], 1)
+    far = along(pick(bases, far_index, pieces), -1)
+    forth = [
+        along(forward(vecs, bases, col_index, pieces, route, tile, n), 1) for n in range(slots // STEP)
+    ]
     back = backward(vecs, far, route, tile)
     parts = spread(col_index, far_index, back, forth, rows, width)
     parts = lax.all_to_all(parts, "row", 0, 0, tiled=True)

time: 114 us -> 112 us (0.982)
  starting transfers between devices: 46.1 us -> 35.2 us
  waiting for transfers between devices: 12.7 us -> 19.8 us
  blocking collectives: 14.9 us -> 18 us
  Pallas kernels: 23.9 us -> 22.4 us
    ppermute x7, starting transfers between devices: 21.3 us -> 13.1 us  [within(): lax.ppermute(block, 'row', [(i, (i // ring ^ flip) * ring + (i % ring + t...]
    ppermute x7, waiting for transfers between devices: 3.02 us -> 9.91 us  [within(): lax.ppermute(block, 'row', [(i, (i // ring ^ flip) * ring + (i % ring + t...]
    all_to_all x1, starting transfers between devices: 22.7 us -> 19.3 us  [body(): parts = lax.all_to_all(parts, 'row', 0, 0, tiled=True)]
    all_to_all x1, blocking collectives: 14.9 us -> 18 us  [body(): lax.all_to_all(flat, BOTH, 0, 0, tiled=True).sum(0).reshape(-1)[:gram.size]]
    pallas_call x3 -> x4, Pallas kernels: 19.1 us -> 17.6 us  [the longest x2 9.12 us: forward(): pl.pallas_call(functools.partial(forward_kernel, vecs, at * STEP), grid=(...]
    ppermute x3 -> x4, starting transfers between devices: 2.05 us -> 2.83 us  [along(): return lax.ppermute(block, BOTH, path)]
    unnamed x26 -> x24, local copies, waits for them, and re-layouts: 3.43 us -> 3.44 us
  transfers between devices with their start and end apart: 11 -> 12, of which waited for: 3 -> 3; matrix products, arithmetic and copies ran while one was open for 5% -> 5% of each run, Pallas kernels for 14% -> 14%
where the time goes in v3:
time: 112 us
  starting transfers between devices  35.2 us (31%)
  Pallas kernels  22.4 us (20%)
  waiting for transfers between devices  19.8 us (18%)
  blocking collectives  18 us (16%)
  local copies, waits for them, and re-layouts  7.12 us (6%)
  matrix products  4.09 us (4%)
  other arithmetic  3.16 us (3%)
  between operations  1.63 us (1%)
    all_to_all x1, starting transfers between devices, body(): parts = lax.all_to_all(parts, 'row', 0, 0, tiled=True)  19.3 us
    all_to_all x1, blocking collectives, body(): lax.all_to_all(flat, BOTH, 0, 0, tiled=True).sum(0).reshape(-1)[:gram.size]  18 us
    ppermute x7, starting transfers between devices, within(): lax.ppermute(block, 'row', [(i, (i // ring ^ flip) * ring + (i % ring + t...  13.1 us
    ppermute x7, waiting for transfers between devices, within(): lax.ppermute(block, 'row', [(i, (i // ring ^ flip) * ring + (i % ring + t...  9.91 us
    all_to_all x1, waiting for transfers between devices, body(): parts = lax.all_to_all(parts, 'row', 0, 0, tiled=True)  9.87 us
    pallas_call x2, Pallas kernels, forward(): pl.pallas_call(functools.partial(forward_kernel, vecs, at * STEP), grid=(...  9.12 us
    pallas_call x1, Pallas kernels, backward(): pl.pallas_call(functools.partial(backward_kernel, vecs), out_shape=jax.Sh...  6.66 us
    pallas_call x1, Pallas kernels, spread(): pl.pallas_call(spread_kernel, grid=(count,), out_shape=jax.ShapeDtypeStru...  4.82 us
  transfers between devices with their start and end apart: 12, of which 3 were waited for; matrix products, arithmetic and copies ran while one was open for 5% of the time, Pallas kernels for 14%

profile of v3, /device:TPU:1, one launch (start us, length us, event | category | flops | bytes accessed | tf_op | source)
XLA Modules:
  0.0 111.5 jit_solution(9130478392496618591)
XLA Ops:
  0.7 1.4 %fusion.7 = (bf16[4,16384]{1,0:T(4,128)(2,1)S(1)}, f32[4,16384]{1,0:T(4,128)S(1)}) fusion(f32[16384]{0:T(1024)} %param.18, f32[4,16384]{1,0:T(4,128)} %param.14, f32[4,16384]{1,0:T(4,128)} %param.13, f32[4]{0:T(128)} %param.17), kind=kLoop, calls=%fused_computation.19 | loop fusion | flops 262144 | bytes 983056 | tf_op jit(solution)/shard_map/convert_element_type | solution.py:220
  2.1 0.3 reshape.57
  2.3 0.1 copy.29
  2.5 5.4 %collective-permute-start.7 = (bf16[256,256]{1,0:T(8,128)(2,1)S(1)}, bf16[256,256]{1,0:T(8,128)(2,1)S(1)}, u32[]{:S(2)}, u32[]{:S(2)}) collective-permute-start(bf16[256,256]{1,0:T(8,128)(2,1)S(1)} %bitcast.23), channel_id=1, source_target_pairs={{0,96},{16,112},{32,64},{48,80},{64,32},{80,48},{96,0},{112,16},{1... | collective-permute-start | bytes 393224 | tf_op jit(solution)/shard_map/ppermute | solution.py:216
  7.9 3.1 %collective-permute-start.5 = (bf16[256,256]{1,0:T(8,128)(2,1)S(1)}, bf16[256,256]{1,0:T(8,128)(2,1)S(1)}, u32[]{:S(2)}, u32[]{:S(2)}) collective-permute-start(bf16[256,256]{1,0:T(8,128)(2,1)S(1)} %bitcast.25), channel_id=1, source_target_pairs={{0,112},{16,64},{32,80},{48,96},{64,48},{80,0},{96,16},{112,32},{1... | collective-permute-start | bytes 393224 | tf_op jit(solution)/shard_map/ppermute | solution.py:216
  11.0 3.6 %collective-permute-start = (bf16[256,256]{1,0:T(8,128)(2,1)S(1)}, bf16[256,256]{1,0:T(8,128)(2,1)S(1)}, u32[]{:S(2)}, u32[]{:S(2)}) collective-permute-start(bf16[256,256]{1,0:T(8,128)(2,1)S(1)} %bitcast.27), channel_id=1, source_target_pairs={{0,48},{16,0},{32,16},{48,32},{64,112},{80,64},{96,80},{112,96},{1... | collective-permute-start | bytes 393224 | tf_op jit(solution)/shard_map/ppermute | solution.py:216
  15.3 0.7 compare_select_fusion
  16.0 5.6 %collective-permute-done.refs_3_ = bf16[256,256]{1,0:T(8,128)(2,1)S(1)} collective-permute-done((bf16[256,256]{1,0:T(8,128)(2,1)S(1)}, bf16[256,256]{1,0:T(8,128)(2,1)S(1)}, u32[]{:S(2)}, u32[]{:S(2)}) %collective-permute-start) | collective-permute-done | bytes 131104 | tf_op jit(solution)/shard_map/ppermute | solution.py:216
  21.6 0.9 collective-permute-start.2
  22.5 0.7 collective-permute-start.1
  23.2 4.3 %collective-permute-done.3.refs_2_ = bf16[256,256]{1,0:T(8,128)(2,1)S(1)} collective-permute-done((bf16[256,256]{1,0:T(8,128)(2,1)S(1)}, bf16[256,256]{1,0:T(8,128)(2,1)S(1)}, u32[]{:S(2)}, u32[]{:S(2)}) %collective-permute-start.3) | collective-permute-done | bytes 131104 | tf_op jit(solution)/shard_map/ppermute | solution.py:216
  27.5 1.8 %pick.1 = bf16[256,1024]{1,0:T(8,128)(2,1)S(1)} custom-call(s32[8]{0:T(128)S(1)} %fusion.4.base_ref, s32[1,1024]{1,0:T(1,128)S(1)} %collective-permute-done.1.index_ref.row_ref, bf16[256,256]{1,0:T(8,128)(2,1)S(1)} %bitcast.30, bf16[256,256]{1,0:T(8,128)(2,1)S(1)} %collective-permute-done.2.refs_1_, bf16[256,256]{1,0:T(8,128)(2,1)S(1)} %collective-permute-done.3.refs_2_, ...), custom_call_target="tpu_custom_call" | custom-call | tf_op jit(solution)/shard_map/pick/pallas_call | solution.py:52
  29.4 0.7 collective-permute-start.8
  30.1 3.4 %copy-done = bf16[1,1,1024,4096]{3,2,1,0:T(8,128)(2,1)S(1)} copy-done((bf16[1,1,1024,4096]{3,2,1,0:T(8,128)(2,1)S(1)}, bf16[1,1,1024,4096]{3,2,1,0:T(8,128)(2,1)}, u32[]{:S(2)}) %copy-start) | copy-done | bytes 8388632
  33.5 4.6 %forward.2 = bf16[512,256]{1,0:T(8,128)(2,1)S(1)} custom-call(s32[8]{0:T(128)S(1)} %fusion.4.base_ref, s32[1,1024]{1,0:T(1,128)S(1)} %compare_select_fusion.1.index_ref.col_ref, bf16[256,256]{1,0:T(8,128)(2,1)S(1)} %bitcast.31, bf16[256,256]{1,0:T(8,128)(2,1)S(1)} %collective-permute-done.2.refs_1_, bf16[256,256]{1,0:T(8,128)(2,1)S(1)} %collective-permute-done.3.refs_2_, ...), custom_call_target="tpu_custom_call" | custom-call | tf_op jit(solution)/shard_map/forward/pallas_call | solution.py:115
  38.1 0.8 collective-permute-start.9
  38.9 4.6 %forward.3 = bf16[512,256]{1,0:T(8,128)(2,1)S(1)} custom-call(s32[8]{0:T(128)S(1)} %fusion.4.base_ref, s32[1,1024]{1,0:T(1,128)S(1)} %compare_select_fusion.1.index_ref.col_ref, bf16[256,256]{1,0:T(8,128)(2,1)S(1)} %bitcast.32, bf16[256,256]{1,0:T(8,128)(2,1)S(1)} %collective-permute-done.2.refs_1_, bf16[256,256]{1,0:T(8,128)(2,1)S(1)} %collective-permute-done.3.refs_2_, ...), custom_call_target="tpu_custom_call" | custom-call | tf_op jit(solution)/shard_map/forward/pallas_call | solution.py:115
  43.4 0.7 collective-permute-start.10
  44.2 6.7 %backward.1.back_ref = bf16[1024,256]{1,0:T(8,128)(2,1)S(1)} custom-call(bf16[256,1024]{1,0:T(8,128)(2,1)S(1)} %collective-permute-done.8.y_ref, bf16[4096,256]{1,0:T(8,128)(2,1)S(1)} %copy-done.1, bf16[1024,4096]{1,0:T(8,128)(2,1)S(1)} %bitcast.22), custom_call_target="tpu_custom_call" | custom-call | tf_op jit(solution)/shard_map/backward/pallas_call | solution.py:161
  50.9 4.8 %spread.1 = bf16[8,256,256]{2,1,0:T(8,128)(2,1)} custom-call(s32[1,1024]{1,0:T(1,128)S(1)} %compare_select_fusion.1.index_ref.col_ref, s32[1,1024]{1,0:T(1,128)S(1)} %collective-permute-done.1.index_ref.row_ref, bf16[1024,256]{1,0:T(8,128)(2,1)S(1)} %backward.1.back_ref, bf16[512,256]{1,0:T(8,128)(2,1)S(1)} %collective-permute-done.9.refs_0_, ...), custom_call_target="tpu_custom_call" | custom-call | tf_op jit(solution)/shard_map/spread/pallas_call | solution.py:185
  55.7 19.3 %all-to-all-start = ((bf16[8,256,256]{2,1,0:T(8,128)(2,1)}), bf16[8,256,256]{2,1,0:T(8,128)(2,1)S(1)}, u32[]{:S(2)}, u32[]{:S(2)}) async-start(bf16[8,256,256]{2,1,0:T(8,128)(2,1)} %spread.1), calls=%async_computation | async-start | bytes 2097152 | tf_op jit(solution)/shard_map/all_to_all | solution.py:233
  75.0 2.5 %concatenate.14 = f32[20,16384]{1,0:T(8,128)S(1)} concatenate(f32[4,16384]{1,0:T(4,128)S(1)} %copy-done.2, f32[4,16384]{1,0:T(4,128)S(1)} %get-tuple-element.6, f32[4,16384]{1,0:T(4,128)} %param.15, f32[4,16384]{1,0:T(4,128)S(1)} %copy-done.3, f32[4,16384]{1,0:T(4,128)} %param.16), dimensions={0} | concatenate | bytes 2621440 | tf_op jit(solution)/shard_map/concatenate | solution.py:238
  77.5 2.6 %fusion.1 = f32[12,20]{1,0:T(8,128)S(1)} fusion(f32[20,16384]{1,0:T(8,128)S(1)} %concatenate.14, f32[4,16384]{1,0:T(4,128)} %param.15, f32[4,16384]{1,0:T(4,128)S(1)} %get-tuple-element.6, f32[4,16384]{1,0:T(4,128)S(1)} %copy-done.2), kind=kOutput, calls=%fused_computation.3 | convolution fusion | flops 47579136 | bytes 2098112 | tf_op jit(solution)/shard_map/dot_general | solution.py:239
  80.1 9.9 %all-to-all-done = bf16[8,256,256]{2,1,0:T(8,128)(2,1)S(1)} async-done(((bf16[8,256,256]{2,1,0:T(8,128)(2,1)}), bf16[8,256,256]{2,1,0:T(8,128)(2,1)S(1)}, u32[]{:S(2)}, u32[]{:S(2)}) %all-to-all-start) | async-done | bytes 1048608 | tf_op jit(solution)/shard_map/all_to_all | solution.py:233
  90.0 0.1 convert_reduce_fusion
  90.1 0.1 copy.30
  90.3 0.2 copy.31
  90.5 0.2 reshape.60
  90.7 1.5 %fusion = f32[12,4]{1,0:T(8,128)S(1)} fusion(f32[4,16384]{1,0:T(4,128)S(1)} %reshape.60, f32[4,16384]{1,0:T(4,128)S(1)} %copy-done.4, f32[4,16384]{1,0:T(4,128)S(1)} %get-tuple-element.6, f32[4,16384]{1,0:T(4,128)S(1)} %copy-done.2), kind=kOutput, calls=%fused_computation.2 | convolution fusion | flops 9830400 | bytes 1048768 | tf_op jit(solution)/shard_map/dot_general | solution.py:240
  92.4 18.0 %all_to_all.10 = f32[128,3,128]{2,1,0:T(4,128)S(1)} all-to-all(f32[128,3,128]{2,1,0:T(4,128)S(1)} %broadcast_in_dim.18), channel_id=1, replica_groups=mesh['row'=8,'col'=16] {'row','col'}, dimensions={0} | all-to-all | bytes 393216 | tf_op jit(solution)/shard_map/all_to_all | solution.py:244
  110.5 0.1 reduce_sum.19
  110.8 0.7 pad_maximum_fusion.4
  (45 shorter events, 0.5 us)
Async XLA Ops:
  0.6 22.5 %copy-start.8 = (s32[8]{0:T(128)S(1)}, s32[8]{0:T(128)}, u32[]{:S(2)}) copy-start(s32[8]{0:T(128)} %constant.66) | copy-start | bytes 100
  0.6 22.5 %copy-start.9 = (s32[8]{0:T(128)S(1)}, s32[8]{0:T(128)}, u32[]{:S(2)}) copy-start(s32[8]{0:T(128)} %constant.58.clone) | copy-start | bytes 100
  0.7 29.4 %copy-start.1 = (bf16[4096,256]{1,0:T(8,128)(2,1)S(1)}, bf16[4096,256]{1,0:T(8,128)(2,1)}, u32[]{:S(2)}) copy-start(bf16[4096,256]{1,0:T(8,128)(2,1)} %constant.57.clone.route_ref.refs_8_) | copy-start | bytes 6291460
  0.7 29.4 %copy-start.7 = (s32[1,1,1024]{2,1,0:T(1,128)S(1)}, s32[1,1,1024]{2,1,0:T(1,128)}, u32[]{:S(2)}) copy-start(s32[1,1,1024]{2,1,0:T(1,128)} %param.21) | copy-start | bytes 12292
  2.5 19.1 %collective-permute-start.7 = (bf16[256,256]{1,0:T(8,128)(2,1)S(1)}, bf16[256,256]{1,0:T(8,128)(2,1)S(1)}, u32[]{:S(2)}, u32[]{:S(2)}) collective-permute-start(bf16[256,256]{1,0:T(8,128)(2,1)S(1)} %bitcast.23), channel_id=1, source_target_pairs={{0,96},{16,112},{32,64},{48,80},{64,32},{80,48},{96,0},{112,16},{1... | collective-permute-start | bytes 393224 | tf_op jit(solution)/shard_map/ppermute | solution.py:216
  7.9 14.6 %collective-permute-start.6 = (bf16[256,256]{1,0:T(8,128)(2,1)S(1)}, bf16[256,256]{1,0:T(8,128)(2,1)S(1)}, u32[]{:S(2)}, u32[]{:S(2)}) collective-permute-start(bf16[256,256]{1,0:T(8,128)(2,1)S(1)} %bitcast.24), channel_id=1, source_target_pairs={{0,32},{16,48},{32,0},{48,16},{64,96},{80,112},{96,64},{112,80},{1... | collective-permute-start | bytes 393224 | tf_op jit(solution)/shard_map/ppermute | solution.py:216
  7.9 15.3 %collective-permute-start.5 = (bf16[256,256]{1,0:T(8,128)(2,1)S(1)}, bf16[256,256]{1,0:T(8,128)(2,1)S(1)}, u32[]{:S(2)}, u32[]{:S(2)}) collective-permute-start(bf16[256,256]{1,0:T(8,128)(2,1)S(1)} %bitcast.25), channel_id=1, source_target_pairs={{0,112},{16,64},{32,80},{48,96},{64,48},{80,0},{96,16},{112,32},{1... | collective-permute-start | bytes 393224 | tf_op jit(solution)/shard_map/ppermute | solution.py:216
  11.0 12.2 %collective-permute-start.4 = (bf16[256,256]{1,0:T(8,128)(2,1)S(1)}, bf16[256,256]{1,0:T(8,128)(2,1)S(1)}, u32[]{:S(2)}, u32[]{:S(2)}) collective-permute-start(bf16[256,256]{1,0:T(8,128)(2,1)S(1)} %bitcast.26), channel_id=1, source_target_pairs={{0,80},{16,96},{32,112},{48,64},{64,16},{80,32},{96,48},{112,0},{1... | collective-permute-start | bytes 393224 | tf_op jit(solution)/shard_map/ppermute | solution.py:216
  11.0 10.5 %collective-permute-start = (bf16[256,256]{1,0:T(8,128)(2,1)S(1)}, bf16[256,256]{1,0:T(8,128)(2,1)S(1)}, u32[]{:S(2)}, u32[]{:S(2)}) collective-permute-start(bf16[256,256]{1,0:T(8,128)(2,1)S(1)} %bitcast.27), channel_id=1, source_target_pairs={{0,48},{16,0},{32,16},{48,32},{64,112},{80,64},{96,80},{112,96},{1... | collective-permute-start | bytes 393224 | tf_op jit(solution)/shard_map/ppermute | solution.py:216
  21.6 5.9 %collective-permute-start.3 = (bf16[256,256]{1,0:T(8,128)(2,1)S(1)}, bf16[256,256]{1,0:T(8,128)(2,1)S(1)}, u32[]{:S(2)}, u32[]{:S(2)}) collective-permute-start(bf16[256,256]{1,0:T(8,128)(2,1)S(1)} %bitcast.28), channel_id=1, source_target_pairs={{0,16},{16,32},{32,48},{48,0},{64,80},{80,96},{96,112},{112,64},{1... | collective-permute-start | bytes 393224 | tf_op jit(solution)/shard_map/ppermute | solution.py:216
  21.6 5.9 %collective-permute-start.2 = (bf16[256,256]{1,0:T(8,128)(2,1)S(1)}, bf16[256,256]{1,0:T(8,128)(2,1)S(1)}, u32[]{:S(2)}, u32[]{:S(2)}) collective-permute-start(bf16[256,256]{1,0:T(8,128)(2,1)S(1)} %bitcast.29), channel_id=1, source_target_pairs={{0,64},{16,80},{32,96},{48,112},{64,0},{80,16},{96,32},{112,48},{1... | collective-permute-start | bytes 393224 | tf_op jit(solution)/shard_map/ppermute | solution.py:216
  22.5 5.0 %collective-permute-start.1 = (s32[1,1024]{1,0:T(1,128)S(1)}, s32[1,1024]{1,0:T(1,128)S(1)}, u32[]{:S(2)}, u32[]{:S(2)}) collective-permute-start(s32[1,1024]{1,0:T(1,128)S(1)} %compare_select_fusion), channel_id=1, source_target_pairs={{0,0},{1,1},{2,2},{3,3},{4,4},{5,5},{6,6},{7,7},{8,8},{9,9},{10,10... | collective-permute-start | bytes 12296 | tf_op jit(solution)/shard_map/ppermute | solution.py:213
  29.4 14.8 %collective-permute-start.8 = (bf16[256,1024]{1,0:T(8,128)(2,1)S(1)}, bf16[256,1024]{1,0:T(8,128)(2,1)S(1)}, u32[]{:S(2)}, u32[]{:S(2)}) collective-permute-start(bf16[256,1024]{1,0:T(8,128)(2,1)S(1)} %pick.1), channel_id=1, source_target_pairs={{0,0},{1,1},{2,2},{3,3},{4,4},{5,5},{6,6},{7,7},{8,8},{9,9},{10,10... | collective-permute-start | bytes 1572872 | tf_op jit(solution)/shard_map/ppermute | solution.py:213
  30.1 3.4 %copy-start = (bf16[1,1,1024,4096]{3,2,1,0:T(8,128)(2,1)S(1)}, bf16[1,1,1024,4096]{3,2,1,0:T(8,128)(2,1)}, u32[]{:S(2)}) copy-start(bf16[1,1,1024,4096]{3,2,1,0:T(8,128)(2,1)} %param.19) | copy-start | bytes 25165828
  33.5 10.7 %slice-start = ((s8[8388608]{0:T(1024)(128)(4,1)}), s8[4194304]{0:T(1024)(128)(4,1)S(1)}, s32[]{:S(2)}) async-start(s8[8388608]{0:T(1024)(128)(4,1)} %bitcast.20), calls=%async_computation.2 | async-start | bytes 8388608
  38.0 6.1 %slice-start.1 = ((s8[8388608]{0:T(1024)(128)(4,1)}), s8[4194304]{0:T(1024)(128)(4,1)S(1)}, s32[]{:S(2)}) async-start(s8[8388608]{0:T(1024)(128)(4,1)} %bitcast.20), calls=%async_computation.3 | async-start | bytes 8388608
  38.1 12.8 %collective-permute-start.9 = (bf16[512,256]{1,0:T(8,128)(2,1)S(1)}, bf16[512,256]{1,0:T(8,128)(2,1)S(1)}, u32[]{:S(2)}, u32[]{:S(2)}) collective-permute-start(bf16[512,256]{1,0:T(8,128)(2,1)S(1)} %forward.2), channel_id=1, source_target_pairs={{0,0},{1,1},{2,2},{3,3},{4,4},{5,5},{6,6},{7,7},{8,8},{9,9},{10,10... | collective-permute-start | bytes 786440 | tf_op jit(solution)/shard_map/ppermute | solution.py:213
  43.4 7.4 %collective-permute-start.10 = (bf16[512,256]{1,0:T(8,128)(2,1)S(1)}, bf16[512,256]{1,0:T(8,128)(2,1)S(1)}, u32[]{:S(2)}, u32[]{:S(2)}) collective-permute-start(bf16[512,256]{1,0:T(8,128)(2,1)S(1)} %forward.3), channel_id=1, source_target_pairs={{0,0},{1,1},{2,2},{3,3},{4,4},{5,5},{6,6},{7,7},{8,8},{9,9},{10,10... | collective-permute-start | bytes 786440 | tf_op jit(solution)/shard_map/ppermute | solution.py:213
  55.7 19.3 %copy-start.2 = (f32[4,16384]{1,0:T(4,128)S(1)}, f32[4,16384]{1,0:T(4,128)}, u32[]{:S(2)}) copy-start(f32[4,16384]{1,0:T(4,128)} %param.13) | copy-start | bytes 786436
  55.7 19.3 %copy-start.3 = (f32[4,16384]{1,0:T(4,128)S(1)}, f32[4,16384]{1,0:T(4,128)}, u32[]{:S(2)}) copy-start(f32[4,16384]{1,0:T(4,128)} %param.14) | copy-start | bytes 786436
  55.7 34.3 %all-to-all-start = ((bf16[8,256,256]{2,1,0:T(8,128)(2,1)}), bf16[8,256,256]{2,1,0:T(8,128)(2,1)S(1)}, u32[]{:S(2)}, u32[]{:S(2)}) async-start(bf16[8,256,256]{2,1,0:T(8,128)(2,1)} %spread.1), calls=%async_computation | async-start | bytes 2097152 | tf_op jit(solution)/shard_map/all_to_all | solution.py:233
  80.1 10.6 %copy-start.4 = (f32[4,16384]{1,0:T(4,128)S(1)}, f32[4,16384]{1,0:T(4,128)}, u32[]{:S(2)}) copy-start(f32[4,16384]{1,0:T(4,128)} %param.15) | copy-start | bytes 786436
  90.7 20.8 %copy-start.5 = (f32[4,16384]{1,0:T(4,128)}, f32[4,16384]{1,0:T(4,128)S(1)}, u32[]{:S(2)}) copy-start(f32[4,16384]{1,0:T(4,128)S(1)} %reshape.60) | copy-start | bytes 786436
  110.7 0.8 copy-start.6

commit v4 on v3

--- a/solution.py
+++ b/solution.py
@@ -1,4 +1,5 @@
 import functools
+
 import jax
 import jax.numpy as jnp
 import numpy as np
@@ -13,7 +14,7 @@
 GROUP = 16
 HALF = PAIRS // 2
 SIZE = PAIRS * GROUP
-STEP = 512
+WIDTH = 1024
 BOTH = ("row", "col")
 NT = (((1,), (1,)), ((), ()))
 NN = (((1,), (0,)), ((), ()))
@@ -44,19 +45,32 @@
 
 
 def pick_kernel(base_ref, index_ref, *refs):
-    refs[-1][...] = gathered(base_ref, index_ref[...], refs[:-1]).astype(BF16)
+    pieces, (out_ref, turned_ref) = refs[:-2], refs[-2:]
+    turned_ref[...] = turned_slots(index_ref[...])
+    out_ref[...] = gathered(base_ref, index_ref[...], pieces).astype(BF16)
 
 
 def pick(bases, index, pieces):
     whole = pl.BlockSpec(memory_space=pltpu.VMEM)
     return pl.pallas_call(
         pick_kernel,
-        out_shape=jax.ShapeDtypeStruct((pieces[0].shape[0], index.shape[1]), BF16),
+        out_shape=(
+            jax.ShapeDtypeStruct((pieces[0].shape[0], index.shape[1]), BF16),
+            jax.ShapeDtypeStruct(index.shape, index.dtype),
+        ),
         in_specs=[pl.BlockSpec(memory_space=pltpu.SMEM)] + [whole] * (1 + len(pieces)),
-        out_specs=whole,
+        out_specs=(whole, whole),
         compiler_params=params(16),
         name="pick",
     )(bases, index, *pieces)
+
+
+def order_matrix(vecs):
+    place = np.arange(vecs * BLOCK)
+    pair, kind = place // GROUP, place % GROUP
+    half, k, parity = kind // (2 * vecs), kind % (2 * vecs) // 2, kind % 2
+    entry = k * BLOCK + 2 * (half * HALF + pair) + parity
+    return jnp.asarray(np.arange(vecs * BLOCK)[:, None] == entry, BF16)
 
 
 def route_matrix(vecs):
@@ -65,11 +79,33 @@
     return jnp.asarray(np.arange(vecs * BLOCK) == kind // 2 * BLOCK + 2 * pair + kind % 2, BF16)
 
 
-def own_mask(rows):
-    shape = (rows, SIZE)
-    return (
-        lax.broadcasted_iota(jnp.int32, shape, 1) % GROUP == lax.broadcasted_iota(jnp.int32, shape, 0) % GROUP
-    )
+def turned_slots(index):
+    lane = lax.broadcasted_iota(jnp.int32, (1, LANES), 1)
+    parts = []
+    for n in range(index.shape[1] // LANES):
+        part = index[:, n * LANES : (n + 1) * LANES]
+        for bit in (1, 2, 4, 8):
+            part = jnp.where(lane & bit != 0, pltpu.roll(part, bit, 1), pltpu.roll(part, LANES - bit, 1))
+        parts.append(part)
+    return jnp.concatenate(parts, 1)
+
+
+def stage_kernel(tile_ref, out_ref, sem):
+    copy = pltpu.make_async_copy(tile_ref, out_ref, sem)
+    copy.start()
+    copy.wait()
+
+
+def stage(tile):
+    return pl.pallas_call(
+        stage_kernel,
+        out_shape=jax.ShapeDtypeStruct(tile.shape, tile.dtype),
+        in_specs=[pl.BlockSpec(memory_space=pl.ANY)],
+        out_specs=pl.BlockSpec(memory_space=pltpu.VMEM),
+        scratch_shapes=[pltpu.SemaphoreType.DMA],
+        compiler_params=params(12),
+        name="stage",
+    )(tile)
 
 
 def stacked(tile_ref, at, half):
@@ -77,16 +113,16 @@
     return jnp.concatenate(parts, 0)
 
 
-def forward_kernel(vecs, base, base_ref, index_ref, *refs):
-    pieces, (route_ref, tile_ref, out_ref, x_ref, wide_ref) = refs[:-5], refs[-5:]
-    x_ref[...] = gathered(base_ref, index_ref[...], pieces).T
-    first = lax.broadcasted_iota(jnp.int32, (GROUP, LANES), 1) < BLOCK
-    own = own_mask(GROUP)
-    span = HALF * GROUP
+def forward_kernel(vecs, base_ref, index_ref, *refs):
+    pieces, (order_ref, tile_ref, out_ref, x_ref, packed_ref) = refs[:-5], refs[-5:]
+    x_ref[...] = gathered(base_ref, turned_slots(index_ref[...]), pieces).T
+    lane = lax.broadcasted_iota(jnp.int32, (GROUP, LANES), 1)
+    row = lax.broadcasted_iota(jnp.int32, (GROUP, LANES), 0)
+    first = lane < BLOCK
+    masks = [as_ones((lane + row + 1) % GROUP == n) for n in range(GROUP)]
 
     def step(g, _):
         at = pl.ds(pl.multiple_of(g * GROUP, GROUP), GROUP)
-        start = pl.ds(pl.multiple_of(base + g * GROUP, GROUP), GROUP)
         rows = []
         for p in range(vecs // 2):
             both = x_ref[at, p * LANES : (p + 1) * LANES]
@@ -98,35 +134,46 @@
                 jnp.where(first, 0.0, both),
             ]
         left = jnp.concatenate(rows, 0).astype(BF16)
+        packed = [[], []]
         for half in range(2):
-            out = dot(left, stacked(tile_ref, start, half), NT)
+            out = dot(left, stacked(tile_ref, at, half), NT).astype(BF16)
             for s in range(2 * vecs):
-                part = jnp.where(own[:, :span], out[s * GROUP : (s + 1) * GROUP], 0.0)
-                wide_ref[at, s * SIZE + half * span : s * SIZE + (half + 1) * span] = part.astype(BF16)
+                shift = half * 2 * vecs + s
+                for v in range(2):
+                    part = out[s * GROUP : (s + 1) * GROUP, v * LANES : (v + 1) * LANES]
+                    packed[v].append((pltpu.roll(part, shift, 1) if shift else part) * masks[shift])
+        for v in range(2):
+            part = sum(packed[v][1:], packed[v][0]).astype(F32)
+            part = pltpu.roll(part, LANES + 1 - GROUP, 1, stride=1, stride_axis=0)
+            packed_ref[at, v * LANES : (v + 1) * LANES] = part.astype(BF16)
         return 0
 
     lax.fori_loop(0, x_ref.shape[0] // GROUP, step, 0, unroll=8)
-    out_ref[...] = dot(wide_ref[...], route_ref[...]).astype(BF16)
-
-
-def forward(vecs, bases, index, pieces, route, tile, at):
-    wide = vecs * BLOCK
+    out_ref[...] = dot(packed_ref[...], order_ref[...], NT).astype(BF16)
+
+
+def forward(vecs, bases, index, pieces, order, tile):
+    slots, wide = tile.shape[0], vecs * BLOCK
     whole = pl.BlockSpec(memory_space=pltpu.VMEM)
     return pl.pallas_call(
-        functools.partial(forward_kernel, vecs, at * STEP),
-        grid=(1,),
-        out_shape=jax.ShapeDtypeStruct((STEP, wide), BF16),
-        in_specs=[pl.BlockSpec(memory_space=pltpu.SMEM), pl.BlockSpec((1, STEP), lambda i: (0, at))]
-        + [whole] * (len(pieces) + 2),
+        functools.partial(forward_kernel, vecs),
+        out_shape=jax.ShapeDtypeStruct((slots, wide), BF16),
+        in_specs=[pl.BlockSpec(memory_space=pltpu.SMEM)] + [whole] * (len(pieces) + 3),
         out_specs=whole,
-        scratch_shapes=[pltpu.VMEM((STEP, wide), F32), pltpu.VMEM((STEP, 2 * vecs * SIZE), BF16)],
+        scratch_shapes=[
+            pltpu.VMEM((slots, wide), F32),
+            pltpu.VMEM((slots, wide), BF16),
+        ],
         compiler_params=params(20),
         name="forward",
-    )(bases, index, *pieces, route, tile)
+    )(bases, index, *pieces, order, tile)
 
 
 def backward_kernel(vecs, y_ref, route_ref, tile_ref, out_ref, wide_ref):
-    own = own_mask(out_ref.shape[0])
+    shape = (out_ref.shape[0], SIZE)
+    own = (
+        lax.broadcasted_iota(jnp.int32, shape, 1) % GROUP == lax.broadcasted_iota(jnp.int32, shape, 0) % GROUP
+    )
     far = y_ref[...].astype(F32).T.astype(BF16)
     for s in range(2 * vecs):
         part = dot(far, route_ref[s * SIZE : (s + 1) * SIZE, :], NT)
@@ -163,34 +210,34 @@
         out_shape=jax.ShapeDtypeStruct((slots, wide), BF16),
         in_specs=[whole] * 3,
         out_specs=whole,
-        scratch_shapes=[pltpu.VMEM((slots, 2 * vecs * SIZE), BF16)],
+        scratch_shapes=[
+            pltpu.VMEM((slots, 2 * vecs * SIZE), BF16),
+        ],
         compiler_params=params(20),
         name="backward",
     )(far, route, tile)
 
 
-def spread_kernel(col_ref, row_ref, back_ref, *refs):
-    forth_refs, out_ref = refs[:-1], refs[-1]
-    count = out_ref.shape[1]
+def spread_kernel(col_ref, row_ref, back_ref, forth_ref, out_ref):
+    count = out_ref.shape[0]
     place = lax.broadcasted_iota(jnp.int32, (count, col_ref.shape[1]), 0) + pl.program_id(0) * count
     total = dot(as_ones(place == col_ref[...]), back_ref[...])
-    hot = as_ones(place == row_ref[...])
-    for n, forth in enumerate(forth_refs):
-        total += dot(hot[:, n * STEP : (n + 1) * STEP], forth[...])
-    out_ref[0] = total.astype(BF16)
-
-
-def spread(col_index, row_index, back, forth, count, width):
+    total += dot(as_ones(place == row_ref[...]), forth_ref[...])
+    out_ref[...] = total.astype(BF16)
+
+
+def spread(col_index, row_index, back, forth, blocks):
     whole = pl.BlockSpec(memory_space=pltpu.VMEM)
+    step = WIDTH
     return pl.pallas_call(
         spread_kernel,
-        grid=(count,),
-        out_shape=jax.ShapeDtypeStruct((count, width, back.shape[1]), BF16),
-        in_specs=[whole] * (3 + len(forth)),
-        out_specs=pl.BlockSpec((1, width, back.shape[1]), lambda i: (i, 0, 0)),
-        compiler_params=params(16),
+        grid=(blocks // step,),
+        out_shape=jax.ShapeDtypeStruct((blocks, back.shape[1]), BF16),
+        in_specs=[whole] * 4,
+        out_specs=pl.BlockSpec((step, back.shape[1]), lambda i: (i, 0)),
+        compiler_params=params(20),
         name="spread",
-    )(col_index, row_index, back, *forth)
+    )(col_index, row_index, back, forth)
 
 
 def body(x_vec, hx_vec, p_vec, hp_vec, theta, precond, tile_vals, tile_rows, tile_cols, tile_count):
@@ -202,7 +249,6 @@
     width = piece_len // BLOCK
     slots = tile_vals.shape[2]
     tile = tile_vals[0, 0]
-    route = route_matrix(vecs)
     residue = (hx_vec - x_vec * theta[:, None]) / precond[None, :]
     live = jnp.arange(slots, dtype=jnp.int32) < tile_count[0, 0]
     row_index = jnp.where(live, tile_rows[0, 0], -1)[None]
@@ -218,26 +264,27 @@
         )
 
     own = residue.astype(BF16).reshape(vecs, width, BLOCK).transpose(0, 2, 1).reshape(vecs * BLOCK, width)
-    offsets = [(0, 0), (1, 0), (0, 1), (0, 3), (1, 1), (1, 3), (0, 2), (1, 2)]
-    pieces = [own] + [within(own, *o) for o in offsets[1:]]
-    flips = jnp.array([o[0] for o in offsets], jnp.int32)
-    turns = jnp.array([o[1] for o in offsets], jnp.int32)
+    across = within(own, 1, 0)
+    pieces = [own, across] + [within(own, 0, n) for n in (1, 3, 2)]
+    pieces += [within(across, 0, n) for n in (1, 3, 2)]
+    flips = jnp.array([0, 1, 0, 0, 0, 1, 1, 1], jnp.int32)
+    turns = jnp.array([0, 0, 1, 3, 2, 1, 3, 2], jnp.int32)
     bases = width * ((row_pos // ring ^ flips) * ring + (row_pos % ring - turns) % ring)
-    far_index = along(lax.optimization_barrier((row_index, pieces[3]))[0], 1)
-    far = along(pick(bases, far_index, pieces), -1)
-    forth = [
-        along(forward(vecs, bases, col_index, pieces, route, tile, n), 1) for n in range(slots // STEP)
-    ]
-    back = backward(vecs, far, route, tile)
-    parts = spread(col_index, far_index, back, forth, rows, width)
+    far_index = along(lax.optimization_barrier((row_index, across))[0], 1)
+    held = stage(lax.optimization_barrier((tile, pieces[2]))[0])
+    picked, far_order = pick(bases, far_index, pieces)
+    far = along(picked, -1)
+    forth = along(forward(vecs, bases, col_index, pieces, order_matrix(vecs), held), 1)
+    back = backward(vecs, far, route_matrix(vecs), held)
+    parts = spread(col_index, far_order, back, forth, rows * width).reshape(rows, width, vecs * BLOCK)
     parts = lax.all_to_all(parts, "row", 0, 0, tiled=True)
     total = parts.astype(F32).sum(0)
     hw_vec = total.reshape(width, vecs, BLOCK).transpose(1, 0, 2).reshape(vecs, piece_len)
 
     vectors = jnp.concatenate([x_vec, residue, p_vec], 0)
     known = jnp.concatenate([vectors, hx_vec, hp_vec], 0)
-    early = jnp.dot(vectors, known.T, precision=lax.Precision.HIGHEST, preferred_element_type=jnp.float32)
-    late = jnp.dot(vectors, hw_vec.T, precision=lax.Precision.HIGHEST, preferred_element_type=jnp.float32)
+    early = jnp.dot(vectors, known.T, precision=lax.Precision.HIGHEST, preferred_element_type=F32)
+    late = jnp.dot(vectors, hw_vec.T, precision=lax.Precision.HIGHEST, preferred_element_type=F32)
     gram = jnp.concatenate([early, late], 1)
     flat = jnp.pad(gram.reshape(-1), (0, 3 * LANES - gram.size)).reshape(1, 3, LANES)
     flat = jnp.broadcast_to(flat, (rows * cols, 3, LANES))

time: 112 us -> 102 us (0.911)
  waiting for transfers between devices: 19.8 us -> 10.3 us
  starting transfers between devices: 35.2 us -> 39.1 us
  blocking collectives: 18 us -> 15.3 us
  Pallas kernels: 22.4 us -> 20 us
  other arithmetic: 3.16 us -> 4.37 us
    ppermute x7, waiting for transfers between devices: 9.91 us -> 0.54 us  [within(): lax.ppermute(block, 'row', [(i, (i // ring ^ flip) * ring + (i % ring + t...]
    all_to_all x1, starting transfers between devices: 19.3 us -> 22.1 us  [body(): parts = lax.all_to_all(parts, 'row', 0, 0, tiled=True)]
    all_to_all x1, blocking collectives: 18 us -> 15.3 us  [body(): lax.all_to_all(flat, BOTH, 0, 0, tiled=True).sum(0).reshape(-1)[:gram.size]]
    pallas_call x4, Pallas kernels: 15.8 us -> 13.4 us  [the longest x1 7.71 us: forward(): pl.pallas_call(functools.partial(forward_kernel, vecs), out_shape=jax.Sha...]
    ppermute x7, starting transfers between devices: 13.1 us -> 14.8 us  [within(): lax.ppermute(block, 'row', [(i, (i // ring ^ flip) * ring + (i % ring + t...]
    ppermute x4 -> x3, starting transfers between devices: 2.83 us -> 2.18 us  [along(): return lax.ppermute(block, BOTH, path)]
    unnamed x24 -> x16, local copies, waits for them, and re-layouts: 3.44 us -> 3.42 us
  transfers between devices with their start and end apart: 12 -> 11, of which waited for: 3 -> 2; matrix products, arithmetic and copies ran while one was open for 5% -> 7% of each run, Pallas kernels for 14% -> 15%
where the time goes in v4:
time: 102 us
  starting transfers between devices  39.1 us (38%)
  Pallas kernels  20 us (20%)
  blocking collectives  15.3 us (15%)
  waiting for transfers between devices  10.3 us (10%)
  local copies, waits for them, and re-layouts  7.11 us (7%)
  other arithmetic  4.37 us (4%)
  matrix products  4.09 us (4%)
  between operations  1.56 us (2%)
    all_to_all x1, starting transfers between devices, body(): parts = lax.all_to_all(parts, 'row', 0, 0, tiled=True)  22.1 us
    all_to_all x1, blocking collectives, body(): lax.all_to_all(flat, BOTH, 0, 0, tiled=True).sum(0).reshape(-1)[:gram.size]  15.3 us
    ppermute x7, starting transfers between devices, within(): lax.ppermute(block, 'row', [(i, (i // ring ^ flip) * ring + (i % ring + t...  14.8 us
    all_to_all x1, waiting for transfers between devices, body(): parts = lax.all_to_all(parts, 'row', 0, 0, tiled=True)  9.79 us
    pallas_call x1, Pallas kernels, forward(): pl.pallas_call(functools.partial(forward_kernel, vecs), out_shape=jax.Sha...  7.71 us
    pallas_call x1, Pallas kernels, backward(): pl.pallas_call(functools.partial(backward_kernel, vecs), out_shape=jax.Sh...  6.55 us
    unnamed x16, local copies, waits for them, and re-layouts  3.42 us
    pallas_call x1, Pallas kernels, spread(): pl.pallas_call(spread_kernel, grid=(blocks // step,), out_shape=jax.Shape...  3.35 us
  transfers between devices with their start and end apart: 11, of which 2 were waited for; matrix products, arithmetic and copies ran while one was open for 7% of the time, Pallas kernels for 15%

profile of v4, /device:TPU:1, one launch (start us, length us, event | category | flops | bytes accessed | tf_op | source)
XLA Modules:
  0.0 101.9 jit_solution(15549220772587761463)
XLA Ops:
  0.6 1.2 %fusion.7 = (bf16[4,16384]{1,0:T(4,128)(2,1)S(1)}, f32[4,16384]{1,0:T(4,128)S(1)}) fusion(f32[16384]{0:T(1024)} %param.19, f32[4,16384]{1,0:T(4,128)} %param.15, f32[4,16384]{1,0:T(4,128)} %param.14, f32[4]{0:T(128)} %param.18), kind=kLoop, calls=%fused_computation.19 | loop fusion | flops 262144 | bytes 983056 | tf_op jit(solution)/shard_map/convert_element_type | solution.py:266
  1.9 0.3 reshape.60
  2.3 2.1 %collective-permute-start = (bf16[256,256]{1,0:T(8,128)(2,1)S(1)}, bf16[256,256]{1,0:T(8,128)(2,1)S(1)}, u32[]{:S(2)}, u32[]{:S(2)}) collective-permute-start(bf16[256,256]{1,0:T(8,128)(2,1)S(1)} %bitcast.20), channel_id=1, source_target_pairs={{0,64},{16,80},{32,96},{48,112},{64,0},{80,16},{96,32},{112,48},{1... | collective-permute-start | bytes 393224 | tf_op jit(solution)/shard_map/ppermute | solution.py:262
  4.4 1.6 %collective-permute-start.2 = (bf16[256,256]{1,0:T(8,128)(2,1)S(1)}, bf16[256,256]{1,0:T(8,128)(2,1)S(1)}, u32[]{:S(2)}, u32[]{:S(2)}) collective-permute-start(bf16[256,256]{1,0:T(8,128)(2,1)S(1)} %bitcast.21), channel_id=1, source_target_pairs={{0,16},{16,32},{32,48},{48,0},{64,80},{80,96},{96,112},{112,64},{1... | collective-permute-start | bytes 393224 | tf_op jit(solution)/shard_map/ppermute | solution.py:262
  6.0 2.1 %collective-permute-start.3 = (bf16[256,256]{1,0:T(8,128)(2,1)S(1)}, bf16[256,256]{1,0:T(8,128)(2,1)S(1)}, u32[]{:S(2)}, u32[]{:S(2)}) collective-permute-start(bf16[256,256]{1,0:T(8,128)(2,1)S(1)} %bitcast.22), channel_id=1, source_target_pairs={{0,48},{16,0},{32,16},{48,32},{64,112},{80,64},{96,80},{112,96},{1... | collective-permute-start | bytes 393224 | tf_op jit(solution)/shard_map/ppermute | solution.py:262
  8.2 1.3 %collective-permute-start.4 = (bf16[256,256]{1,0:T(8,128)(2,1)S(1)}, bf16[256,256]{1,0:T(8,128)(2,1)S(1)}, u32[]{:S(2)}, u32[]{:S(2)}) collective-permute-start(bf16[256,256]{1,0:T(8,128)(2,1)S(1)} %bitcast.23), channel_id=1, source_target_pairs={{0,32},{16,48},{32,0},{48,16},{64,96},{80,112},{96,64},{112,80},{1... | collective-permute-start | bytes 393224 | tf_op jit(solution)/shard_map/ppermute | solution.py:262
  10.1 0.7 compare_select_fusion.1.index_ref.col_ref
  10.8 0.7 compare_select_fusion
  11.5 0.7 collective-permute-start.1
  12.2 5.0 %collective-permute-start.5 = (bf16[256,256]{1,0:T(8,128)(2,1)S(1)}, bf16[256,256]{1,0:T(8,128)(2,1)S(1)}, u32[]{:S(2)}, u32[]{:S(2)}) collective-permute-start(bf16[256,256]{1,0:T(8,128)(2,1)S(1)} %collective-permute-done.refs_1_), channel_id=1, source_target_pairs={{0,16},{16,32},{32,48},{48,0},{64,80},{80,96},{96,112},{112,64},{1... | collective-permute-start | bytes 393224 | tf_op jit(solution)/shard_map/ppermute | solution.py:262
  17.2 1.4 %collective-permute-start.6 = (bf16[256,256]{1,0:T(8,128)(2,1)S(1)}, bf16[256,256]{1,0:T(8,128)(2,1)S(1)}, u32[]{:S(2)}, u32[]{:S(2)}) collective-permute-start(bf16[256,256]{1,0:T(8,128)(2,1)S(1)} %collective-permute-done.refs_1_), channel_id=1, source_target_pairs={{0,48},{16,0},{32,16},{48,32},{64,112},{80,64},{96,80},{112,96},{1... | collective-permute-start | bytes 393224 | tf_op jit(solution)/shard_map/ppermute | solution.py:262
  18.6 1.2 %collective-permute-start.7 = (bf16[256,256]{1,0:T(8,128)(2,1)S(1)}, bf16[256,256]{1,0:T(8,128)(2,1)S(1)}, u32[]{:S(2)}, u32[]{:S(2)}) collective-permute-start(bf16[256,256]{1,0:T(8,128)(2,1)S(1)} %collective-permute-done.refs_1_), channel_id=1, source_target_pairs={{0,32},{16,48},{32,0},{48,16},{64,96},{80,112},{96,64},{112,80},{1... | collective-permute-start | bytes 393224 | tf_op jit(solution)/shard_map/ppermute | solution.py:262
  19.8 0.7 fusion.4.base_ref
  20.5 3.4 %copy-done = bf16[1,1,1024,4096]{3,2,1,0:T(8,128)(2,1)S(1)} copy-done((bf16[1,1,1024,4096]{3,2,1,0:T(8,128)(2,1)S(1)}, bf16[1,1,1024,4096]{3,2,1,0:T(8,128)(2,1)}, u32[]{:S(2)}) %copy-start) | copy-done | bytes 8388632
  23.9 0.6 stage.1.tile_ref.refs_9_
  24.5 0.5 collective-permute-done.7.refs_7_
  25.0 1.8 %pick.1 = (bf16[256,1024]{1,0:T(8,128)(2,1)S(1)}, s32[1,1024]{1,0:T(1,128)S(1)}) custom-call(s32[8]{0:T(128)S(1)} %fusion.4.base_ref, s32[1,1024]{1,0:T(1,128)S(1)} %collective-permute-done.1.index_ref, bf16[256,256]{1,0:T(8,128)(2,1)S(1)} %bitcast.24, bf16[256,256]{1,0:T(8,128)(2,1)S(1)} %collective-permute-done.refs_1_, ...), custom_call_target="tpu_custom_call" | custom-call | tf_op jit(solution)/shard_map/pick/pallas_call | solution.py:55
  26.9 0.8 collective-permute-start.8
  27.7 7.7 %forward.1 = bf16[1024,256]{1,0:T(8,128)(2,1)S(1)} custom-call(s32[8]{0:T(128)S(1)} %fusion.4.base_ref, s32[1,1024]{1,0:T(1,128)S(1)} %compare_select_fusion.1.index_ref.col_ref, bf16[256,256]{1,0:T(8,128)(2,1)S(1)} %bitcast.25, bf16[256,256]{1,0:T(8,128)(2,1)S(1)} %collective-permute-done.refs_1_, bf16[256,256]{1,0:T(8,128)(2,1)S(1)} %collective-permute-done.2.refs_2_, ...), custom_call_target="tpu_custom_call" | custom-call | tf_op jit(solution)/shard_map/forward/pallas_call | solution.py:158
  35.4 0.7 collective-permute-start.9
  36.1 6.6 %backward.1.back_ref = bf16[1024,256]{1,0:T(8,128)(2,1)S(1)} custom-call(bf16[256,1024]{1,0:T(8,128)(2,1)S(1)} %collective-permute-done.8.y_ref, bf16[4096,256]{1,0:T(8,128)(2,1)S(1)} %copy-done.1, bf16[1024,4096]{1,0:T(8,128)(2,1)S(1)} %stage.1.tile_ref.refs_9_), custom_call_target="tpu_custom_call" | custom-call | tf_op jit(solution)/shard_map/backward/pallas_call | solution.py:208
  42.7 3.3 %spread.1 = bf16[2048,256]{1,0:T(8,128)(2,1)} custom-call(s32[1,1024]{1,0:T(1,128)S(1)} %compare_select_fusion.1.index_ref.col_ref, s32[1,1024]{1,0:T(1,128)S(1)} %get-tuple-element.8.row_ref, bf16[1024,256]{1,0:T(8,128)(2,1)S(1)} %backward.1.back_ref, bf16[1024,256]{1,0:T(8,128)(2,1)S(1)} %collective-permute-done.9.forth_ref), custom_call_target="tpu_custom_call" | custom-call | tf_op jit(solution)/shard_map/spread/pallas_call | solution.py:232
  46.1 22.1 %all-to-all-start = ((bf16[8,256,256]{2,1,0:T(8,128)(2,1)}), bf16[8,256,256]{2,1,0:T(8,128)(2,1)S(1)}, u32[]{:S(2)}, u32[]{:S(2)}) async-start(bf16[8,256,256]{2,1,0:T(8,128)(2,1)} %bitcast.6), calls=%async_computation | async-start | bytes 2097152 | tf_op jit(solution)/shard_map/all_to_all | solution.py:280
  68.2 2.5 %concatenate.14 = f32[20,16384]{1,0:T(8,128)S(1)} concatenate(f32[4,16384]{1,0:T(4,128)S(1)} %copy-done.3, f32[4,16384]{1,0:T(4,128)S(1)} %get-tuple-element.12, f32[4,16384]{1,0:T(4,128)} %param.16, f32[4,16384]{1,0:T(4,128)S(1)} %copy-done.4, f32[4,16384]{1,0:T(4,128)} %param.17), dimensions={0} | concatenate | bytes 2621440 | tf_op jit(solution)/shard_map/concatenate | solution.py:285
  70.7 2.6 %fusion.1 = f32[12,20]{1,0:T(8,128)S(1)} fusion(f32[20,16384]{1,0:T(8,128)S(1)} %concatenate.14, f32[4,16384]{1,0:T(4,128)} %param.16, f32[4,16384]{1,0:T(4,128)S(1)} %get-tuple-element.12, f32[4,16384]{1,0:T(4,128)S(1)} %copy-done.3), kind=kOutput, calls=%fused_computation.3 | convolution fusion | flops 47579136 | bytes 2098112 | tf_op jit(solution)/shard_map/dot_general | solution.py:286
  73.3 9.8 %all-to-all-done = bf16[8,256,256]{2,1,0:T(8,128)(2,1)S(1)} async-done(((bf16[8,256,256]{2,1,0:T(8,128)(2,1)}), bf16[8,256,256]{2,1,0:T(8,128)(2,1)S(1)}, u32[]{:S(2)}, u32[]{:S(2)}) %all-to-all-start) | async-done | bytes 1048608 | tf_op jit(solution)/shard_map/all_to_all | solution.py:280
  83.4 0.2 copy.32
  83.6 0.2 reshape.64
  83.8 1.5 %fusion = f32[12,4]{1,0:T(8,128)S(1)} fusion(f32[4,16384]{1,0:T(4,128)S(1)} %reshape.64, f32[4,16384]{1,0:T(4,128)S(1)} %copy-done.5, f32[4,16384]{1,0:T(4,128)S(1)} %get-tuple-element.12, f32[4,16384]{1,0:T(4,128)S(1)} %copy-done.3), kind=kOutput, calls=%fused_computation.2 | convolution fusion | flops 9830400 | bytes 1048768 | tf_op jit(solution)/shard_map/dot_general | solution.py:287
  85.6 15.3 %all_to_all.10 = f32[128,3,128]{2,1,0:T(4,128)S(1)} all-to-all(f32[128,3,128]{2,1,0:T(4,128)S(1)} %broadcast_in_dim.18), channel_id=1, replica_groups=mesh['row'=8,'col'=16] {'row','col'}, dimensions={0} | all-to-all | bytes 393216 | tf_op jit(solution)/shard_map/all_to_all | solution.py:291
  100.9 0.1 reduce_sum.19
  101.2 0.7 pad_maximum_fusion.4
  (34 shorter events, 0.8 us)
Async XLA Ops:
  2.3 9.2 %collective-permute-start = (bf16[256,256]{1,0:T(8,128)(2,1)S(1)}, bf16[256,256]{1,0:T(8,128)(2,1)S(1)}, u32[]{:S(2)}, u32[]{:S(2)}) collective-permute-start(bf16[256,256]{1,0:T(8,128)(2,1)S(1)} %bitcast.20), channel_id=1, source_target_pairs={{0,64},{16,80},{32,96},{48,112},{64,0},{80,16},{96,32},{112,48},{1... | collective-permute-start | bytes 393224 | tf_op jit(solution)/shard_map/ppermute | solution.py:262
  4.4 12.8 %collective-permute-start.2 = (bf16[256,256]{1,0:T(8,128)(2,1)S(1)}, bf16[256,256]{1,0:T(8,128)(2,1)S(1)}, u32[]{:S(2)}, u32[]{:S(2)}) collective-permute-start(bf16[256,256]{1,0:T(8,128)(2,1)S(1)} %bitcast.21), channel_id=1, source_target_pairs={{0,16},{16,32},{32,48},{48,0},{64,80},{80,96},{96,112},{112,64},{1... | collective-permute-start | bytes 393224 | tf_op jit(solution)/shard_map/ppermute | solution.py:262
  6.0 12.6 %collective-permute-start.3 = (bf16[256,256]{1,0:T(8,128)(2,1)S(1)}, bf16[256,256]{1,0:T(8,128)(2,1)S(1)}, u32[]{:S(2)}, u32[]{:S(2)}) collective-permute-start(bf16[256,256]{1,0:T(8,128)(2,1)S(1)} %bitcast.22), channel_id=1, source_target_pairs={{0,48},{16,0},{32,16},{48,32},{64,112},{80,64},{96,80},{112,96},{1... | collective-permute-start | bytes 393224 | tf_op jit(solution)/shard_map/ppermute | solution.py:262
  8.2 16.3 %collective-permute-start.4 = (bf16[256,256]{1,0:T(8,128)(2,1)S(1)}, bf16[256,256]{1,0:T(8,128)(2,1)S(1)}, u32[]{:S(2)}, u32[]{:S(2)}) collective-permute-start(bf16[256,256]{1,0:T(8,128)(2,1)S(1)} %bitcast.23), channel_id=1, source_target_pairs={{0,32},{16,48},{32,0},{48,16},{64,96},{80,112},{96,64},{112,80},{1... | collective-permute-start | bytes 393224 | tf_op jit(solution)/shard_map/ppermute | solution.py:262
  11.5 12.9 %collective-permute-start.1 = (s32[1,1024]{1,0:T(1,128)S(1)}, s32[1,1024]{1,0:T(1,128)S(1)}, u32[]{:S(2)}, u32[]{:S(2)}) collective-permute-start(s32[1,1024]{1,0:T(1,128)S(1)} %compare_select_fusion), channel_id=1, source_target_pairs={{0,0},{1,1},{2,2},{3,3},{4,4},{5,5},{6,6},{7,7},{8,8},{9,9},{10,10... | collective-permute-start | bytes 12296 | tf_op jit(solution)/shard_map/ppermute | solution.py:259
  12.2 12.3 %collective-permute-start.5 = (bf16[256,256]{1,0:T(8,128)(2,1)S(1)}, bf16[256,256]{1,0:T(8,128)(2,1)S(1)}, u32[]{:S(2)}, u32[]{:S(2)}) collective-permute-start(bf16[256,256]{1,0:T(8,128)(2,1)S(1)} %collective-permute-done.refs_1_), channel_id=1, source_target_pairs={{0,16},{16,32},{32,48},{48,0},{64,80},{80,96},{96,112},{112,64},{1... | collective-permute-start | bytes 393224 | tf_op jit(solution)/shard_map/ppermute | solution.py:262
  17.2 7.3 %collective-permute-start.6 = (bf16[256,256]{1,0:T(8,128)(2,1)S(1)}, bf16[256,256]{1,0:T(8,128)(2,1)S(1)}, u32[]{:S(2)}, u32[]{:S(2)}) collective-permute-start(bf16[256,256]{1,0:T(8,128)(2,1)S(1)} %collective-permute-done.refs_1_), channel_id=1, source_target_pairs={{0,48},{16,0},{32,16},{48,32},{64,112},{80,64},{96,80},{112,96},{1... | collective-permute-start | bytes 393224 | tf_op jit(solution)/shard_map/ppermute | solution.py:262
  18.6 6.4 %collective-permute-start.7 = (bf16[256,256]{1,0:T(8,128)(2,1)S(1)}, bf16[256,256]{1,0:T(8,128)(2,1)S(1)}, u32[]{:S(2)}, u32[]{:S(2)}) collective-permute-start(bf16[256,256]{1,0:T(8,128)(2,1)S(1)} %collective-permute-done.refs_1_), channel_id=1, source_target_pairs={{0,32},{16,48},{32,0},{48,16},{64,96},{80,112},{96,64},{112,80},{1... | collective-permute-start | bytes 393224 | tf_op jit(solution)/shard_map/ppermute | solution.py:262
  20.5 3.4 %copy-start = (bf16[1,1,1024,4096]{3,2,1,0:T(8,128)(2,1)S(1)}, bf16[1,1,1024,4096]{3,2,1,0:T(8,128)(2,1)}, u32[]{:S(2)}) copy-start(bf16[1,1,1024,4096]{3,2,1,0:T(8,128)(2,1)} %param.20) | copy-start | bytes 25165828
  23.9 3.8 %copy-start.2 = (bf16[256,256]{1,0:T(8,128)(2,1)S(1)}, bf16[256,256]{1,0:T(8,128)(2,1)}, u32[]{:S(2)}) copy-start(bf16[256,256]{1,0:T(8,128)(2,1)} %constant.61.clone.refs_8_) | copy-start | bytes 393220
  26.8 9.3 %copy-start.1 = (bf16[4096,256]{1,0:T(8,128)(2,1)S(1)}, bf16[4096,256]{1,0:T(8,128)(2,1)}, u32[]{:S(2)}) copy-start(bf16[4096,256]{1,0:T(8,128)(2,1)} %constant.62.clone.route_ref) | copy-start | bytes 6291460
  26.9 9.3 %collective-permute-start.8 = (bf16[256,1024]{1,0:T(8,128)(2,1)S(1)}, bf16[256,1024]{1,0:T(8,128)(2,1)S(1)}, u32[]{:S(2)}, u32[]{:S(2)}) collective-permute-start(bf16[256,1024]{1,0:T(8,128)(2,1)S(1)} %get-tuple-element.9), channel_id=1, source_target_pairs={{0,0},{1,1},{2,2},{3,3},{4,4},{5,5},{6,6},{7,7},{8,8},{9,9},{10,10... | collective-permute-start | bytes 1572872 | tf_op jit(solution)/shard_map/ppermute | solution.py:259
  35.4 7.3 %collective-permute-start.9 = (bf16[1024,256]{1,0:T(8,128)(2,1)S(1)}, bf16[1024,256]{1,0:T(8,128)(2,1)S(1)}, u32[]{:S(2)}, u32[]{:S(2)}) collective-permute-start(bf16[1024,256]{1,0:T(8,128)(2,1)S(1)} %forward.1), channel_id=1, source_target_pairs={{0,0},{1,1},{2,2},{3,3},{4,4},{5,5},{6,6},{7,7},{8,8},{9,9},{10,10... | collective-permute-start | bytes 1572872 | tf_op jit(solution)/shard_map/ppermute | solution.py:259
  42.7 25.5 %copy-start.3 = (f32[4,16384]{1,0:T(4,128)S(1)}, f32[4,16384]{1,0:T(4,128)}, u32[]{:S(2)}) copy-start(f32[4,16384]{1,0:T(4,128)} %param.14) | copy-start | bytes 786436
  42.7 25.5 %copy-start.4 = (f32[4,16384]{1,0:T(4,128)S(1)}, f32[4,16384]{1,0:T(4,128)}, u32[]{:S(2)}) copy-start(f32[4,16384]{1,0:T(4,128)} %param.15) | copy-start | bytes 786436
  46.1 37.0 %all-to-all-start = ((bf16[8,256,256]{2,1,0:T(8,128)(2,1)}), bf16[8,256,256]{2,1,0:T(8,128)(2,1)S(1)}, u32[]{:S(2)}, u32[]{:S(2)}) async-start(bf16[8,256,256]{2,1,0:T(8,128)(2,1)} %bitcast.6), calls=%async_computation | async-start | bytes 2097152 | tf_op jit(solution)/shard_map/all_to_all | solution.py:280
  73.3 10.5 %copy-start.5 = (f32[4,16384]{1,0:T(4,128)S(1)}, f32[4,16384]{1,0:T(4,128)}, u32[]{:S(2)}) copy-start(f32[4,16384]{1,0:T(4,128)} %param.16) | copy-start | bytes 786436
  83.8 18.1 %copy-start.6 = (f32[4,16384]{1,0:T(4,128)}, f32[4,16384]{1,0:T(4,128)S(1)}, u32[]{:S(2)}) copy-start(f32[4,16384]{1,0:T(4,128)S(1)} %reshape.64) | copy-start | bytes 786436
  101.1 0.8 copy-start.7

commit v5 on v4

--- a/solution.py
+++ b/solution.py
@@ -44,6 +44,10 @@
     return total
 
 
+def masked(index, count):
+    return jnp.where(lax.broadcasted_iota(jnp.int32, index.shape, 1) < count, index, -1)
+
+
 def pick_kernel(base_ref, index_ref, *refs):
     pieces, (out_ref, turned_ref) = refs[:-2], refs[-2:]
     turned_ref[...] = turned_slots(index_ref[...])
@@ -113,9 +117,9 @@
     return jnp.concatenate(parts, 0)
 
 
-def forward_kernel(vecs, base_ref, index_ref, *refs):
+def forward_kernel(vecs, base_ref, count_ref, index_ref, *refs):
     pieces, (order_ref, tile_ref, out_ref, x_ref, packed_ref) = refs[:-5], refs[-5:]
-    x_ref[...] = gathered(base_ref, turned_slots(index_ref[...]), pieces).T
+    x_ref[...] = gathered(base_ref, turned_slots(masked(index_ref[...], count_ref[0])), pieces).T
     lane = lax.broadcasted_iota(jnp.int32, (GROUP, LANES), 1)
     row = lax.broadcasted_iota(jnp.int32, (GROUP, LANES), 0)
     first = lane < BLOCK
@@ -152,13 +156,13 @@
     out_ref[...] = dot(packed_ref[...], order_ref[...], NT).astype(BF16)
 
 
-def forward(vecs, bases, index, pieces, order, tile):
+def forward(vecs, bases, used, index, pieces, order, tile):
     slots, wide = tile.shape[0], vecs * BLOCK
     whole = pl.BlockSpec(memory_space=pltpu.VMEM)
     return pl.pallas_call(
         functools.partial(forward_kernel, vecs),
         out_shape=jax.ShapeDtypeStruct((slots, wide), BF16),
-        in_specs=[pl.BlockSpec(memory_space=pltpu.SMEM)] + [whole] * (len(pieces) + 3),
+        in_specs=[pl.BlockSpec(memory_space=pltpu.SMEM)] * 2 + [whole] * (len(pieces) + 3),
         out_specs=whole,
         scratch_shapes=[
             pltpu.VMEM((slots, wide), F32),
@@ -166,7 +170,7 @@
         ],
         compiler_params=params(20),
         name="forward",
-    )(bases, index, *pieces, order, tile)
+    )(bases, used, index, *pieces, order, tile)
 
 
 def backward_kernel(vecs, y_ref, route_ref, tile_ref, out_ref, wide_ref):
@@ -218,26 +222,100 @@
     )(far, route, tile)
 
 
-def spread_kernel(col_ref, row_ref, back_ref, forth_ref, out_ref):
+def spread_kernel(count_ref, col_ref, row_ref, back_ref, forth_ref, out_ref):
     count = out_ref.shape[0]
     place = lax.broadcasted_iota(jnp.int32, (count, col_ref.shape[1]), 0) + pl.program_id(0) * count
-    total = dot(as_ones(place == col_ref[...]), back_ref[...])
+    total = dot(as_ones(place == masked(col_ref[...], count_ref[0])), back_ref[...])
     total += dot(as_ones(place == row_ref[...]), forth_ref[...])
     out_ref[...] = total.astype(BF16)
 
 
-def spread(col_index, row_index, back, forth, blocks):
+def spread(used, col_index, row_index, back, forth, blocks):
     whole = pl.BlockSpec(memory_space=pltpu.VMEM)
     step = WIDTH
     return pl.pallas_call(
         spread_kernel,
         grid=(blocks // step,),
         out_shape=jax.ShapeDtypeStruct((blocks, back.shape[1]), BF16),
-        in_specs=[whole] * 4,
+        in_specs=[pl.BlockSpec(memory_space=pltpu.SMEM)] + [whole] * 4,
         out_specs=pl.BlockSpec((step, back.shape[1]), lambda i: (i, 0)),
         compiler_params=params(20),
         name="spread",
-    )(col_index, row_index, back, forth)
+    )(used, col_index, row_index, back, forth)
+
+
+def total_kernel(vecs, part_ref, vector_ref, early_ref, sum_ref, gram_ref):
+    total = part_ref[0].astype(F32)
+    for n in range(1, part_ref.shape[0]):
+        total += part_ref[n].astype(F32)
+    sum_ref[...] = total
+    lines = []
+    for p in range(3 * vecs // 2):
+        pair = vector_ref[:, p * LANES : (p + 1) * LANES]
+        swapped = pltpu.roll(pair, BLOCK, 1)
+        for q in range(vecs // 2):
+            both = total[:, q * LANES : (q + 1) * LANES]
+            lines += [(pair * both).sum(0, keepdims=True), (swapped * both).sum(0, keepdims=True)]
+    lines = jnp.concatenate(lines, 0)
+    shape = lines.shape
+    row = lax.broadcasted_iota(jnp.int32, shape, 0)
+    lane = lax.broadcasted_iota(jnp.int32, shape, 1)
+    swap, q, p = row % 2, row // 2 % (vecs // 2), row // vecs
+    even = (2 * p + swap) * vecs + 2 * q
+    odd = (2 * p + 1 - swap) * vecs + 2 * q + 1
+    late = jnp.where(lane == even, lines[:, :BLOCK].sum(1, keepdims=True), 0.0)
+    late += jnp.where(lane == odd, lines[:, BLOCK:].sum(1, keepdims=True), 0.0)
+    packed = jnp.concatenate([early_ref[...], late.sum(0, keepdims=True)], 0)
+    gram_ref[...] = jnp.broadcast_to(packed[None], gram_ref.shape)
+
+
+def totalled(vecs, parts, vectors, early, peers):
+    whole = pl.BlockSpec(memory_space=pltpu.VMEM)
+    return pl.pallas_call(
+        functools.partial(total_kernel, vecs),
+        out_shape=(
+            jax.ShapeDtypeStruct(parts.shape[1:], F32),
+            jax.ShapeDtypeStruct((peers, early.shape[0] + 1, LANES), F32),
+        ),
+        in_specs=[whole] * 3,
+        out_specs=(whole, whole),
+        compiler_params=params(12),
+        name="totalled",
+    )(parts, vectors, early)
+
+
+def unpack_kernel(vecs, scale, gram_ref, a_ref, b_ref):
+    packed = gram_ref[0]
+    for n in range(1, gram_ref.shape[0]):
+        packed += gram_ref[n]
+    packed = packed * scale
+    wide, half = 5 * vecs, 3 * vecs // 2
+    lane = lax.broadcasted_iota(jnp.int32, (1, LANES), 1)
+
+    def shifted(line, by):
+        by = by % LANES
+        return pltpu.roll(packed[line : line + 1], by, 1) if by else packed[line : line + 1]
+
+    for m in range(3 * vecs):
+        line, at = m // half, m % half * wide
+        b_ref[m : m + 1, :] = shifted(line, -at)[:, : 3 * vecs]
+        first, last = shifted(line, -at - 3 * vecs), shifted(line, -at - 2 * vecs)
+        middle = shifted(2, vecs - m * vecs)
+        mixed = jnp.where(lane < vecs, first, jnp.where(lane < 2 * vecs, middle, last))
+        a_ref[m : m + 1, :] = mixed[:, : 3 * vecs]
+
+
+def unpacked(vecs, gram, scale):
+    whole = pl.BlockSpec(memory_space=pltpu.VMEM)
+    shape = jax.ShapeDtypeStruct((3 * vecs, 3 * vecs), F32)
+    return pl.pallas_call(
+        functools.partial(unpack_kernel, vecs, scale),
+        out_shape=(shape, shape),
+        in_specs=[whole],
+        out_specs=(whole, whole),
+        compiler_params=params(12),
+        name="unpacked",
+    )(gram)
 
 
 def body(x_vec, hx_vec, p_vec, hp_vec, theta, precond, tile_vals, tile_rows, tile_cols, tile_count):
@@ -252,7 +330,8 @@
     residue = (hx_vec - x_vec * theta[:, None]) / precond[None, :]
     live = jnp.arange(slots, dtype=jnp.int32) < tile_count[0, 0]
     row_index = jnp.where(live, tile_rows[0, 0], -1)[None]
-    col_index = jnp.where(live, tile_cols[0, 0], -1)[None]
+    col_index = tile_cols[0, 0][None]
+    used = tile_count.reshape(1)
 
     def along(block, sign):
         path = [(r * cols + c, r * cols + (c + sign * r) % cols) for r in range(rows) for c in range(cols)]
@@ -270,29 +349,25 @@
     flips = jnp.array([0, 1, 0, 0, 0, 1, 1, 1], jnp.int32)
     turns = jnp.array([0, 0, 1, 3, 2, 1, 3, 2], jnp.int32)
     bases = width * ((row_pos // ring ^ flips) * ring + (row_pos % ring - turns) % ring)
-    far_index = along(lax.optimization_barrier((row_index, across))[0], 1)
+    far_index = along(lax.optimization_barrier((row_index, pieces[2]))[0], 1)
     held = stage(lax.optimization_barrier((tile, pieces[2]))[0])
     picked, far_order = pick(bases, far_index, pieces)
     far = along(picked, -1)
-    forth = along(forward(vecs, bases, col_index, pieces, order_matrix(vecs), held), 1)
+    forth = along(forward(vecs, bases, used, col_index, pieces, order_matrix(vecs), held), 1)
     back = backward(vecs, far, route_matrix(vecs), held)
-    parts = spread(col_index, far_order, back, forth, rows * width).reshape(rows, width, vecs * BLOCK)
+    parts = spread(used, col_index, far_order, back, forth, rows * width).reshape(rows, width, vecs * BLOCK)
     parts = lax.all_to_all(parts, "row", 0, 0, tiled=True)
-    total = parts.astype(F32).sum(0)
-    hw_vec = total.reshape(width, vecs, BLOCK).transpose(1, 0, 2).reshape(vecs, piece_len)
-
     vectors = jnp.concatenate([x_vec, residue, p_vec], 0)
     known = jnp.concatenate([vectors, hx_vec, hp_vec], 0)
     early = jnp.dot(vectors, known.T, precision=lax.Precision.HIGHEST, preferred_element_type=F32)
-    late = jnp.dot(vectors, hw_vec.T, precision=lax.Precision.HIGHEST, preferred_element_type=F32)
-    gram = jnp.concatenate([early, late], 1)
-    flat = jnp.pad(gram.reshape(-1), (0, 3 * LANES - gram.size)).reshape(1, 3, LANES)
-    flat = jnp.broadcast_to(flat, (rows * cols, 3, LANES))
-    gram = lax.all_to_all(flat, BOTH, 0, 0, tiled=True).sum(0).reshape(-1)[: gram.size].reshape(gram.shape)
-    gram = gram / ndim_total
-    n = 3 * vecs
-    gram_a = jnp.concatenate([gram[:, n : n + vecs], gram[:, n + 2 * vecs :], gram[:, n + vecs : n + 2 * vecs]], 1)
-    return hw_vec, gram_a, gram[:, :n]
+    early = early.reshape(2, -1)
+    early = jnp.pad(early, ((0, 0), (0, LANES - early.shape[1])))
+    blocked = vectors.reshape(-1, width, BLOCK).transpose(1, 0, 2).reshape(width, -1)
+    total, gram = totalled(vecs, parts, blocked, early, rows * cols)
+    hw_vec = total.reshape(width, vecs, BLOCK).transpose(1, 0, 2).reshape(vecs, piece_len)
+    gram = lax.all_to_all(gram, BOTH, 0, 0, tiled=True)
+    gram_a, gram_b = unpacked(vecs, gram, 1.0 / ndim_total)
+    return hw_vec, gram_a, gram_b
 
 
 def solution(mesh):

time: 102 us -> 99.8 us (0.978)
  blocking collectives: 15.3 us -> 0 us
  waiting for transfers between devices: 10.3 us -> 16 us
  starting transfers between devices: 39.1 us -> 43.4 us
  local copies, waits for them, and re-layouts: 7.11 us -> 11.2 us
  Pallas kernels: 20 us -> 22.2 us
  other arithmetic: 4.37 us -> 2.39 us
  matrix products: 4.09 us -> 2.64 us
    all_to_all x1 -> x0, blocking collectives: 15.3 us -> none  [body(): lax.all_to_all(flat, BOTH, 0, 0, tiled=True).sum(0).reshape(-1)[:gram.size]]
    all_to_all x0 -> x1, waiting for transfers between devices: none -> 9.95 us  [body(): gram = lax.all_to_all(gram, BOTH, 0, 0, tiled=True)]
    all_to_all x1, waiting for transfers between devices: 9.79 us -> 4.9 us  [body(): parts = lax.all_to_all(parts, 'row', 0, 0, tiled=True)]
    all_to_all x0 -> x1, starting transfers between devices: none -> 4.27 us  [body(): gram = lax.all_to_all(gram, BOTH, 0, 0, tiled=True)]
    reshape x1 -> x3, local copies, waits for them, and re-layouts: 0.09 us -> 2.18 us  [the longest x2 2.1 us: body(): vectors.reshape(-1, width, BLOCK).transpose(1, 0, 2).reshape(width, -1)]
    pallas_call x0 -> x2, Pallas kernels: none -> 2.09 us  [the longest x1 1.24 us: totalled(): pl.pallas_call(functools.partial(total_kernel, vecs), out_shape=(jax.Shap...]
    dot_general x1 -> x0, matrix products: 1.47 us -> none  [body(): jnp.dot(vectors, hw_vec.T, precision=lax.Precision.HIGHEST, preferred_ele...]
    unnamed x16 -> x20, local copies, waits for them, and re-layouts: 3.42 us -> 3.42 us
  transfers between devices with their start and end apart: 11 -> 12, of which waited for: 2 -> 3; matrix products, arithmetic and copies ran while one was open for 7% -> 11% of each run, Pallas kernels for 15% -> 15%
where the time goes in v5:
time: 99.8 us; the launch traced here: 99.4 us
  starting transfers between devices  43.4 us (43%)
  Pallas kernels  22.2 us (22%)
  waiting for transfers between devices  16 us (16%)
  local copies, waits for them, and re-layouts  11.2 us (11%)
  matrix products  2.64 us (3%)
  other arithmetic  2.39 us (2%)
  between operations  1.59 us (2%)
    all_to_all x1, starting transfers between devices, body(): parts = lax.all_to_all(parts, 'row', 0, 0, tiled=True)  21.9 us
    ppermute x7, starting transfers between devices, within(): lax.ppermute(block, 'row', [(i, (i // ring ^ flip) * ring + (i % ring + t...  15.2 us
    all_to_all x1, waiting for transfers between devices, body(): gram = lax.all_to_all(gram, BOTH, 0, 0, tiled=True)  9.95 us
    pallas_call x1, Pallas kernels, forward(): pl.pallas_call(functools.partial(forward_kernel, vecs), out_shape=jax.Sha...  7.73 us
    pallas_call x1, Pallas kernels, backward(): pl.pallas_call(functools.partial(backward_kernel, vecs), out_shape=jax.Sh...  6.64 us
    all_to_all x1, waiting for transfers between devices, body(): parts = lax.all_to_all(parts, 'row', 0, 0, tiled=True)  4.9 us
    all_to_all x1, starting transfers between devices, body(): gram = lax.all_to_all(gram, BOTH, 0, 0, tiled=True)  4.27 us
    concatenate x1, local copies, waits for them, and re-layouts, body(): known = jnp.concatenate([vectors, hx_vec, hp_vec], 0)  3.47 us
  transfers between devices with their start and end apart: 12, of which 3 were waited for; matrix products, arithmetic and copies ran while one was open for 11% of the time, Pallas kernels for 15%

profile of v5, /device:TPU:1, one launch (start us, length us, event | category | flops | bytes accessed | tf_op | source)
XLA Modules:
  0.0 99.4 jit_solution(16091422266863827206)
XLA Ops:
  0.7 1.2 %fusion.4 = (bf16[4,16384]{1,0:T(4,128)(2,1)S(1)}, f32[4,16384]{1,0:T(4,128)S(1)}) fusion(f32[16384]{0:T(1024)} %param.19, f32[4,16384]{1,0:T(4,128)} %param.15, f32[4,16384]{1,0:T(4,128)} %param.14, f32[4]{0:T(128)} %param.18), kind=kLoop, calls=%fused_computation.10 | loop fusion | flops 262144 | bytes 983056 | tf_op jit(solution)/shard_map/convert_element_type | solution.py:345
  1.9 0.3 reshape.53
  2.3 2.5 %collective-permute-start = (bf16[256,256]{1,0:T(8,128)(2,1)S(1)}, bf16[256,256]{1,0:T(8,128)(2,1)S(1)}, u32[]{:S(2)}, u32[]{:S(2)}) collective-permute-start(bf16[256,256]{1,0:T(8,128)(2,1)S(1)} %bitcast.19), channel_id=1, source_target_pairs={{0,16},{16,32},{32,48},{48,0},{64,80},{80,96},{96,112},{112,64},{1... | collective-permute-start | bytes 393224 | tf_op jit(solution)/shard_map/ppermute | solution.py:341
  4.9 1.2 %collective-permute-start.2 = (bf16[256,256]{1,0:T(8,128)(2,1)S(1)}, bf16[256,256]{1,0:T(8,128)(2,1)S(1)}, u32[]{:S(2)}, u32[]{:S(2)}) collective-permute-start(bf16[256,256]{1,0:T(8,128)(2,1)S(1)} %bitcast.20), channel_id=1, source_target_pairs={{0,64},{16,80},{32,96},{48,112},{64,0},{80,16},{96,32},{112,48},{1... | collective-permute-start | bytes 393224 | tf_op jit(solution)/shard_map/ppermute | solution.py:341
  6.1 2.2 %collective-permute-start.3 = (bf16[256,256]{1,0:T(8,128)(2,1)S(1)}, bf16[256,256]{1,0:T(8,128)(2,1)S(1)}, u32[]{:S(2)}, u32[]{:S(2)}) collective-permute-start(bf16[256,256]{1,0:T(8,128)(2,1)S(1)} %bitcast.21), channel_id=1, source_target_pairs={{0,48},{16,0},{32,16},{48,32},{64,112},{80,64},{96,80},{112,96},{1... | collective-permute-start | bytes 393224 | tf_op jit(solution)/shard_map/ppermute | solution.py:341
  8.3 1.2 %collective-permute-start.4 = (bf16[256,256]{1,0:T(8,128)(2,1)S(1)}, bf16[256,256]{1,0:T(8,128)(2,1)S(1)}, u32[]{:S(2)}, u32[]{:S(2)}) collective-permute-start(bf16[256,256]{1,0:T(8,128)(2,1)S(1)} %bitcast.22), channel_id=1, source_target_pairs={{0,32},{16,48},{32,0},{48,16},{64,96},{80,112},{96,64},{112,80},{1... | collective-permute-start | bytes 393224 | tf_op jit(solution)/shard_map/ppermute | solution.py:341
  10.2 0.7 collective-permute-start.1
  10.9 5.0 %collective-permute-start.5 = (bf16[256,256]{1,0:T(8,128)(2,1)S(1)}, bf16[256,256]{1,0:T(8,128)(2,1)S(1)}, u32[]{:S(2)}, u32[]{:S(2)}) collective-permute-start(bf16[256,256]{1,0:T(8,128)(2,1)S(1)} %collective-permute-done.2.refs_1_), channel_id=1, source_target_pairs={{0,16},{16,32},{32,48},{48,0},{64,80},{80,96},{96,112},{112,64},{1... | collective-permute-start | bytes 393224 | tf_op jit(solution)/shard_map/ppermute | solution.py:341
  15.9 1.8 %collective-permute-start.6 = (bf16[256,256]{1,0:T(8,128)(2,1)S(1)}, bf16[256,256]{1,0:T(8,128)(2,1)S(1)}, u32[]{:S(2)}, u32[]{:S(2)}) collective-permute-start(bf16[256,256]{1,0:T(8,128)(2,1)S(1)} %collective-permute-done.2.refs_1_), channel_id=1, source_target_pairs={{0,48},{16,0},{32,16},{48,32},{64,112},{80,64},{96,80},{112,96},{1... | collective-permute-start | bytes 393224 | tf_op jit(solution)/shard_map/ppermute | solution.py:341
  17.8 1.1 %collective-permute-start.7 = (bf16[256,256]{1,0:T(8,128)(2,1)S(1)}, bf16[256,256]{1,0:T(8,128)(2,1)S(1)}, u32[]{:S(2)}, u32[]{:S(2)}) collective-permute-start(bf16[256,256]{1,0:T(8,128)(2,1)S(1)} %collective-permute-done.2.refs_1_), channel_id=1, source_target_pairs={{0,32},{16,48},{32,0},{48,16},{64,96},{80,112},{96,64},{112,80},{1... | collective-permute-start | bytes 393224 | tf_op jit(solution)/shard_map/ppermute | solution.py:341
  18.9 3.4 %copy-done = bf16[1,1,1024,4096]{3,2,1,0:T(8,128)(2,1)S(1)} copy-done((bf16[1,1,1024,4096]{3,2,1,0:T(8,128)(2,1)S(1)}, bf16[1,1,1024,4096]{3,2,1,0:T(8,128)(2,1)}, u32[]{:S(2)}) %copy-start) | copy-done | bytes 8388632
  22.3 0.6 stage.1.tile_ref.refs_9_
  22.9 1.1 %collective-permute-done.7.refs_7_ = bf16[256,256]{1,0:T(8,128)(2,1)S(1)} collective-permute-done((bf16[256,256]{1,0:T(8,128)(2,1)S(1)}, bf16[256,256]{1,0:T(8,128)(2,1)S(1)}, u32[]{:S(2)}, u32[]{:S(2)}) %collective-permute-start.7) | collective-permute-done | bytes 131104 | tf_op jit(solution)/shard_map/ppermute | solution.py:341
  24.0 1.8 %pick.1 = (bf16[256,1024]{1,0:T(8,128)(2,1)S(1)}, s32[1,1024]{1,0:T(1,128)S(1)}) custom-call(s32[8]{0:T(128)S(1)} %fusion.2.base_ref, s32[1,1024]{1,0:T(1,128)S(1)} %collective-permute-done.1.index_ref, bf16[256,256]{1,0:T(8,128)(2,1)S(1)} %bitcast.23, bf16[256,256]{1,0:T(8,128)(2,1)S(1)} %collective-permute-done.2.refs_1_, ...), custom_call_target="tpu_custom_call" | custom-call | tf_op jit(solution)/shard_map/pick/pallas_call | solution.py:59
  25.9 0.7 collective-permute-start.8
  26.6 7.7 %forward.1 = bf16[1024,256]{1,0:T(8,128)(2,1)S(1)} custom-call(s32[8]{0:T(128)S(1)} %fusion.2.base_ref, s32[1]{0:T(128)} %bitcast.15.count_ref, s32[1,1024]{1,0:T(1,128)S(1)} %bitcast.25, bf16[256,256]{1,0:T(8,128)(2,1)S(1)} %bitcast.24, bf16[256,256]{1,0:T(8,128)(2,1)S(1)} %collective-permute-done.2.refs_1_, ...), custom_call_target="tpu_custom_call" | custom-call | tf_op jit(solution)/shard_map/forward/pallas_call | solution.py:162
  34.3 0.7 collective-permute-start.9
  35.1 6.6 %backward.1.back_ref = bf16[1024,256]{1,0:T(8,128)(2,1)S(1)} custom-call(bf16[256,1024]{1,0:T(8,128)(2,1)S(1)} %collective-permute-done.8.y_ref, bf16[4096,256]{1,0:T(8,128)(2,1)S(1)} %copy-done.1, bf16[1024,4096]{1,0:T(8,128)(2,1)S(1)} %stage.1.tile_ref.refs_9_), custom_call_target="tpu_custom_call" | custom-call | tf_op jit(solution)/shard_map/backward/pallas_call | solution.py:212
  41.7 3.3 %spread.1 = bf16[2048,256]{1,0:T(8,128)(2,1)} custom-call(s32[1]{0:T(128)} %bitcast.16.count_ref, s32[1,1024]{1,0:T(1,128)S(1)} %bitcast.26, s32[1,1024]{1,0:T(1,128)S(1)} %get-tuple-element.12.row_ref, bf16[1024,256]{1,0:T(8,128)(2,1)S(1)} %backward.1.back_ref, bf16[1024,256]{1,0:T(8,128)(2,1)S(1)} %collective-permute-done.9.forth_ref), custom_call_target="tpu_custom_call" | custom-call | tf_op jit(solution)/shard_map/spread/pallas_call | solution.py:236
  45.1 21.9 %all-to-all-start = ((bf16[8,256,256]{2,1,0:T(8,128)(2,1)}), bf16[8,256,256]{2,1,0:T(8,128)(2,1)S(1)}, u32[]{:S(2)}, u32[]{:S(2)}) async-start(bf16[8,256,256]{2,1,0:T(8,128)(2,1)} %bitcast.7), calls=%async_computation | async-start | bytes 2097152 | tf_op jit(solution)/shard_map/all_to_all | solution.py:359
  67.0 1.1 %pad_maximum_fusion = f32[12,16384]{1,0:T(8,128)} fusion(f32[4,16384]{1,0:T(4,128)S(1)} %copy-done.6, f32[4,16384]{1,0:T(4,128)S(1)} %get-tuple-element.20, f32[4,16384]{1,0:T(4,128)S(1)} %copy-done.4), kind=kLoop, calls=%fused_computation | loop fusion | flops 393216 | bytes 1572864 | tf_op jit(solution)/shard_map/concatenate | solution.py:360
  68.1 1.8 %reshape.56 = f32[12,256,64]{2,1,0:T(8,128)S(1)} reshape(f32[12,16384]{1,0:T(8,128)} %pad_maximum_fusion) | data formatting | bytes 1572864 | tf_op jit(solution)/shard_map/reshape | solution.py:365
  70.0 0.4 copy.21
  70.4 0.3 copy.22.vector_ref
  70.7 3.5 %concatenate.8 = f32[20,16384]{1,0:T(8,128)S(1)} concatenate(f32[4,16384]{1,0:T(4,128)} %param.14, f32[4,16384]{1,0:T(4,128)} %copy-done.5, f32[4,16384]{1,0:T(4,128)} %param.16, f32[4,16384]{1,0:T(4,128)} %param.15, f32[4,16384]{1,0:T(4,128)} %param.17), dimensions={0} | concatenate | bytes 2621440 | tf_op jit(solution)/shard_map/concatenate | solution.py:361
  74.2 2.6 %fusion.3 = f32[12,20]{1,0:T(8,128)S(1)} fusion(f32[20,16384]{1,0:T(8,128)S(1)} %concatenate.8, f32[4,16384]{1,0:T(4,128)} %param.16, f32[4,16384]{1,0:T(4,128)} %copy-done.5, f32[4,16384]{1,0:T(4,128)} %param.14), kind=kOutput, calls=%fused_computation.9 | convolution fusion | flops 47579136 | bytes 2098112 | tf_op jit(solution)/shard_map/dot_general | solution.py:362
  76.9 4.9 %all-to-all-done.part_ref = bf16[8,256,256]{2,1,0:T(8,128)(2,1)S(1)} async-done(((bf16[8,256,256]{2,1,0:T(8,128)(2,1)}), bf16[8,256,256]{2,1,0:T(8,128)(2,1)S(1)}, u32[]{:S(2)}, u32[]{:S(2)}) %all-to-all-start) | async-done | bytes 1048608 | tf_op jit(solution)/shard_map/all_to_all | solution.py:359
  81.8 1.2 %totalled.1 = (f32[256,256]{1,0:T(8,128)S(1)}, f32[128,3,128]{2,1,0:T(4,128)}) custom-call(bf16[8,256,256]{2,1,0:T(8,128)(2,1)S(1)} %all-to-all-done.part_ref, f32[256,768]{1,0:T(8,128)S(1)} %copy.22.vector_ref, f32[2,128]{1,0:T(2,128)S(1)} %pad.4.early_ref), custom_call_target="tpu_custom_call" | custom-call | tf_op jit(solution)/shard_map/totalled/pallas_call | solution.py:274
  83.0 4.3 %all-to-all-start.1 = ((f32[128,3,128]{2,1,0:T(4,128)}), f32[128,3,128]{2,1,0:T(4,128)S(1)}, u32[]{:S(2)}, u32[]{:S(2)}) async-start(f32[128,3,128]{2,1,0:T(4,128)} %get-tuple-element.16), calls=%async_computation.1 | async-start | bytes 524288 | tf_op jit(solution)/shard_map/all_to_all | solution.py:368
  87.7 0.9 reshape.60
  88.6 9.9 %all-to-all-done.1.gram_ref = f32[128,3,128]{2,1,0:T(4,128)S(1)} async-done(((f32[128,3,128]{2,1,0:T(4,128)}), f32[128,3,128]{2,1,0:T(4,128)S(1)}, u32[]{:S(2)}, u32[]{:S(2)}) %all-to-all-start.1) | async-done | bytes 196640 | tf_op jit(solution)/shard_map/all_to_all | solution.py:368
  98.5 0.8 unpacked.1
  (35 shorter events, 0.7 us)
Async XLA Ops:
  0.6 18.2 %copy-start.8 = (s32[8]{0:T(128)S(1)}, s32[8]{0:T(128)}, u32[]{:S(2)}) copy-start(s32[8]{0:T(128)} %constant.65) | copy-start | bytes 100
  0.6 18.2 %copy-start.9 = (s32[8]{0:T(128)S(1)}, s32[8]{0:T(128)}, u32[]{:S(2)}) copy-start(s32[8]{0:T(128)} %constant.55.clone) | copy-start | bytes 100
  0.7 9.5 %copy-start.7 = (s32[1,1,1024]{2,1,0:T(1,128)S(1)}, s32[1,1,1024]{2,1,0:T(1,128)}, u32[]{:S(2)}) copy-start(s32[1,1,1024]{2,1,0:T(1,128)} %param.21) | copy-start | bytes 12292
  1.9 65.1 %copy-start.5 = (f32[4,16384]{1,0:T(4,128)}, f32[4,16384]{1,0:T(4,128)S(1)}, u32[]{:S(2)}) copy-start(f32[4,16384]{1,0:T(4,128)S(1)} %get-tuple-element.20) | copy-start | bytes 786436
  2.3 7.9 %collective-permute-start = (bf16[256,256]{1,0:T(8,128)(2,1)S(1)}, bf16[256,256]{1,0:T(8,128)(2,1)S(1)}, u32[]{:S(2)}, u32[]{:S(2)}) collective-permute-start(bf16[256,256]{1,0:T(8,128)(2,1)S(1)} %bitcast.19), channel_id=1, source_target_pairs={{0,16},{16,32},{32,48},{48,0},{64,80},{80,96},{96,112},{112,64},{1... | collective-permute-start | bytes 393224 | tf_op jit(solution)/shard_map/ppermute | solution.py:341
  4.9 6.0 %collective-permute-start.2 = (bf16[256,256]{1,0:T(8,128)(2,1)S(1)}, bf16[256,256]{1,0:T(8,128)(2,1)S(1)}, u32[]{:S(2)}, u32[]{:S(2)}) collective-permute-start(bf16[256,256]{1,0:T(8,128)(2,1)S(1)} %bitcast.20), channel_id=1, source_target_pairs={{0,64},{16,80},{32,96},{48,112},{64,0},{80,16},{96,32},{112,48},{1... | collective-permute-start | bytes 393224 | tf_op jit(solution)/shard_map/ppermute | solution.py:341
  6.1 11.7 %collective-permute-start.3 = (bf16[256,256]{1,0:T(8,128)(2,1)S(1)}, bf16[256,256]{1,0:T(8,128)(2,1)S(1)}, u32[]{:S(2)}, u32[]{:S(2)}) collective-permute-start(bf16[256,256]{1,0:T(8,128)(2,1)S(1)} %bitcast.21), channel_id=1, source_target_pairs={{0,48},{16,0},{32,16},{48,32},{64,112},{80,64},{96,80},{112,96},{1... | collective-permute-start | bytes 393224 | tf_op jit(solution)/shard_map/ppermute | solution.py:341
  8.3 14.6 %collective-permute-start.4 = (bf16[256,256]{1,0:T(8,128)(2,1)S(1)}, bf16[256,256]{1,0:T(8,128)(2,1)S(1)}, u32[]{:S(2)}, u32[]{:S(2)}) collective-permute-start(bf16[256,256]{1,0:T(8,128)(2,1)S(1)} %bitcast.22), channel_id=1, source_target_pairs={{0,32},{16,48},{32,0},{48,16},{64,96},{80,112},{96,64},{112,80},{1... | collective-permute-start | bytes 393224 | tf_op jit(solution)/shard_map/ppermute | solution.py:341
  10.2 12.7 %collective-permute-start.1 = (s32[1,1024]{1,0:T(1,128)S(1)}, s32[1,1024]{1,0:T(1,128)S(1)}, u32[]{:S(2)}, u32[]{:S(2)}) collective-permute-start(s32[1,1024]{1,0:T(1,128)S(1)} %compare_select_fusion), channel_id=1, source_target_pairs={{0,0},{1,1},{2,2},{3,3},{4,4},{5,5},{6,6},{7,7},{8,8},{9,9},{10,10... | collective-permute-start | bytes 12296 | tf_op jit(solution)/shard_map/ppermute | solution.py:338
  10.9 12.0 %collective-permute-start.5 = (bf16[256,256]{1,0:T(8,128)(2,1)S(1)}, bf16[256,256]{1,0:T(8,128)(2,1)S(1)}, u32[]{:S(2)}, u32[]{:S(2)}) collective-permute-start(bf16[256,256]{1,0:T(8,128)(2,1)S(1)} %collective-permute-done.2.refs_1_), channel_id=1, source_target_pairs={{0,16},{16,32},{32,48},{48,0},{64,80},{80,96},{96,112},{112,64},{1... | collective-permute-start | bytes 393224 | tf_op jit(solution)/shard_map/ppermute | solution.py:341
  15.9 7.0 %collective-permute-start.6 = (bf16[256,256]{1,0:T(8,128)(2,1)S(1)}, bf16[256,256]{1,0:T(8,128)(2,1)S(1)}, u32[]{:S(2)}, u32[]{:S(2)}) collective-permute-start(bf16[256,256]{1,0:T(8,128)(2,1)S(1)} %collective-permute-done.2.refs_1_), channel_id=1, source_target_pairs={{0,48},{16,0},{32,16},{48,32},{64,112},{80,64},{96,80},{112,96},{1... | collective-permute-start | bytes 393224 | tf_op jit(solution)/shard_map/ppermute | solution.py:341
  17.8 6.3 %collective-permute-start.7 = (bf16[256,256]{1,0:T(8,128)(2,1)S(1)}, bf16[256,256]{1,0:T(8,128)(2,1)S(1)}, u32[]{:S(2)}, u32[]{:S(2)}) collective-permute-start(bf16[256,256]{1,0:T(8,128)(2,1)S(1)} %collective-permute-done.2.refs_1_), channel_id=1, source_target_pairs={{0,32},{16,48},{32,0},{48,16},{64,96},{80,112},{96,64},{112,80},{1... | collective-permute-start | bytes 393224 | tf_op jit(solution)/shard_map/ppermute | solution.py:341
  18.9 3.4 %copy-start = (bf16[1,1,1024,4096]{3,2,1,0:T(8,128)(2,1)S(1)}, bf16[1,1,1024,4096]{3,2,1,0:T(8,128)(2,1)}, u32[]{:S(2)}) copy-start(bf16[1,1,1024,4096]{3,2,1,0:T(8,128)(2,1)} %param.20) | copy-start | bytes 25165828
  22.3 4.3 %copy-start.2 = (bf16[256,256]{1,0:T(8,128)(2,1)S(1)}, bf16[256,256]{1,0:T(8,128)(2,1)}, u32[]{:S(2)}) copy-start(bf16[256,256]{1,0:T(8,128)(2,1)} %constant.57.clone.refs_8_) | copy-start | bytes 393220
  22.3 4.3 %copy-start.3 = (s32[1,1,1024]{2,1,0:T(1,128)S(1)}, s32[1,1,1024]{2,1,0:T(1,128)}, u32[]{:S(2)}) copy-start(s32[1,1,1024]{2,1,0:T(1,128)} %param.22) | copy-start | bytes 12292
  25.9 9.2 %collective-permute-start.8 = (bf16[256,1024]{1,0:T(8,128)(2,1)S(1)}, bf16[256,1024]{1,0:T(8,128)(2,1)S(1)}, u32[]{:S(2)}, u32[]{:S(2)}) collective-permute-start(bf16[256,1024]{1,0:T(8,128)(2,1)S(1)} %get-tuple-element.13), channel_id=1, source_target_pairs={{0,0},{1,1},{2,2},{3,3},{4,4},{5,5},{6,6},{7,7},{8,8},{9,9},{10,10... | collective-permute-start | bytes 1572872 | tf_op jit(solution)/shard_map/ppermute | solution.py:338
  26.6 8.5 %copy-start.1 = (bf16[4096,256]{1,0:T(8,128)(2,1)S(1)}, bf16[4096,256]{1,0:T(8,128)(2,1)}, u32[]{:S(2)}) copy-start(bf16[4096,256]{1,0:T(8,128)(2,1)} %constant.58.clone.route_ref) | copy-start | bytes 6291460
  34.3 7.4 %collective-permute-start.9 = (bf16[1024,256]{1,0:T(8,128)(2,1)S(1)}, bf16[1024,256]{1,0:T(8,128)(2,1)S(1)}, u32[]{:S(2)}, u32[]{:S(2)}) collective-permute-start(bf16[1024,256]{1,0:T(8,128)(2,1)S(1)} %forward.1), channel_id=1, source_target_pairs={{0,0},{1,1},{2,2},{3,3},{4,4},{5,5},{6,6},{7,7},{8,8},{9,9},{10,10... | collective-permute-start | bytes 1572872 | tf_op jit(solution)/shard_map/ppermute | solution.py:338
  45.1 21.9 %copy-start.4 = (f32[4,16384]{1,0:T(4,128)S(1)}, f32[4,16384]{1,0:T(4,128)}, u32[]{:S(2)}) copy-start(f32[4,16384]{1,0:T(4,128)} %param.14) | copy-start | bytes 786436
  45.1 21.9 %copy-start.6 = (f32[4,16384]{1,0:T(4,128)S(1)}, f32[4,16384]{1,0:T(4,128)}, u32[]{:S(2)}) copy-start(f32[4,16384]{1,0:T(4,128)} %param.16) | copy-start | bytes 786436
  45.1 36.7 %all-to-all-start = ((bf16[8,256,256]{2,1,0:T(8,128)(2,1)}), bf16[8,256,256]{2,1,0:T(8,128)(2,1)S(1)}, u32[]{:S(2)}, u32[]{:S(2)}) async-start(bf16[8,256,256]{2,1,0:T(8,128)(2,1)} %bitcast.7), calls=%async_computation | async-start | bytes 2097152 | tf_op jit(solution)/shard_map/all_to_all | solution.py:359
  83.0 15.5 %all-to-all-start.1 = ((f32[128,3,128]{2,1,0:T(4,128)}), f32[128,3,128]{2,1,0:T(4,128)S(1)}, u32[]{:S(2)}, u32[]{:S(2)}) async-start(f32[128,3,128]{2,1,0:T(4,128)} %get-tuple-element.16), calls=%async_computation.1 | async-start | bytes 524288 | tf_op jit(solution)/shard_map/all_to_all | solution.py:368

commit v6 on v5

--- a/solution.py
+++ b/solution.py
@@ -48,25 +48,53 @@
     return jnp.where(lax.broadcasted_iota(jnp.int32, index.shape, 1) < count, index, -1)
 
 
-def pick_kernel(base_ref, index_ref, *refs):
-    pieces, (out_ref, turned_ref) = refs[:-2], refs[-2:]
-    turned_ref[...] = turned_slots(index_ref[...])
-    out_ref[...] = gathered(base_ref, index_ref[...], pieces).astype(BF16)
-
-
-def pick(bases, index, pieces):
+def early_kernel(base_ref, count_ref, far_ref, own_ref, *refs):
+    pieces, (tile_ref, picked_ref, x_ref, far_order_ref, held_ref, sem) = refs[:-6], refs[-6:]
+    copy = pltpu.make_async_copy(tile_ref, held_ref, sem)
+    copy.start()
+    far_order_ref[...] = turned_slots(far_ref[...])
+    picked_ref[...] = gathered(base_ref, far_ref[...], pieces).astype(BF16)
+    own_order = turned_slots(masked(own_ref[...], count_ref[0]))
+    x_ref[...] = gathered(base_ref, own_order, pieces).astype(BF16)
+    copy.wait()
+
+
+def early_pick(bases, used, far_index, own_index, pieces, tile):
+    whole = pl.BlockSpec(memory_space=pltpu.VMEM)
+    shape = jax.ShapeDtypeStruct((pieces[0].shape[0], far_index.shape[1]), BF16)
+    return pl.pallas_call(
+        early_kernel,
+        out_shape=(
+            shape,
+            shape,
+            jax.ShapeDtypeStruct(far_index.shape, far_index.dtype),
+            jax.ShapeDtypeStruct(tile.shape, tile.dtype),
+        ),
+        in_specs=[pl.BlockSpec(memory_space=pltpu.SMEM)] * 2
+        + [whole] * (2 + len(pieces))
+        + [pl.BlockSpec(memory_space=pl.ANY)],
+        out_specs=(whole,) * 4,
+        scratch_shapes=[pltpu.SemaphoreType.DMA],
+        compiler_params=params(42),
+        name="early_pick",
+    )(bases, used, far_index, own_index, *pieces, tile)
+
+
+def pick_kernel(base_ref, index_ref, before_ref, *refs):
+    total = gathered(base_ref, index_ref[...], refs[:-1])
+    refs[-1][...] = (before_ref[...].astype(F32) + total).astype(BF16)
+
+
+def pick(bases, index, before, pieces):
     whole = pl.BlockSpec(memory_space=pltpu.VMEM)
     return pl.pallas_call(
         pick_kernel,
-        out_shape=(
-            jax.ShapeDtypeStruct((pieces[0].shape[0], index.shape[1]), BF16),
-            jax.ShapeDtypeStruct(index.shape, index.dtype),
-        ),
-        in_specs=[pl.BlockSpec(memory_space=pltpu.SMEM)] + [whole] * (1 + len(pieces)),
-        out_specs=(whole, whole),
+        out_shape=jax.ShapeDtypeStruct(before.shape, BF16),
+        in_specs=[pl.BlockSpec(memory_space=pltpu.SMEM)] + [whole] * (2 + len(pieces)),
+        out_specs=whole,
         compiler_params=params(16),
         name="pick",
-    )(bases, index, *pieces)
+    )(bases, index, before, *pieces)
 
 
 def order_matrix(vecs):
@@ -94,32 +122,15 @@
     return jnp.concatenate(parts, 1)
 
 
-def stage_kernel(tile_ref, out_ref, sem):
-    copy = pltpu.make_async_copy(tile_ref, out_ref, sem)
-    copy.start()
-    copy.wait()
-
-
-def stage(tile):
-    return pl.pallas_call(
-        stage_kernel,
-        out_shape=jax.ShapeDtypeStruct(tile.shape, tile.dtype),
-        in_specs=[pl.BlockSpec(memory_space=pl.ANY)],
-        out_specs=pl.BlockSpec(memory_space=pltpu.VMEM),
-        scratch_shapes=[pltpu.SemaphoreType.DMA],
-        compiler_params=params(12),
-        name="stage",
-    )(tile)
-
-
 def stacked(tile_ref, at, half):
     parts = [tile_ref[at, c * LANES : (c + 1) * LANES] for c in range(half * HALF, (half + 1) * HALF)]
     return jnp.concatenate(parts, 0)
 
 
-def forward_kernel(vecs, base_ref, count_ref, index_ref, *refs):
+def forward_kernel(vecs, base_ref, count_ref, index_ref, before_ref, *refs):
     pieces, (order_ref, tile_ref, out_ref, x_ref, packed_ref) = refs[:-5], refs[-5:]
-    x_ref[...] = gathered(base_ref, turned_slots(masked(index_ref[...], count_ref[0])), pieces).T
+    own_order = turned_slots(masked(index_ref[...], count_ref[0]))
+    x_ref[...] = (before_ref[...].astype(F32) + gathered(base_ref, own_order, pieces)).T
     lane = lax.broadcasted_iota(jnp.int32, (GROUP, LANES), 1)
     row = lax.broadcasted_iota(jnp.int32, (GROUP, LANES), 0)
     first = lane < BLOCK
@@ -156,13 +167,13 @@
     out_ref[...] = dot(packed_ref[...], order_ref[...], NT).astype(BF16)
 
 
-def forward(vecs, bases, used, index, pieces, order, tile):
+def forward(vecs, bases, used, index, before, pieces, order, tile):
     slots, wide = tile.shape[0], vecs * BLOCK
     whole = pl.BlockSpec(memory_space=pltpu.VMEM)
     return pl.pallas_call(
         functools.partial(forward_kernel, vecs),
         out_shape=jax.ShapeDtypeStruct((slots, wide), BF16),
-        in_specs=[pl.BlockSpec(memory_space=pltpu.SMEM)] * 2 + [whole] * (len(pieces) + 3),
+        in_specs=[pl.BlockSpec(memory_space=pltpu.SMEM)] * 2 + [whole] * (len(pieces) + 4),
         out_specs=whole,
         scratch_shapes=[
             pltpu.VMEM((slots, wide), F32),
@@ -170,7 +181,7 @@
         ],
         compiler_params=params(20),
         name="forward",
-    )(bases, used, index, *pieces, order, tile)
+    )(bases, used, index, before, *pieces, order, tile)
 
 
 def backward_kernel(vecs, y_ref, route_ref, tile_ref, out_ref, wide_ref):
@@ -222,26 +233,28 @@
     )(far, route, tile)
 
 
-def spread_kernel(count_ref, col_ref, row_ref, back_ref, forth_ref, out_ref):
+def spread_kernel(count_ref, index_ref, part_ref, *refs):
+    before, out_ref = refs[:-1], refs[-1]
     count = out_ref.shape[0]
-    place = lax.broadcasted_iota(jnp.int32, (count, col_ref.shape[1]), 0) + pl.program_id(0) * count
-    total = dot(as_ones(place == masked(col_ref[...], count_ref[0])), back_ref[...])
-    total += dot(as_ones(place == row_ref[...]), forth_ref[...])
-    out_ref[...] = total.astype(BF16)
-
-
-def spread(used, col_index, row_index, back, forth, blocks):
-    whole = pl.BlockSpec(memory_space=pltpu.VMEM)
-    step = WIDTH
+    base = pl.program_id(0) * count
+    place = lax.broadcasted_iota(jnp.int32, (count, index_ref.shape[1]), 0) + base
+    total = dot(as_ones(place == masked(index_ref[...], count_ref[0])), part_ref[...])
+    for more in before:
+        total += more[pl.ds(pl.multiple_of(base, count), count), :]
+    out_ref[...] = total.astype(out_ref.dtype)
+
+
+def spread(used, index, part, blocks, dtype, *before):
+    whole = pl.BlockSpec(memory_space=pltpu.VMEM)
     return pl.pallas_call(
         spread_kernel,
-        grid=(blocks // step,),
-        out_shape=jax.ShapeDtypeStruct((blocks, back.shape[1]), BF16),
-        in_specs=[pl.BlockSpec(memory_space=pltpu.SMEM)] + [whole] * 4,
-        out_specs=pl.BlockSpec((step, back.shape[1]), lambda i: (i, 0)),
+        grid=(blocks // WIDTH,),
+        out_shape=jax.ShapeDtypeStruct((blocks, part.shape[1]), dtype),
+        in_specs=[pl.BlockSpec(memory_space=pltpu.SMEM)] + [whole] * (2 + len(before)),
+        out_specs=pl.BlockSpec((WIDTH, part.shape[1]), lambda i: (i, 0)),
         compiler_params=params(20),
         name="spread",
-    )(used, col_index, row_index, back, forth)
+    )(used, index, part, *before)
 
 
 def total_kernel(vecs, part_ref, vector_ref, early_ref, sum_ref, gram_ref):
@@ -350,12 +363,17 @@
     turns = jnp.array([0, 0, 1, 3, 2, 1, 3, 2], jnp.int32)
     bases = width * ((row_pos // ring ^ flips) * ring + (row_pos % ring - turns) % ring)
     far_index = along(lax.optimization_barrier((row_index, pieces[2]))[0], 1)
-    held = stage(lax.optimization_barrier((tile, pieces[2]))[0])
-    picked, far_order = pick(bases, far_index, pieces)
-    far = along(picked, -1)
-    forth = along(forward(vecs, bases, used, col_index, pieces, order_matrix(vecs), held), 1)
+    near = 5
+    picked, x_slots, far_order, held = early_pick(
+        bases[:near], used, far_index, col_index, pieces[:near], tile
+    )
+    far = along(pick(bases[near:], far_index, picked, pieces[near:]), -1)
+    forth = forward(vecs, bases[near:], used, col_index, x_slots, pieces[near:], order_matrix(vecs), held)
+    forth = along(forth, 1)
     back = backward(vecs, far, route_matrix(vecs), held)
-    parts = spread(used, col_index, far_order, back, forth, rows * width).reshape(rows, width, vecs * BLOCK)
+    back = spread(used, col_index, back, rows * width, F32)
+    every = jnp.full((1,), slots, jnp.int32)
+    parts = spread(every, far_order, forth, rows * width, BF16, back).reshape(rows, width, vecs * BLOCK)
     parts = lax.all_to_all(parts, "row", 0, 0, tiled=True)
     vectors = jnp.concatenate([x_vec, residue, p_vec], 0)
     known = jnp.concatenate([vectors, hx_vec, hp_vec], 0)

time: 99.8 us -> 97.7 us (0.979)
  Pallas kernels: 22.2 us -> 25.7 us
  local copies, waits for them, and re-layouts: 11.2 us -> 7.88 us
  starting transfers between devices: 43.4 us -> 42.1 us
  waiting for transfers between devices: 16 us -> 14.8 us
    pallas_call x3 -> x4, Pallas kernels: 5.74 us -> 9.76 us  [the longest x1 4.9 us: early_pick(): pl.pallas_call(early_kernel, out_shape=(shape, shape, jax.ShapeDtypeStruc...]
    unnamed x20 -> x18, local copies, waits for them, and re-layouts: 3.42 us -> 0.05 us
    all_to_all x1, starting transfers between devices: 21.9 us -> 20.4 us  [body(): parts = lax.all_to_all(parts, 'row', 0, 0, tiled=True)]
    ppermute x7, waiting for transfers between devices: 1.16 us -> 0.14 us  [within(): lax.ppermute(block, 'row', [(i, (i // ring ^ flip) * ring + (i % ring + t...]
  transfers between devices with their start and end apart: 12 -> 12, of which waited for: 3 -> 3; matrix products, arithmetic and copies ran while one was open for 11% -> 12% of each run, Pallas kernels for 15% -> 21%
where the time goes in v6:
time: 97.7 us; the launch traced here: 97.3 us
  starting transfers between devices  42.1 us (43%)
  Pallas kernels  25.7 us (26%)
  waiting for transfers between devices  14.8 us (15%)
  local copies, waits for them, and re-layouts  7.88 us (8%)
  matrix products  2.78 us (3%)
  other arithmetic  2.4 us (2%)
  between operations  1.58 us (2%)
    all_to_all x1, starting transfers between devices, body(): parts = lax.all_to_all(parts, 'row', 0, 0, tiled=True)  20.4 us
    ppermute x7, starting transfers between devices, within(): lax.ppermute(block, 'row', [(i, (i // ring ^ flip) * ring + (i % ring + t...  15.2 us
    all_to_all x1, waiting for transfers between devices, body(): gram = lax.all_to_all(gram, BOTH, 0, 0, tiled=True)  9.95 us
    pallas_call x1, Pallas kernels, forward(): pl.pallas_call(functools.partial(forward_kernel, vecs), out_shape=jax.Sha...  7.08 us
    pallas_call x1, Pallas kernels, backward(): pl.pallas_call(functools.partial(backward_kernel, vecs), out_shape=jax.Sh...  6.72 us
    pallas_call x1, Pallas kernels, early_pick(): pl.pallas_call(early_kernel, out_shape=(shape, shape, jax.ShapeDtypeStruc...  4.9 us
    all_to_all x1, waiting for transfers between devices, body(): parts = lax.all_to_all(parts, 'row', 0, 0, tiled=True)  4.73 us
    all_to_all x1, starting transfers between devices, body(): gram = lax.all_to_all(gram, BOTH, 0, 0, tiled=True)  4.53 us
  transfers between devices with their start and end apart: 12, of which 3 were waited for; matrix products, arithmetic and copies ran while one was open for 12% of the time, Pallas kernels for 21%

profile of v6, /device:TPU:1, one launch (start us, length us, event | category | flops | bytes accessed | tf_op | source)
XLA Modules:
  0.0 97.3 jit_solution(12689342900736784691)
XLA Ops:
  0.7 1.2 %fusion.4 = (bf16[4,16384]{1,0:T(4,128)(2,1)S(1)}, f32[4,16384]{1,0:T(4,128)S(1)}) fusion(f32[16384]{0:T(1024)} %param.19, f32[4,16384]{1,0:T(4,128)} %param.15, f32[4,16384]{1,0:T(4,128)} %param.14, f32[4]{0:T(128)} %param.18), kind=kLoop, calls=%fused_computation.10 | loop fusion | flops 262144 | bytes 983056 | tf_op jit(solution)/shard_map/convert_element_type | solution.py:358
  1.9 0.3 reshape.53
  2.3 2.5 %collective-permute-start = (bf16[256,256]{1,0:T(8,128)(2,1)S(1)}, bf16[256,256]{1,0:T(8,128)(2,1)S(1)}, u32[]{:S(2)}, u32[]{:S(2)}) collective-permute-start(bf16[256,256]{1,0:T(8,128)(2,1)S(1)} %bitcast.20), channel_id=1, source_target_pairs={{0,16},{16,32},{32,48},{48,0},{64,80},{80,96},{96,112},{112,64},{1... | collective-permute-start | bytes 393224 | tf_op jit(solution)/shard_map/ppermute | solution.py:354
  4.9 1.2 %collective-permute-start.2 = (bf16[256,256]{1,0:T(8,128)(2,1)S(1)}, bf16[256,256]{1,0:T(8,128)(2,1)S(1)}, u32[]{:S(2)}, u32[]{:S(2)}) collective-permute-start(bf16[256,256]{1,0:T(8,128)(2,1)S(1)} %bitcast.21), channel_id=1, source_target_pairs={{0,64},{16,80},{32,96},{48,112},{64,0},{80,16},{96,32},{112,48},{1... | collective-permute-start | bytes 393224 | tf_op jit(solution)/shard_map/ppermute | solution.py:354
  6.1 2.2 %collective-permute-start.3 = (bf16[256,256]{1,0:T(8,128)(2,1)S(1)}, bf16[256,256]{1,0:T(8,128)(2,1)S(1)}, u32[]{:S(2)}, u32[]{:S(2)}) collective-permute-start(bf16[256,256]{1,0:T(8,128)(2,1)S(1)} %bitcast.22), channel_id=1, source_target_pairs={{0,48},{16,0},{32,16},{48,32},{64,112},{80,64},{96,80},{112,96},{1... | collective-permute-start | bytes 393224 | tf_op jit(solution)/shard_map/ppermute | solution.py:354
  8.3 1.2 %collective-permute-start.4 = (bf16[256,256]{1,0:T(8,128)(2,1)S(1)}, bf16[256,256]{1,0:T(8,128)(2,1)S(1)}, u32[]{:S(2)}, u32[]{:S(2)}) collective-permute-start(bf16[256,256]{1,0:T(8,128)(2,1)S(1)} %bitcast.23), channel_id=1, source_target_pairs={{0,32},{16,48},{32,0},{48,16},{64,96},{80,112},{96,64},{112,80},{1... | collective-permute-start | bytes 393224 | tf_op jit(solution)/shard_map/ppermute | solution.py:354
  10.2 0.7 collective-permute-start.1
  10.9 5.0 %collective-permute-start.5 = (bf16[256,256]{1,0:T(8,128)(2,1)S(1)}, bf16[256,256]{1,0:T(8,128)(2,1)S(1)}, u32[]{:S(2)}, u32[]{:S(2)}) collective-permute-start(bf16[256,256]{1,0:T(8,128)(2,1)S(1)} %collective-permute-done.2.refs_1_), channel_id=1, source_target_pairs={{0,16},{16,32},{32,48},{48,0},{64,80},{80,96},{96,112},{112,64},{1... | collective-permute-start | bytes 393224 | tf_op jit(solution)/shard_map/ppermute | solution.py:354
  15.9 1.9 %collective-permute-start.6 = (bf16[256,256]{1,0:T(8,128)(2,1)S(1)}, bf16[256,256]{1,0:T(8,128)(2,1)S(1)}, u32[]{:S(2)}, u32[]{:S(2)}) collective-permute-start(bf16[256,256]{1,0:T(8,128)(2,1)S(1)} %collective-permute-done.2.refs_1_), channel_id=1, source_target_pairs={{0,48},{16,0},{32,16},{48,32},{64,112},{80,64},{96,80},{112,96},{1... | collective-permute-start | bytes 393224 | tf_op jit(solution)/shard_map/ppermute | solution.py:354
  17.8 1.1 %collective-permute-start.7 = (bf16[256,256]{1,0:T(8,128)(2,1)S(1)}, bf16[256,256]{1,0:T(8,128)(2,1)S(1)}, u32[]{:S(2)}, u32[]{:S(2)}) collective-permute-start(bf16[256,256]{1,0:T(8,128)(2,1)S(1)} %collective-permute-done.2.refs_1_), channel_id=1, source_target_pairs={{0,32},{16,48},{32,0},{48,16},{64,96},{80,112},{96,64},{112,80},{1... | collective-permute-start | bytes 393224 | tf_op jit(solution)/shard_map/ppermute | solution.py:354
  19.0 4.9 %early_pick.1 = (bf16[256,1024]{1,0:T(8,128)(2,1)S(1)}, bf16[256,1024]{1,0:T(8,128)(2,1)S(1)}, s32[1,1024]{1,0:T(1,128)S(1)}, bf16[1024,4096]{1,0:T(8,128)(2,1)S(1)}) custom-call(s32[5]{0:T(128)S(1)} %bitcast.28, s32[1]{0:T(128)} %bitcast.16.count_ref, s32[1,1024]{1,0:T(1,128)S(1)} %collective-permute-done.1.far_ref.index_ref, s32[1,1024]{1,0:T(1,128)S(1)} %bitcast.25, ...), custom_call_target="tpu_custom_call" | custom-call | tf_op jit(solution)/shard_map/early_pick/pallas_call | solution.py:65
  24.0 1.2 %pick.1 = bf16[256,1024]{1,0:T(8,128)(2,1)S(1)} custom-call(s32[3]{0:T(128)S(1)} %slice.8.base_ref, s32[1,1024]{1,0:T(1,128)S(1)} %collective-permute-done.1.far_ref.index_ref, bf16[256,1024]{1,0:T(8,128)(2,1)S(1)} %get-tuple-element.16.before_ref, bf16[256,256]{1,0:T(8,128)(2,1)S(1)} %collective-permute-done.5.refs_0_, ...), custom_call_target="tpu_custom_call" | custom-call | tf_op jit(solution)/shard_map/pick/pallas_call | solution.py:90
  25.2 0.7 collective-permute-start.9
  25.9 7.1 %forward.1 = bf16[1024,256]{1,0:T(8,128)(2,1)S(1)} custom-call(s32[3]{0:T(128)S(1)} %slice.8.base_ref, s32[1]{0:T(128)} %bitcast.17.count_ref, s32[1,1024]{1,0:T(1,128)S(1)} %bitcast.26, bf16[256,1024]{1,0:T(8,128)(2,1)S(1)} %get-tuple-element.14.before_ref, bf16[256,256]{1,0:T(8,128)(2,1)S(1)} %collective-permute-done.5.refs_0_, ...), custom_call_target="tpu_custom_call" | custom-call | tf_op jit(solution)/shard_map/forward/pallas_call | solution.py:173
  33.0 0.7 collective-permute-start.8
  33.7 6.7 %backward.1.part_ref = bf16[1024,256]{1,0:T(8,128)(2,1)S(1)} custom-call(bf16[256,1024]{1,0:T(8,128)(2,1)S(1)} %collective-permute-done.9.y_ref, bf16[4096,256]{1,0:T(8,128)(2,1)S(1)} %copy-done, bf16[1024,4096]{1,0:T(8,128)(2,1)S(1)} %get-tuple-element.15.refs_4_.tile_ref), custom_call_target="tpu_custom_call" | custom-call | tf_op jit(solution)/shard_map/backward/pallas_call | solution.py:223
  40.4 1.4 %spread.2.refs_0_ = f32[2048,256]{1,0:T(8,128)S(1)} custom-call(s32[1]{0:T(128)} %bitcast.18.count_ref, s32[1,1024]{1,0:T(1,128)S(1)} %bitcast.27, bf16[1024,256]{1,0:T(8,128)(2,1)S(1)} %backward.1.part_ref), custom_call_target="tpu_custom_call" | custom-call | tf_op jit(solution)/shard_map/spread/pallas_call | solution.py:249
  41.9 2.3 %spread.3 = bf16[2048,256]{1,0:T(8,128)(2,1)} custom-call(s32[1]{0:T(128)} %constant.46.clone.1.count_ref, s32[1,1024]{1,0:T(1,128)S(1)} %get-tuple-element.13.index_ref, bf16[1024,256]{1,0:T(8,128)(2,1)S(1)} %collective-permute-done.8.part_ref, f32[2048,256]{1,0:T(8,128)S(1)} %spread.2.refs_0_), custom_call_target="tpu_custom_call" | custom-call | tf_op jit(solution)/shard_map/spread/pallas_call | solution.py:249
  44.2 20.4 %all-to-all-start = ((bf16[8,256,256]{2,1,0:T(8,128)(2,1)}), bf16[8,256,256]{2,1,0:T(8,128)(2,1)S(1)}, u32[]{:S(2)}, u32[]{:S(2)}) async-start(bf16[8,256,256]{2,1,0:T(8,128)(2,1)} %bitcast.7), calls=%async_computation | async-start | bytes 2097152 | tf_op jit(solution)/shard_map/all_to_all | solution.py:377
  64.6 1.1 %pad_maximum_fusion = f32[12,16384]{1,0:T(8,128)} fusion(f32[4,16384]{1,0:T(4,128)S(1)} %copy-done.5, f32[4,16384]{1,0:T(4,128)S(1)} %get-tuple-element.22, f32[4,16384]{1,0:T(4,128)S(1)} %copy-done.3), kind=kLoop, calls=%fused_computation | loop fusion | flops 393216 | bytes 1572864 | tf_op jit(solution)/shard_map/concatenate | solution.py:378
  65.7 1.8 %reshape.56 = f32[12,256,64]{2,1,0:T(8,128)S(1)} reshape(f32[12,16384]{1,0:T(8,128)} %pad_maximum_fusion) | data formatting | bytes 1572864 | tf_op jit(solution)/shard_map/reshape | solution.py:383
  67.6 0.4 copy.21
  68.0 0.3 copy.22.vector_ref
  68.3 3.5 %concatenate.8 = f32[20,16384]{1,0:T(8,128)S(1)} concatenate(f32[4,16384]{1,0:T(4,128)} %param.14, f32[4,16384]{1,0:T(4,128)} %copy-done.4, f32[4,16384]{1,0:T(4,128)} %param.16, f32[4,16384]{1,0:T(4,128)} %param.15, f32[4,16384]{1,0:T(4,128)} %param.17), dimensions={0} | concatenate | bytes 2621440 | tf_op jit(solution)/shard_map/concatenate | solution.py:379
  71.8 2.8 %fusion.3 = f32[12,20]{1,0:T(8,128)S(1)} fusion(f32[20,16384]{1,0:T(8,128)S(1)} %concatenate.8, f32[4,16384]{1,0:T(4,128)} %param.16, f32[4,16384]{1,0:T(4,128)} %copy-done.4, f32[4,16384]{1,0:T(4,128)} %param.14), kind=kOutput, calls=%fused_computation.9 | convolution fusion | flops 47579136 | bytes 2098112 | tf_op jit(solution)/shard_map/dot_general | solution.py:380
  74.7 4.7 %all-to-all-done.part_ref = bf16[8,256,256]{2,1,0:T(8,128)(2,1)S(1)} async-done(((bf16[8,256,256]{2,1,0:T(8,128)(2,1)}), bf16[8,256,256]{2,1,0:T(8,128)(2,1)S(1)}, u32[]{:S(2)}, u32[]{:S(2)}) %all-to-all-start) | async-done | bytes 1048608 | tf_op jit(solution)/shard_map/all_to_all | solution.py:377
  79.4 1.3 %totalled.1 = (f32[256,256]{1,0:T(8,128)S(1)}, f32[128,3,128]{2,1,0:T(4,128)}) custom-call(bf16[8,256,256]{2,1,0:T(8,128)(2,1)S(1)} %all-to-all-done.part_ref, f32[256,768]{1,0:T(8,128)S(1)} %copy.22.vector_ref, f32[2,128]{1,0:T(2,128)S(1)} %pad.4.early_ref), custom_call_target="tpu_custom_call" | custom-call | tf_op jit(solution)/shard_map/totalled/pallas_call | solution.py:287
  80.7 4.5 %all-to-all-start.1 = ((f32[128,3,128]{2,1,0:T(4,128)}), f32[128,3,128]{2,1,0:T(4,128)S(1)}, u32[]{:S(2)}, u32[]{:S(2)}) async-start(f32[128,3,128]{2,1,0:T(4,128)} %get-tuple-element.18), calls=%async_computation.1 | async-start | bytes 524288 | tf_op jit(solution)/shard_map/all_to_all | solution.py:386
  85.3 0.2 copy.24
  85.5 0.9 reshape.60
  86.5 9.9 %all-to-all-done.1.gram_ref = f32[128,3,128]{2,1,0:T(4,128)S(1)} async-done(((f32[128,3,128]{2,1,0:T(4,128)}), f32[128,3,128]{2,1,0:T(4,128)S(1)}, u32[]{:S(2)}, u32[]{:S(2)}) %all-to-all-start.1) | async-done | bytes 196640 | tf_op jit(solution)/shard_map/all_to_all | solution.py:386
  96.4 0.8 unpacked.1
  (35 shorter events, 0.6 us)
Async XLA Ops:
  0.6 18.3 %copy-start.7 = (s32[8]{0:T(128)S(1)}, s32[8]{0:T(128)}, u32[]{:S(2)}) copy-start(s32[8]{0:T(128)} %constant.67) | copy-start | bytes 100
  0.6 18.2 %copy-start.8 = (s32[8]{0:T(128)S(1)}, s32[8]{0:T(128)}, u32[]{:S(2)}) copy-start(s32[8]{0:T(128)} %constant.57.clone) | copy-start | bytes 100
  0.7 9.5 %copy-start.6 = (s32[1,1,1024]{2,1,0:T(1,128)S(1)}, s32[1,1,1024]{2,1,0:T(1,128)}, u32[]{:S(2)}) copy-start(s32[1,1,1024]{2,1,0:T(1,128)} %param.21) | copy-start | bytes 12292
  0.7 18.3 %copy-start.2 = (s32[1,1,1024]{2,1,0:T(1,128)S(1)}, s32[1,1,1024]{2,1,0:T(1,128)}, u32[]{:S(2)}) copy-start(s32[1,1,1024]{2,1,0:T(1,128)} %param.22) | copy-start | bytes 12292
  1.9 62.6 %copy-start.4 = (f32[4,16384]{1,0:T(4,128)}, f32[4,16384]{1,0:T(4,128)S(1)}, u32[]{:S(2)}) copy-start(f32[4,16384]{1,0:T(4,128)S(1)} %get-tuple-element.22) | copy-start | bytes 786436
  2.3 7.9 %collective-permute-start = (bf16[256,256]{1,0:T(8,128)(2,1)S(1)}, bf16[256,256]{1,0:T(8,128)(2,1)S(1)}, u32[]{:S(2)}, u32[]{:S(2)}) collective-permute-start(bf16[256,256]{1,0:T(8,128)(2,1)S(1)} %bitcast.20), channel_id=1, source_target_pairs={{0,16},{16,32},{32,48},{48,0},{64,80},{80,96},{96,112},{112,64},{1... | collective-permute-start | bytes 393224 | tf_op jit(solution)/shard_map/ppermute | solution.py:354
  4.9 6.0 %collective-permute-start.2 = (bf16[256,256]{1,0:T(8,128)(2,1)S(1)}, bf16[256,256]{1,0:T(8,128)(2,1)S(1)}, u32[]{:S(2)}, u32[]{:S(2)}) collective-permute-start(bf16[256,256]{1,0:T(8,128)(2,1)S(1)} %bitcast.21), channel_id=1, source_target_pairs={{0,64},{16,80},{32,96},{48,112},{64,0},{80,16},{96,32},{112,48},{1... | collective-permute-start | bytes 393224 | tf_op jit(solution)/shard_map/ppermute | solution.py:354
  6.1 11.7 %collective-permute-start.3 = (bf16[256,256]{1,0:T(8,128)(2,1)S(1)}, bf16[256,256]{1,0:T(8,128)(2,1)S(1)}, u32[]{:S(2)}, u32[]{:S(2)}) collective-permute-start(bf16[256,256]{1,0:T(8,128)(2,1)S(1)} %bitcast.22), channel_id=1, source_target_pairs={{0,48},{16,0},{32,16},{48,32},{64,112},{80,64},{96,80},{112,96},{1... | collective-permute-start | bytes 393224 | tf_op jit(solution)/shard_map/ppermute | solution.py:354
  8.3 10.7 %collective-permute-start.4 = (bf16[256,256]{1,0:T(8,128)(2,1)S(1)}, bf16[256,256]{1,0:T(8,128)(2,1)S(1)}, u32[]{:S(2)}, u32[]{:S(2)}) collective-permute-start(bf16[256,256]{1,0:T(8,128)(2,1)S(1)} %bitcast.23), channel_id=1, source_target_pairs={{0,32},{16,48},{32,0},{48,16},{64,96},{80,112},{96,64},{112,80},{1... | collective-permute-start | bytes 393224 | tf_op jit(solution)/shard_map/ppermute | solution.py:354
  10.2 8.8 %collective-permute-start.1 = (s32[1,1024]{1,0:T(1,128)S(1)}, s32[1,1024]{1,0:T(1,128)S(1)}, u32[]{:S(2)}, u32[]{:S(2)}) collective-permute-start(s32[1,1024]{1,0:T(1,128)S(1)} %compare_select_fusion), channel_id=1, source_target_pairs={{0,0},{1,1},{2,2},{3,3},{4,4},{5,5},{6,6},{7,7},{8,8},{9,9},{10,10... | collective-permute-start | bytes 12296 | tf_op jit(solution)/shard_map/ppermute | solution.py:351
  10.9 13.0 %collective-permute-start.5 = (bf16[256,256]{1,0:T(8,128)(2,1)S(1)}, bf16[256,256]{1,0:T(8,128)(2,1)S(1)}, u32[]{:S(2)}, u32[]{:S(2)}) collective-permute-start(bf16[256,256]{1,0:T(8,128)(2,1)S(1)} %collective-permute-done.2.refs_1_), channel_id=1, source_target_pairs={{0,16},{16,32},{32,48},{48,0},{64,80},{80,96},{96,112},{112,64},{1... | collective-permute-start | bytes 393224 | tf_op jit(solution)/shard_map/ppermute | solution.py:354
  15.9 8.0 %collective-permute-start.6 = (bf16[256,256]{1,0:T(8,128)(2,1)S(1)}, bf16[256,256]{1,0:T(8,128)(2,1)S(1)}, u32[]{:S(2)}, u32[]{:S(2)}) collective-permute-start(bf16[256,256]{1,0:T(8,128)(2,1)S(1)} %collective-permute-done.2.refs_1_), channel_id=1, source_target_pairs={{0,48},{16,0},{32,16},{48,32},{64,112},{80,64},{96,80},{112,96},{1... | collective-permute-start | bytes 393224 | tf_op jit(solution)/shard_map/ppermute | solution.py:354
  17.8 6.3 %collective-permute-start.7 = (bf16[256,256]{1,0:T(8,128)(2,1)S(1)}, bf16[256,256]{1,0:T(8,128)(2,1)S(1)}, u32[]{:S(2)}, u32[]{:S(2)}) collective-permute-start(bf16[256,256]{1,0:T(8,128)(2,1)S(1)} %collective-permute-done.2.refs_1_), channel_id=1, source_target_pairs={{0,32},{16,48},{32,0},{48,16},{64,96},{80,112},{96,64},{112,80},{1... | collective-permute-start | bytes 393224 | tf_op jit(solution)/shard_map/ppermute | solution.py:354
  19.0 6.9 %copy-start.1 = (bf16[256,256]{1,0:T(8,128)(2,1)S(1)}, bf16[256,256]{1,0:T(8,128)(2,1)}, u32[]{:S(2)}) copy-start(bf16[256,256]{1,0:T(8,128)(2,1)} %constant.59.clone.refs_3_) | copy-start | bytes 393220
  25.2 8.5 %collective-permute-start.9 = (bf16[256,1024]{1,0:T(8,128)(2,1)S(1)}, bf16[256,1024]{1,0:T(8,128)(2,1)S(1)}, u32[]{:S(2)}, u32[]{:S(2)}) collective-permute-start(bf16[256,1024]{1,0:T(8,128)(2,1)S(1)} %pick.1), channel_id=1, source_target_pairs={{0,0},{1,1},{2,2},{3,3},{4,4},{5,5},{6,6},{7,7},{8,8},{9,9},{10,10... | collective-permute-start | bytes 1572872 | tf_op jit(solution)/shard_map/ppermute | solution.py:351
  25.9 7.8 %copy-start = (bf16[4096,256]{1,0:T(8,128)(2,1)S(1)}, bf16[4096,256]{1,0:T(8,128)(2,1)}, u32[]{:S(2)}) copy-start(bf16[4096,256]{1,0:T(8,128)(2,1)} %constant.60.clone.route_ref) | copy-start | bytes 6291460
  33.0 8.9 %collective-permute-start.8 = (bf16[1024,256]{1,0:T(8,128)(2,1)S(1)}, bf16[1024,256]{1,0:T(8,128)(2,1)S(1)}, u32[]{:S(2)}, u32[]{:S(2)}) collective-permute-start(bf16[1024,256]{1,0:T(8,128)(2,1)S(1)} %forward.1), channel_id=1, source_target_pairs={{0,0},{1,1},{2,2},{3,3},{4,4},{5,5},{6,6},{7,7},{8,8},{9,9},{10,10... | collective-permute-start | bytes 1572872 | tf_op jit(solution)/shard_map/ppermute | solution.py:351
  44.2 20.4 %copy-start.3 = (f32[4,16384]{1,0:T(4,128)S(1)}, f32[4,16384]{1,0:T(4,128)}, u32[]{:S(2)}) copy-start(f32[4,16384]{1,0:T(4,128)} %param.14) | copy-start | bytes 786436
  44.2 20.4 %copy-start.5 = (f32[4,16384]{1,0:T(4,128)S(1)}, f32[4,16384]{1,0:T(4,128)}, u32[]{:S(2)}) copy-start(f32[4,16384]{1,0:T(4,128)} %param.16) | copy-start | bytes 786436
  44.2 35.2 %all-to-all-start = ((bf16[8,256,256]{2,1,0:T(8,128)(2,1)}), bf16[8,256,256]{2,1,0:T(8,128)(2,1)S(1)}, u32[]{:S(2)}, u32[]{:S(2)}) async-start(bf16[8,256,256]{2,1,0:T(8,128)(2,1)} %bitcast.7), calls=%async_computation | async-start | bytes 2097152 | tf_op jit(solution)/shard_map/all_to_all | solution.py:377
  80.7 15.8 %all-to-all-start.1 = ((f32[128,3,128]{2,1,0:T(4,128)}), f32[128,3,128]{2,1,0:T(4,128)S(1)}, u32[]{:S(2)}, u32[]{:S(2)}) async-start(f32[128,3,128]{2,1,0:T(4,128)} %get-tuple-element.18), calls=%async_computation.1 | async-start | bytes 524288 | tf_op jit(solution)/shard_map/all_to_all | solution.py:386

commit v7 on v6

--- a/solution.py
+++ b/solution.py
@@ -163,7 +163,7 @@
             packed_ref[at, v * LANES : (v + 1) * LANES] = part.astype(BF16)
         return 0
 
-    lax.fori_loop(0, x_ref.shape[0] // GROUP, step, 0, unroll=8)
+    lax.fori_loop(0, x_ref.shape[0] // GROUP, step, 0, unroll=32)
     out_ref[...] = dot(packed_ref[...], order_ref[...], NT).astype(BF16)
 
 
@@ -214,7 +214,7 @@
             out_ref[at, p * LANES : (p + 1) * LANES] = jnp.where(first, sums[2 * p], sums[2 * p + 1]).astype(BF16)
         return 0
 
-    lax.fori_loop(0, out_ref.shape[0] // GROUP, step, 0, unroll=8)
+    lax.fori_loop(0, out_ref.shape[0] // GROUP, step, 0, unroll=32)
 
 
 def backward(vecs, far, route, tile):

time: 97.7 us -> 96.7 us (0.990)
  Pallas kernels: 25.7 us -> 22.3 us
  starting transfers between devices: 42.1 us -> 44.1 us
    pallas_call x1, Pallas kernels: 7.08 us -> 5.02 us  [forward(): pl.pallas_call(functools.partial(forward_kernel, vecs), out_shape=jax.Sha...]
    pallas_call x1, Pallas kernels: 6.72 us -> 5.35 us  [backward(): pl.pallas_call(functools.partial(backward_kernel, vecs), out_shape=jax.Sh...]
    all_to_all x1, starting transfers between devices: 20.4 us -> 21.6 us  [body(): parts = lax.all_to_all(parts, 'row', 0, 0, tiled=True)]
  transfers between devices with their start and end apart: 12 -> 12, of which waited for: 3 -> 3; matrix products, arithmetic and copies ran while one was open for 12% -> 12% of each run, Pallas kernels for 21% -> 17%
where the time goes in v7:
time: 96.7 us; the launch traced here: 96.3 us
  starting transfers between devices  44.1 us (46%)
  Pallas kernels  22.3 us (23%)
  waiting for transfers between devices  15.3 us (16%)
  local copies, waits for them, and re-layouts  7.88 us (8%)
  matrix products  2.78 us (3%)
  other arithmetic  2.4 us (2%)
  between operations  1.58 us (2%)
    all_to_all x1, starting transfers between devices, body(): parts = lax.all_to_all(parts, 'row', 0, 0, tiled=True)  21.6 us
    ppermute x7, starting transfers between devices, within(): lax.ppermute(block, 'row', [(i, (i // ring ^ flip) * ring + (i % ring + t...  15.2 us
    all_to_all x1, waiting for transfers between devices, body(): gram = lax.all_to_all(gram, BOTH, 0, 0, tiled=True)  9.95 us
    pallas_call x1, Pallas kernels, backward(): pl.pallas_call(functools.partial(backward_kernel, vecs), out_shape=jax.Sh...  5.35 us
    all_to_all x1, waiting for transfers between devices, body(): parts = lax.all_to_all(parts, 'row', 0, 0, tiled=True)  5.21 us
    all_to_all x1, starting transfers between devices, body(): gram = lax.all_to_all(gram, BOTH, 0, 0, tiled=True)  5.14 us
    pallas_call x1, Pallas kernels, forward(): pl.pallas_call(functools.partial(forward_kernel, vecs), out_shape=jax.Sha...  5.02 us
    pallas_call x1, Pallas kernels, early_pick(): pl.pallas_call(early_kernel, out_shape=(shape, shape, jax.ShapeDtypeStruc...  4.9 us
  transfers between devices with their start and end apart: 12, of which 3 were waited for; matrix products, arithmetic and copies ran while one was open for 12% of the time, Pallas kernels for 17%

profile of v7, /device:TPU:1, one launch (start us, length us, event | category | flops | bytes accessed | tf_op | source)
XLA Modules:
  0.0 96.3 jit_solution(9504769435872619251)
XLA Ops:
  0.7 1.2 %fusion.4 = (bf16[4,16384]{1,0:T(4,128)(2,1)S(1)}, f32[4,16384]{1,0:T(4,128)S(1)}) fusion(f32[16384]{0:T(1024)} %param.19, f32[4,16384]{1,0:T(4,128)} %param.15, f32[4,16384]{1,0:T(4,128)} %param.14, f32[4]{0:T(128)} %param.18), kind=kLoop, calls=%fused_computation.10 | loop fusion | flops 262144 | bytes 983056 | tf_op jit(solution)/shard_map/convert_element_type | solution.py:358
  1.9 0.3 reshape.53
  2.3 2.5 %collective-permute-start = (bf16[256,256]{1,0:T(8,128)(2,1)S(1)}, bf16[256,256]{1,0:T(8,128)(2,1)S(1)}, u32[]{:S(2)}, u32[]{:S(2)}) collective-permute-start(bf16[256,256]{1,0:T(8,128)(2,1)S(1)} %bitcast.20), channel_id=1, source_target_pairs={{0,16},{16,32},{32,48},{48,0},{64,80},{80,96},{96,112},{112,64},{1... | collective-permute-start | bytes 393224 | tf_op jit(solution)/shard_map/ppermute | solution.py:354
  4.9 1.2 %collective-permute-start.2 = (bf16[256,256]{1,0:T(8,128)(2,1)S(1)}, bf16[256,256]{1,0:T(8,128)(2,1)S(1)}, u32[]{:S(2)}, u32[]{:S(2)}) collective-permute-start(bf16[256,256]{1,0:T(8,128)(2,1)S(1)} %bitcast.21), channel_id=1, source_target_pairs={{0,64},{16,80},{32,96},{48,112},{64,0},{80,16},{96,32},{112,48},{1... | collective-permute-start | bytes 393224 | tf_op jit(solution)/shard_map/ppermute | solution.py:354
  6.1 2.2 %collective-permute-start.3 = (bf16[256,256]{1,0:T(8,128)(2,1)S(1)}, bf16[256,256]{1,0:T(8,128)(2,1)S(1)}, u32[]{:S(2)}, u32[]{:S(2)}) collective-permute-start(bf16[256,256]{1,0:T(8,128)(2,1)S(1)} %bitcast.22), channel_id=1, source_target_pairs={{0,48},{16,0},{32,16},{48,32},{64,112},{80,64},{96,80},{112,96},{1... | collective-permute-start | bytes 393224 | tf_op jit(solution)/shard_map/ppermute | solution.py:354
  8.3 1.2 %collective-permute-start.4 = (bf16[256,256]{1,0:T(8,128)(2,1)S(1)}, bf16[256,256]{1,0:T(8,128)(2,1)S(1)}, u32[]{:S(2)}, u32[]{:S(2)}) collective-permute-start(bf16[256,256]{1,0:T(8,128)(2,1)S(1)} %bitcast.23), channel_id=1, source_target_pairs={{0,32},{16,48},{32,0},{48,16},{64,96},{80,112},{96,64},{112,80},{1... | collective-permute-start | bytes 393224 | tf_op jit(solution)/shard_map/ppermute | solution.py:354
  10.2 0.7 collective-permute-start.1
  10.9 5.0 %collective-permute-start.5 = (bf16[256,256]{1,0:T(8,128)(2,1)S(1)}, bf16[256,256]{1,0:T(8,128)(2,1)S(1)}, u32[]{:S(2)}, u32[]{:S(2)}) collective-permute-start(bf16[256,256]{1,0:T(8,128)(2,1)S(1)} %collective-permute-done.2.refs_1_), channel_id=1, source_target_pairs={{0,16},{16,32},{32,48},{48,0},{64,80},{80,96},{96,112},{112,64},{1... | collective-permute-start | bytes 393224 | tf_op jit(solution)/shard_map/ppermute | solution.py:354
  15.9 1.9 %collective-permute-start.6 = (bf16[256,256]{1,0:T(8,128)(2,1)S(1)}, bf16[256,256]{1,0:T(8,128)(2,1)S(1)}, u32[]{:S(2)}, u32[]{:S(2)}) collective-permute-start(bf16[256,256]{1,0:T(8,128)(2,1)S(1)} %collective-permute-done.2.refs_1_), channel_id=1, source_target_pairs={{0,48},{16,0},{32,16},{48,32},{64,112},{80,64},{96,80},{112,96},{1... | collective-permute-start | bytes 393224 | tf_op jit(solution)/shard_map/ppermute | solution.py:354
  17.8 1.1 %collective-permute-start.7 = (bf16[256,256]{1,0:T(8,128)(2,1)S(1)}, bf16[256,256]{1,0:T(8,128)(2,1)S(1)}, u32[]{:S(2)}, u32[]{:S(2)}) collective-permute-start(bf16[256,256]{1,0:T(8,128)(2,1)S(1)} %collective-permute-done.2.refs_1_), channel_id=1, source_target_pairs={{0,32},{16,48},{32,0},{48,16},{64,96},{80,112},{96,64},{112,80},{1... | collective-permute-start | bytes 393224 | tf_op jit(solution)/shard_map/ppermute | solution.py:354
  19.0 4.9 %early_pick.1 = (bf16[256,1024]{1,0:T(8,128)(2,1)S(1)}, bf16[256,1024]{1,0:T(8,128)(2,1)S(1)}, s32[1,1024]{1,0:T(1,128)S(1)}, bf16[1024,4096]{1,0:T(8,128)(2,1)S(1)}) custom-call(s32[5]{0:T(128)S(1)} %bitcast.28, s32[1]{0:T(128)} %bitcast.16.count_ref, s32[1,1024]{1,0:T(1,128)S(1)} %collective-permute-done.1.far_ref.index_ref, s32[1,1024]{1,0:T(1,128)S(1)} %bitcast.25, ...), custom_call_target="tpu_custom_call" | custom-call | tf_op jit(solution)/shard_map/early_pick/pallas_call | solution.py:65
  24.0 1.2 %pick.1 = bf16[256,1024]{1,0:T(8,128)(2,1)S(1)} custom-call(s32[3]{0:T(128)S(1)} %slice.8.base_ref, s32[1,1024]{1,0:T(1,128)S(1)} %collective-permute-done.1.far_ref.index_ref, bf16[256,1024]{1,0:T(8,128)(2,1)S(1)} %get-tuple-element.16.before_ref, bf16[256,256]{1,0:T(8,128)(2,1)S(1)} %collective-permute-done.5.refs_0_, ...), custom_call_target="tpu_custom_call" | custom-call | tf_op jit(solution)/shard_map/pick/pallas_call | solution.py:90
  25.2 0.7 collective-permute-start.9
  25.9 5.0 %forward.1 = bf16[1024,256]{1,0:T(8,128)(2,1)S(1)} custom-call(s32[3]{0:T(128)S(1)} %slice.8.base_ref, s32[1]{0:T(128)} %bitcast.17.count_ref, s32[1,1024]{1,0:T(1,128)S(1)} %bitcast.26, bf16[256,1024]{1,0:T(8,128)(2,1)S(1)} %get-tuple-element.14.before_ref, bf16[256,256]{1,0:T(8,128)(2,1)S(1)} %collective-permute-done.5.refs_0_, ...), custom_call_target="tpu_custom_call" | custom-call | tf_op jit(solution)/shard_map/forward/pallas_call | solution.py:173
  30.9 0.9 collective-permute-start.8
  31.8 5.3 %backward.1.part_ref = bf16[1024,256]{1,0:T(8,128)(2,1)S(1)} custom-call(bf16[256,1024]{1,0:T(8,128)(2,1)S(1)} %collective-permute-done.9.y_ref, bf16[4096,256]{1,0:T(8,128)(2,1)S(1)} %copy-done, bf16[1024,4096]{1,0:T(8,128)(2,1)S(1)} %get-tuple-element.15.refs_4_.tile_ref), custom_call_target="tpu_custom_call" | custom-call | tf_op jit(solution)/shard_map/backward/pallas_call | solution.py:223
  37.2 1.4 %spread.2.refs_0_ = f32[2048,256]{1,0:T(8,128)S(1)} custom-call(s32[1]{0:T(128)} %bitcast.18.count_ref, s32[1,1024]{1,0:T(1,128)S(1)} %bitcast.27, bf16[1024,256]{1,0:T(8,128)(2,1)S(1)} %backward.1.part_ref), custom_call_target="tpu_custom_call" | custom-call | tf_op jit(solution)/shard_map/spread/pallas_call | solution.py:249
  38.7 2.3 %spread.3 = bf16[2048,256]{1,0:T(8,128)(2,1)} custom-call(s32[1]{0:T(128)} %constant.46.clone.1.count_ref, s32[1,1024]{1,0:T(1,128)S(1)} %get-tuple-element.13.index_ref, bf16[1024,256]{1,0:T(8,128)(2,1)S(1)} %collective-permute-done.8.part_ref, f32[2048,256]{1,0:T(8,128)S(1)} %spread.2.refs_0_), custom_call_target="tpu_custom_call" | custom-call | tf_op jit(solution)/shard_map/spread/pallas_call | solution.py:249
  40.9 21.6 %all-to-all-start = ((bf16[8,256,256]{2,1,0:T(8,128)(2,1)}), bf16[8,256,256]{2,1,0:T(8,128)(2,1)S(1)}, u32[]{:S(2)}, u32[]{:S(2)}) async-start(bf16[8,256,256]{2,1,0:T(8,128)(2,1)} %bitcast.7), calls=%async_computation | async-start | bytes 2097152 | tf_op jit(solution)/shard_map/all_to_all | solution.py:377
  62.5 1.1 %pad_maximum_fusion = f32[12,16384]{1,0:T(8,128)} fusion(f32[4,16384]{1,0:T(4,128)S(1)} %copy-done.5, f32[4,16384]{1,0:T(4,128)S(1)} %get-tuple-element.22, f32[4,16384]{1,0:T(4,128)S(1)} %copy-done.3), kind=kLoop, calls=%fused_computation | loop fusion | flops 393216 | bytes 1572864 | tf_op jit(solution)/shard_map/concatenate | solution.py:378
  63.7 1.8 %reshape.56 = f32[12,256,64]{2,1,0:T(8,128)S(1)} reshape(f32[12,16384]{1,0:T(8,128)} %pad_maximum_fusion) | data formatting | bytes 1572864 | tf_op jit(solution)/shard_map/reshape | solution.py:383
  65.5 0.4 copy.21
  66.0 0.3 copy.22.vector_ref
  66.2 3.5 %concatenate.8 = f32[20,16384]{1,0:T(8,128)S(1)} concatenate(f32[4,16384]{1,0:T(4,128)} %param.14, f32[4,16384]{1,0:T(4,128)} %copy-done.4, f32[4,16384]{1,0:T(4,128)} %param.16, f32[4,16384]{1,0:T(4,128)} %param.15, f32[4,16384]{1,0:T(4,128)} %param.17), dimensions={0} | concatenate | bytes 2621440 | tf_op jit(solution)/shard_map/concatenate | solution.py:379
  69.7 2.8 %fusion.3 = f32[12,20]{1,0:T(8,128)S(1)} fusion(f32[20,16384]{1,0:T(8,128)S(1)} %concatenate.8, f32[4,16384]{1,0:T(4,128)} %param.16, f32[4,16384]{1,0:T(4,128)} %copy-done.4, f32[4,16384]{1,0:T(4,128)} %param.14), kind=kOutput, calls=%fused_computation.9 | convolution fusion | flops 47579136 | bytes 2098112 | tf_op jit(solution)/shard_map/dot_general | solution.py:380
  72.6 5.2 %all-to-all-done.part_ref = bf16[8,256,256]{2,1,0:T(8,128)(2,1)S(1)} async-done(((bf16[8,256,256]{2,1,0:T(8,128)(2,1)}), bf16[8,256,256]{2,1,0:T(8,128)(2,1)S(1)}, u32[]{:S(2)}, u32[]{:S(2)}) %all-to-all-start) | async-done | bytes 1048608 | tf_op jit(solution)/shard_map/all_to_all | solution.py:377
  77.8 1.3 %totalled.1 = (f32[256,256]{1,0:T(8,128)S(1)}, f32[128,3,128]{2,1,0:T(4,128)}) custom-call(bf16[8,256,256]{2,1,0:T(8,128)(2,1)S(1)} %all-to-all-done.part_ref, f32[256,768]{1,0:T(8,128)S(1)} %copy.22.vector_ref, f32[2,128]{1,0:T(2,128)S(1)} %pad.4.early_ref), custom_call_target="tpu_custom_call" | custom-call | tf_op jit(solution)/shard_map/totalled/pallas_call | solution.py:287
  79.1 5.1 %all-to-all-start.1 = ((f32[128,3,128]{2,1,0:T(4,128)}), f32[128,3,128]{2,1,0:T(4,128)S(1)}, u32[]{:S(2)}, u32[]{:S(2)}) async-start(f32[128,3,128]{2,1,0:T(4,128)} %get-tuple-element.18), calls=%async_computation.1 | async-start | bytes 524288 | tf_op jit(solution)/shard_map/all_to_all | solution.py:386
  84.4 0.2 copy.24
  84.6 0.9 reshape.60
  85.5 9.9 %all-to-all-done.1.gram_ref = f32[128,3,128]{2,1,0:T(4,128)S(1)} async-done(((f32[128,3,128]{2,1,0:T(4,128)}), f32[128,3,128]{2,1,0:T(4,128)S(1)}, u32[]{:S(2)}, u32[]{:S(2)}) %all-to-all-start.1) | async-done | bytes 196640 | tf_op jit(solution)/shard_map/all_to_all | solution.py:386
  95.4 0.8 unpacked.1
  (35 shorter events, 0.6 us)
Async XLA Ops:
  0.6 18.3 %copy-start.7 = (s32[8]{0:T(128)S(1)}, s32[8]{0:T(128)}, u32[]{:S(2)}) copy-start(s32[8]{0:T(128)} %constant.67) | copy-start | bytes 100
  0.6 18.2 %copy-start.8 = (s32[8]{0:T(128)S(1)}, s32[8]{0:T(128)}, u32[]{:S(2)}) copy-start(s32[8]{0:T(128)} %constant.57.clone) | copy-start | bytes 100
  0.7 9.5 %copy-start.6 = (s32[1,1,1024]{2,1,0:T(1,128)S(1)}, s32[1,1,1024]{2,1,0:T(1,128)}, u32[]{:S(2)}) copy-start(s32[1,1,1024]{2,1,0:T(1,128)} %param.21) | copy-start | bytes 12292
  0.7 18.3 %copy-start.2 = (s32[1,1,1024]{2,1,0:T(1,128)S(1)}, s32[1,1,1024]{2,1,0:T(1,128)}, u32[]{:S(2)}) copy-start(s32[1,1,1024]{2,1,0:T(1,128)} %param.22) | copy-start | bytes 12292
  1.9 60.6 %copy-start.4 = (f32[4,16384]{1,0:T(4,128)}, f32[4,16384]{1,0:T(4,128)S(1)}, u32[]{:S(2)}) copy-start(f32[4,16384]{1,0:T(4,128)S(1)} %get-tuple-element.22) | copy-start | bytes 786436
  2.3 7.9 %collective-permute-start = (bf16[256,256]{1,0:T(8,128)(2,1)S(1)}, bf16[256,256]{1,0:T(8,128)(2,1)S(1)}, u32[]{:S(2)}, u32[]{:S(2)}) collective-permute-start(bf16[256,256]{1,0:T(8,128)(2,1)S(1)} %bitcast.20), channel_id=1, source_target_pairs={{0,16},{16,32},{32,48},{48,0},{64,80},{80,96},{96,112},{112,64},{1... | collective-permute-start | bytes 393224 | tf_op jit(solution)/shard_map/ppermute | solution.py:354
  4.9 6.0 %collective-permute-start.2 = (bf16[256,256]{1,0:T(8,128)(2,1)S(1)}, bf16[256,256]{1,0:T(8,128)(2,1)S(1)}, u32[]{:S(2)}, u32[]{:S(2)}) collective-permute-start(bf16[256,256]{1,0:T(8,128)(2,1)S(1)} %bitcast.21), channel_id=1, source_target_pairs={{0,64},{16,80},{32,96},{48,112},{64,0},{80,16},{96,32},{112,48},{1... | collective-permute-start | bytes 393224 | tf_op jit(solution)/shard_map/ppermute | solution.py:354
  6.1 11.7 %collective-permute-start.3 = (bf16[256,256]{1,0:T(8,128)(2,1)S(1)}, bf16[256,256]{1,0:T(8,128)(2,1)S(1)}, u32[]{:S(2)}, u32[]{:S(2)}) collective-permute-start(bf16[256,256]{1,0:T(8,128)(2,1)S(1)} %bitcast.22), channel_id=1, source_target_pairs={{0,48},{16,0},{32,16},{48,32},{64,112},{80,64},{96,80},{112,96},{1... | collective-permute-start | bytes 393224 | tf_op jit(solution)/shard_map/ppermute | solution.py:354
  8.3 10.7 %collective-permute-start.4 = (bf16[256,256]{1,0:T(8,128)(2,1)S(1)}, bf16[256,256]{1,0:T(8,128)(2,1)S(1)}, u32[]{:S(2)}, u32[]{:S(2)}) collective-permute-start(bf16[256,256]{1,0:T(8,128)(2,1)S(1)} %bitcast.23), channel_id=1, source_target_pairs={{0,32},{16,48},{32,0},{48,16},{64,96},{80,112},{96,64},{112,80},{1... | collective-permute-start | bytes 393224 | tf_op jit(solution)/shard_map/ppermute | solution.py:354
  10.2 8.8 %collective-permute-start.1 = (s32[1,1024]{1,0:T(1,128)S(1)}, s32[1,1024]{1,0:T(1,128)S(1)}, u32[]{:S(2)}, u32[]{:S(2)}) collective-permute-start(s32[1,1024]{1,0:T(1,128)S(1)} %compare_select_fusion), channel_id=1, source_target_pairs={{0,0},{1,1},{2,2},{3,3},{4,4},{5,5},{6,6},{7,7},{8,8},{9,9},{10,10... | collective-permute-start | bytes 12296 | tf_op jit(solution)/shard_map/ppermute | solution.py:351
  10.9 13.0 %collective-permute-start.5 = (bf16[256,256]{1,0:T(8,128)(2,1)S(1)}, bf16[256,256]{1,0:T(8,128)(2,1)S(1)}, u32[]{:S(2)}, u32[]{:S(2)}) collective-permute-start(bf16[256,256]{1,0:T(8,128)(2,1)S(1)} %collective-permute-done.2.refs_1_), channel_id=1, source_target_pairs={{0,16},{16,32},{32,48},{48,0},{64,80},{80,96},{96,112},{112,64},{1... | collective-permute-start | bytes 393224 | tf_op jit(solution)/shard_map/ppermute | solution.py:354
  15.9 8.0 %collective-permute-start.6 = (bf16[256,256]{1,0:T(8,128)(2,1)S(1)}, bf16[256,256]{1,0:T(8,128)(2,1)S(1)}, u32[]{:S(2)}, u32[]{:S(2)}) collective-permute-start(bf16[256,256]{1,0:T(8,128)(2,1)S(1)} %collective-permute-done.2.refs_1_), channel_id=1, source_target_pairs={{0,48},{16,0},{32,16},{48,32},{64,112},{80,64},{96,80},{112,96},{1... | collective-permute-start | bytes 393224 | tf_op jit(solution)/shard_map/ppermute | solution.py:354
  17.8 6.3 %collective-permute-start.7 = (bf16[256,256]{1,0:T(8,128)(2,1)S(1)}, bf16[256,256]{1,0:T(8,128)(2,1)S(1)}, u32[]{:S(2)}, u32[]{:S(2)}) collective-permute-start(bf16[256,256]{1,0:T(8,128)(2,1)S(1)} %collective-permute-done.2.refs_1_), channel_id=1, source_target_pairs={{0,32},{16,48},{32,0},{48,16},{64,96},{80,112},{96,64},{112,80},{1... | collective-permute-start | bytes 393224 | tf_op jit(solution)/shard_map/ppermute | solution.py:354
  19.0 6.9 %copy-start.1 = (bf16[256,256]{1,0:T(8,128)(2,1)S(1)}, bf16[256,256]{1,0:T(8,128)(2,1)}, u32[]{:S(2)}) copy-start(bf16[256,256]{1,0:T(8,128)(2,1)} %constant.59.clone.refs_3_) | copy-start | bytes 393220
  25.2 6.6 %collective-permute-start.9 = (bf16[256,1024]{1,0:T(8,128)(2,1)S(1)}, bf16[256,1024]{1,0:T(8,128)(2,1)S(1)}, u32[]{:S(2)}, u32[]{:S(2)}) collective-permute-start(bf16[256,1024]{1,0:T(8,128)(2,1)S(1)} %pick.1), channel_id=1, source_target_pairs={{0,0},{1,1},{2,2},{3,3},{4,4},{5,5},{6,6},{7,7},{8,8},{9,9},{10,10... | collective-permute-start | bytes 1572872 | tf_op jit(solution)/shard_map/ppermute | solution.py:351
  25.9 5.9 %copy-start = (bf16[4096,256]{1,0:T(8,128)(2,1)S(1)}, bf16[4096,256]{1,0:T(8,128)(2,1)}, u32[]{:S(2)}) copy-start(bf16[4096,256]{1,0:T(8,128)(2,1)} %constant.60.clone.route_ref) | copy-start | bytes 6291460
  30.9 7.7 %collective-permute-start.8 = (bf16[1024,256]{1,0:T(8,128)(2,1)S(1)}, bf16[1024,256]{1,0:T(8,128)(2,1)S(1)}, u32[]{:S(2)}, u32[]{:S(2)}) collective-permute-start(bf16[1024,256]{1,0:T(8,128)(2,1)S(1)} %forward.1), channel_id=1, source_target_pairs={{0,0},{1,1},{2,2},{3,3},{4,4},{5,5},{6,6},{7,7},{8,8},{9,9},{10,10... | collective-permute-start | bytes 1572872 | tf_op jit(solution)/shard_map/ppermute | solution.py:351
  40.9 21.6 %copy-start.3 = (f32[4,16384]{1,0:T(4,128)S(1)}, f32[4,16384]{1,0:T(4,128)}, u32[]{:S(2)}) copy-start(f32[4,16384]{1,0:T(4,128)} %param.14) | copy-start | bytes 786436
  40.9 21.6 %copy-start.5 = (f32[4,16384]{1,0:T(4,128)S(1)}, f32[4,16384]{1,0:T(4,128)}, u32[]{:S(2)}) copy-start(f32[4,16384]{1,0:T(4,128)} %param.16) | copy-start | bytes 786436
  40.9 36.9 %all-to-all-start = ((bf16[8,256,256]{2,1,0:T(8,128)(2,1)}), bf16[8,256,256]{2,1,0:T(8,128)(2,1)S(1)}, u32[]{:S(2)}, u32[]{:S(2)}) async-start(bf16[8,256,256]{2,1,0:T(8,128)(2,1)} %bitcast.7), calls=%async_computation | async-start | bytes 2097152 | tf_op jit(solution)/shard_map/all_to_all | solution.py:377
  79.1 16.4 %all-to-all-start.1 = ((f32[128,3,128]{2,1,0:T(4,128)}), f32[128,3,128]{2,1,0:T(4,128)S(1)}, u32[]{:S(2)}, u32[]{:S(2)}) async-start(f32[128,3,128]{2,1,0:T(4,128)} %get-tuple-element.18), calls=%async_computation.1 | async-start | bytes 524288 | tf_op jit(solution)/shard_map/all_to_all | solution.py:386

commit v8 on v7

--- a/solution.py
+++ b/solution.py
@@ -15,6 +15,7 @@
 HALF = PAIRS // 2
 SIZE = PAIRS * GROUP
 WIDTH = 1024
+COPIES = 8
 BOTH = ("row", "col")
 NT = (((1,), (1,)), ((), ()))
 NN = (((1,), (0,)), ((), ()))
@@ -48,53 +49,57 @@
     return jnp.where(lax.broadcasted_iota(jnp.int32, index.shape, 1) < count, index, -1)
 
 
-def early_kernel(base_ref, count_ref, far_ref, own_ref, *refs):
-    pieces, (tile_ref, picked_ref, x_ref, far_order_ref, held_ref, sem) = refs[:-6], refs[-6:]
-    copy = pltpu.make_async_copy(tile_ref, held_ref, sem)
-    copy.start()
-    far_order_ref[...] = turned_slots(far_ref[...])
-    picked_ref[...] = gathered(base_ref, far_ref[...], pieces).astype(BF16)
+def early_kernel(base_ref, count_ref, own_ref, *refs):
+    pieces, (tile_ref, x_ref, held_ref, sems) = refs[:-4], refs[-4:]
+    size = held_ref.shape[0] // COPIES
+    copies = []
+    for n in range(COPIES):
+        at = pl.ds(n * size, size)
+        copies.append(pltpu.make_async_copy(tile_ref.at[at], held_ref.at[at], sems.at[n]))
+        copies[-1].start()
     own_order = turned_slots(masked(own_ref[...], count_ref[0]))
     x_ref[...] = gathered(base_ref, own_order, pieces).astype(BF16)
-    copy.wait()
-
-
-def early_pick(bases, used, far_index, own_index, pieces, tile):
-    whole = pl.BlockSpec(memory_space=pltpu.VMEM)
-    shape = jax.ShapeDtypeStruct((pieces[0].shape[0], far_index.shape[1]), BF16)
+    for copy in copies:
+        copy.wait()
+
+
+def early_pick(bases, used, own_index, pieces, tile):
+    whole = pl.BlockSpec(memory_space=pltpu.VMEM)
     return pl.pallas_call(
         early_kernel,
         out_shape=(
-            shape,
-            shape,
-            jax.ShapeDtypeStruct(far_index.shape, far_index.dtype),
-            jax.ShapeDtypeStruct(tile.shape, tile.dtype),
+            jax.ShapeDtypeStruct((pieces[0].shape[0], own_index.shape[1]), BF16),
+            jax.ShapeDtypeStruct((tile.shape[0] // 2, tile.shape[1]), tile.dtype),
         ),
         in_specs=[pl.BlockSpec(memory_space=pltpu.SMEM)] * 2
-        + [whole] * (2 + len(pieces))
+        + [whole] * (1 + len(pieces))
         + [pl.BlockSpec(memory_space=pl.ANY)],
-        out_specs=(whole,) * 4,
-        scratch_shapes=[pltpu.SemaphoreType.DMA],
+        out_specs=(whole,) * 2,
+        scratch_shapes=[pltpu.SemaphoreType.DMA((COPIES,))],
         compiler_params=params(42),
         name="early_pick",
-    )(bases, used, far_index, own_index, *pieces, tile)
-
-
-def pick_kernel(base_ref, index_ref, before_ref, *refs):
-    total = gathered(base_ref, index_ref[...], refs[:-1])
-    refs[-1][...] = (before_ref[...].astype(F32) + total).astype(BF16)
-
-
-def pick(bases, index, before, pieces):
+    )(bases, used, own_index, *pieces, tile)
+
+
+def pick_kernel(base_ref, index_ref, *refs):
+    pieces, (out_ref, order_ref) = refs[:-2], refs[-2:]
+    order_ref[...] = turned_slots(index_ref[...])
+    out_ref[...] = gathered(base_ref, index_ref[...], pieces).astype(BF16)
+
+
+def pick(bases, index, pieces):
     whole = pl.BlockSpec(memory_space=pltpu.VMEM)
     return pl.pallas_call(
         pick_kernel,
-        out_shape=jax.ShapeDtypeStruct(before.shape, BF16),
-        in_specs=[pl.BlockSpec(memory_space=pltpu.SMEM)] + [whole] * (2 + len(pieces)),
-        out_specs=whole,
+        out_shape=(
+            jax.ShapeDtypeStruct((pieces[0].shape[0], index.shape[1]), BF16),
+            jax.ShapeDtypeStruct(index.shape, index.dtype),
+        ),
+        in_specs=[pl.BlockSpec(memory_space=pltpu.SMEM)] + [whole] * (1 + len(pieces)),
+        out_specs=(whole,) * 2,
         compiler_params=params(16),
         name="pick",
-    )(bases, index, before, *pieces)
+    )(bases, index, *pieces)
 
 
 def order_matrix(vecs):
@@ -128,7 +133,10 @@
 
 
 def forward_kernel(vecs, base_ref, count_ref, index_ref, before_ref, *refs):
-    pieces, (order_ref, tile_ref, out_ref, x_ref, packed_ref) = refs[:-5], refs[-5:]
+    pieces, (order_ref, half_ref, tile_ref, out_ref, rest_ref, x_ref, packed_ref, sem) = refs[:-8], refs[-8:]
+    size = rest_ref.shape[0]
+    copy = pltpu.make_async_copy(tile_ref.at[pl.ds(size, size)], rest_ref, sem)
+    copy.start()
     own_order = turned_slots(masked(index_ref[...], count_ref[0]))
     x_ref[...] = (before_ref[...].astype(F32) + gathered(base_ref, own_order, pieces)).T
     lane = lax.broadcasted_iota(jnp.int32, (GROUP, LANES), 1)
@@ -136,8 +144,9 @@
     first = lane < BLOCK
     masks = [as_ones((lane + row + 1) % GROUP == n) for n in range(GROUP)]
 
-    def step(g, _):
-        at = pl.ds(pl.multiple_of(g * GROUP, GROUP), GROUP)
+    def step(held_ref, base, g, _):
+        at = pl.ds(pl.multiple_of(base + g * GROUP, GROUP), GROUP)
+        here = pl.ds(pl.multiple_of(g * GROUP, GROUP), GROUP)
         rows = []
         for p in range(vecs // 2):
             both = x_ref[at, p * LANES : (p + 1) * LANES]
@@ -151,7 +160,7 @@
         left = jnp.concatenate(rows, 0).astype(BF16)
         packed = [[], []]
         for half in range(2):
-            out = dot(left, stacked(tile_ref, at, half), NT).astype(BF16)
+            out = dot(left, stacked(held_ref, here, half), NT).astype(BF16)
             for s in range(2 * vecs):
                 shift = half * 2 * vecs + s
                 for v in range(2):
@@ -163,28 +172,36 @@
             packed_ref[at, v * LANES : (v + 1) * LANES] = part.astype(BF16)
         return 0
 
-    lax.fori_loop(0, x_ref.shape[0] // GROUP, step, 0, unroll=32)
+    lax.fori_loop(0, size // GROUP, functools.partial(step, half_ref, 0), 0, unroll=32)
+    copy.wait()
+    lax.fori_loop(0, size // GROUP, functools.partial(step, rest_ref, size), 0, unroll=32)
     out_ref[...] = dot(packed_ref[...], order_ref[...], NT).astype(BF16)
 
 
-def forward(vecs, bases, used, index, before, pieces, order, tile):
+def forward(vecs, bases, used, index, before, pieces, order, half, tile):
     slots, wide = tile.shape[0], vecs * BLOCK
     whole = pl.BlockSpec(memory_space=pltpu.VMEM)
     return pl.pallas_call(
         functools.partial(forward_kernel, vecs),
-        out_shape=jax.ShapeDtypeStruct((slots, wide), BF16),
-        in_specs=[pl.BlockSpec(memory_space=pltpu.SMEM)] * 2 + [whole] * (len(pieces) + 4),
-        out_specs=whole,
+        out_shape=(
+            jax.ShapeDtypeStruct((slots, wide), BF16),
+            jax.ShapeDtypeStruct((slots - half.shape[0], tile.shape[1]), tile.dtype),
+        ),
+        in_specs=[pl.BlockSpec(memory_space=pltpu.SMEM)] * 2
+        + [whole] * (len(pieces) + 4)
+        + [pl.BlockSpec(memory_space=pl.ANY)],
+        out_specs=(whole,) * 2,
         scratch_shapes=[
             pltpu.VMEM((slots, wide), F32),
             pltpu.VMEM((slots, wide), BF16),
+            pltpu.SemaphoreType.DMA,
         ],
-        compiler_params=params(20),
+        compiler_params=params(42),
         name="forward",
-    )(bases, used, index, before, *pieces, order, tile)
-
-
-def backward_kernel(vecs, y_ref, route_ref, tile_ref, out_ref, wide_ref):
+    )(bases, used, index, before, *pieces, order, half, tile)
+
+
+def backward_kernel(vecs, y_ref, route_ref, half_ref, rest_ref, out_ref, wide_ref):
     shape = (out_ref.shape[0], SIZE)
     own = (
         lax.broadcasted_iota(jnp.int32, shape, 1) % GROUP == lax.broadcasted_iota(jnp.int32, shape, 0) % GROUP
@@ -196,14 +213,15 @@
     first = lax.broadcasted_iota(jnp.int32, (GROUP, LANES), 1) < BLOCK
     span = HALF * GROUP
 
-    def step(g, _):
-        at = pl.ds(pl.multiple_of(g * GROUP, GROUP), GROUP)
+    def step(held_ref, base, g, _):
+        at = pl.ds(pl.multiple_of(base + g * GROUP, GROUP), GROUP)
+        here = pl.ds(pl.multiple_of(g * GROUP, GROUP), GROUP)
         out = None
         for half in range(2):
             left = [
                 wide_ref[at, s * SIZE + half * span : s * SIZE + (half + 1) * span] for s in range(2 * vecs)
             ]
-            part = dot(jnp.concatenate(left, 0), stacked(tile_ref, at, half))
+            part = dot(jnp.concatenate(left, 0), stacked(held_ref, here, half))
             out = part if out is None else out + part
         sums = []
         for k in range(vecs):
@@ -214,23 +232,25 @@
             out_ref[at, p * LANES : (p + 1) * LANES] = jnp.where(first, sums[2 * p], sums[2 * p + 1]).astype(BF16)
         return 0
 
-    lax.fori_loop(0, out_ref.shape[0] // GROUP, step, 0, unroll=32)
-
-
-def backward(vecs, far, route, tile):
+    size = half_ref.shape[0]
+    for n, held_ref in enumerate((half_ref, rest_ref)):
+        lax.fori_loop(0, size // GROUP, functools.partial(step, held_ref, n * size), 0, unroll=32)
+
+
+def backward(vecs, far, route, half, rest):
     wide, slots = far.shape
     whole = pl.BlockSpec(memory_space=pltpu.VMEM)
     return pl.pallas_call(
         functools.partial(backward_kernel, vecs),
         out_shape=jax.ShapeDtypeStruct((slots, wide), BF16),
-        in_specs=[whole] * 3,
+        in_specs=[whole] * 4,
         out_specs=whole,
         scratch_shapes=[
             pltpu.VMEM((slots, 2 * vecs * SIZE), BF16),
         ],
         compiler_params=params(20),
         name="backward",
-    )(far, route, tile)
+    )(far, route, half, rest)
 
 
 def spread_kernel(count_ref, index_ref, part_ref, *refs):
@@ -255,6 +275,31 @@
         compiler_params=params(20),
         name="spread",
     )(used, index, part, *before)
+
+
+def early_kernel_gram(vecs, *refs):
+    vectors, (out_ref, held_ref) = refs[:-2], refs[-2:]
+    for n, vector in enumerate(vectors):
+        held_ref[n * vecs : (n + 1) * vecs, :] = vector[...]
+    left, right = held_ref[: 3 * vecs, :], held_ref[...]
+    gram = lax.dot_general(left, right, NT, precision=lax.Precision.HIGHEST, preferred_element_type=F32)
+    rows = [gram[m : m + 1, m // vecs * vecs :] for m in range(3 * vecs)]
+    for line, some in enumerate((rows[:vecs], rows[vecs:])):
+        blank = jnp.zeros((1, LANES - sum(row.shape[1] for row in some)), F32)
+        out_ref[line : line + 1, :] = jnp.concatenate(some + [blank], 1)
+
+
+def early_gram(vecs, *vectors):
+    whole = pl.BlockSpec(memory_space=pltpu.VMEM)
+    return pl.pallas_call(
+        functools.partial(early_kernel_gram, vecs),
+        out_shape=jax.ShapeDtypeStruct((2, LANES), F32),
+        in_specs=[whole] * len(vectors),
+        out_specs=whole,
+        scratch_shapes=[pltpu.VMEM((vecs * len(vectors), vectors[0].shape[1]), F32)],
+        compiler_params=params(16),
+        name="early_gram",
+    )(*vectors)
 
 
 def total_kernel(vecs, part_ref, vector_ref, early_ref, sum_ref, gram_ref):
@@ -274,11 +319,13 @@
     row = lax.broadcasted_iota(jnp.int32, shape, 0)
     lane = lax.broadcasted_iota(jnp.int32, shape, 1)
     swap, q, p = row % 2, row // 2 % (vecs // 2), row // vecs
-    even = (2 * p + swap) * vecs + 2 * q
-    odd = (2 * p + 1 - swap) * vecs + 2 * q + 1
+    first = 5 * vecs * vecs
+    even = first + (2 * p + swap) * vecs + 2 * q
+    odd = first + (2 * p + 1 - swap) * vecs + 2 * q + 1
     late = jnp.where(lane == even, lines[:, :BLOCK].sum(1, keepdims=True), 0.0)
     late += jnp.where(lane == odd, lines[:, BLOCK:].sum(1, keepdims=True), 0.0)
-    packed = jnp.concatenate([early_ref[...], late.sum(0, keepdims=True)], 0)
+    late = late.sum(0, keepdims=True)
+    packed = early_ref[...] + jnp.concatenate([late, jnp.zeros_like(late)], 0)
     gram_ref[...] = jnp.broadcast_to(packed[None], gram_ref.shape)
 
 
@@ -288,7 +335,7 @@
         functools.partial(total_kernel, vecs),
         out_shape=(
             jax.ShapeDtypeStruct(parts.shape[1:], F32),
-            jax.ShapeDtypeStruct((peers, early.shape[0] + 1, LANES), F32),
+            jax.ShapeDtypeStruct((peers, *early.shape), F32),
         ),
         in_specs=[whole] * 3,
         out_specs=(whole, whole),
@@ -302,20 +349,35 @@
     for n in range(1, gram_ref.shape[0]):
         packed += gram_ref[n]
     packed = packed * scale
-    wide, half = 5 * vecs, 3 * vecs // 2
     lane = lax.broadcasted_iota(jnp.int32, (1, LANES), 1)
-
-    def shifted(line, by):
-        by = by % LANES
-        return pltpu.roll(packed[line : line + 1], by, 1) if by else packed[line : line + 1]
+    late = 5 * vecs * vecs
+
+    def assembled(runs):
+        out = jnp.zeros((1, LANES), F32)
+        for line, source, to, count in runs:
+            by = (to - source) % LANES
+            moved = packed[line : line + 1]
+            moved = pltpu.roll(moved, by, 1) if by else moved
+            out = jnp.where((lane >= to) & (lane < to + count), moved, out)
+        return out[:, : 3 * vecs]
+
+    def place(block, i, column):
+        if block == 0:
+            return 0, (5 * i + column) * vecs
+        if block == 1:
+            return 1, (4 * i + column - 1) * vecs
+        return 1, (4 * vecs + 3 * i + column - 2) * vecs
 
     for m in range(3 * vecs):
-        line, at = m // half, m % half * wide
-        b_ref[m : m + 1, :] = shifted(line, -at)[:, : 3 * vecs]
-        first, last = shifted(line, -at - 3 * vecs), shifted(line, -at - 2 * vecs)
-        middle = shifted(2, vecs - m * vecs)
-        mixed = jnp.where(lane < vecs, first, jnp.where(lane < 2 * vecs, middle, last))
-        a_ref[m : m + 1, :] = mixed[:, : 3 * vecs]
+        block, i = m // vecs, m % vecs
+        runs = [(*place(block, i, column), column * vecs, vecs) for column in range(block, 3)]
+        for column in range(block):
+            for j in range(vecs):
+                line, at = place(column, j, block)
+                runs.append((line, at + i, column * vecs + j, 1))
+        b_ref[m : m + 1, :] = assembled(runs)
+        images = [(*place(block, i, 3), 0, vecs), (0, late + m * vecs, vecs, vecs)]
+        a_ref[m : m + 1, :] = assembled(images + [(*place(block, i, 4), 2 * vecs, vecs)])
 
 
 def unpacked(vecs, gram, scale):
@@ -359,28 +421,26 @@
     across = within(own, 1, 0)
     pieces = [own, across] + [within(own, 0, n) for n in (1, 3, 2)]
     pieces += [within(across, 0, n) for n in (1, 3, 2)]
-    flips = jnp.array([0, 1, 0, 0, 0, 1, 1, 1], jnp.int32)
-    turns = jnp.array([0, 0, 1, 3, 2, 1, 3, 2], jnp.int32)
-    bases = width * ((row_pos // ring ^ flips) * ring + (row_pos % ring - turns) % ring)
+    order = jnp.arange(rows, dtype=jnp.int32)
+    flips = sum(1 << n for n in (1, 5, 6, 7)) >> order & 1
+    turns = sum(turn << 2 * n for n, turn in enumerate((0, 0, 1, 3, 2, 1, 3, 2))) >> 2 * order & 3
+    bases = width * ((row_pos // ring ^ flips) * ring + (row_pos % ring + ring - turns) % ring)
     far_index = along(lax.optimization_barrier((row_index, pieces[2]))[0], 1)
     near = 5
-    picked, x_slots, far_order, held = early_pick(
-        bases[:near], used, far_index, col_index, pieces[:near], tile
-    )
-    far = along(pick(bases[near:], far_index, picked, pieces[near:]), -1)
-    forth = forward(vecs, bases[near:], used, col_index, x_slots, pieces[near:], order_matrix(vecs), held)
+    x_slots, held = early_pick(bases[:near], used, col_index, pieces[:near], tile)
+    picked, far_order = pick(bases, far_index, pieces)
+    far = along(picked, -1)
+    forth, rest = forward(vecs, bases[near:], used, col_index, x_slots, pieces[near:], order_matrix(vecs), held, tile)
     forth = along(forth, 1)
-    back = backward(vecs, far, route_matrix(vecs), held)
+    back = backward(vecs, far, route_matrix(vecs), held, rest)
     back = spread(used, col_index, back, rows * width, F32)
     every = jnp.full((1,), slots, jnp.int32)
     parts = spread(every, far_order, forth, rows * width, BF16, back).reshape(rows, width, vecs * BLOCK)
-    parts = lax.all_to_all(parts, "row", 0, 0, tiled=True)
     vectors = jnp.concatenate([x_vec, residue, p_vec], 0)
-    known = jnp.concatenate([vectors, hx_vec, hp_vec], 0)
-    early = jnp.dot(vectors, known.T, precision=lax.Precision.HIGHEST, preferred_element_type=F32)
-    early = early.reshape(2, -1)
-    early = jnp.pad(early, ((0, 0), (0, LANES - early.shape[1])))
+    tied = lax.optimization_barrier((x_vec, residue, p_vec, hx_vec, hp_vec, parts))
+    early = early_gram(vecs, *tied[:5])
     blocked = vectors.reshape(-1, width, BLOCK).transpose(1, 0, 2).reshape(width, -1)
+    parts = lax.all_to_all(tied[5], "row", 0, 0, tiled=True)
     total, gram = totalled(vecs, parts, blocked, early, rows * cols)
     hw_vec = total.reshape(width, vecs, BLOCK).transpose(1, 0, 2).reshape(vecs, piece_len)
     gram = lax.all_to_all(gram, BOTH, 0, 0, tiled=True)

time: 96.7 us -> 95.3 us (0.986)
  matrix products: 2.78 us -> 0 us
  waiting for transfers between devices: 15.3 us -> 17.4 us
  starting transfers between devices: 44.1 us -> 42.1 us
  Pallas kernels: 22.3 us -> 23.3 us
    ppermute x7, starting transfers between devices: 15.2 us -> 10.4 us  [within(): lax.ppermute(block, 'row', [(i, (i // ring ^ flip) * ring + (i % ring + t...]
    concatenate x1 -> x0, local copies, waits for them, and re-layouts: 3.47 us -> none  [body(): known = jnp.concatenate([vectors, hx_vec, hp_vec], 0)]
    dot_general x1 -> x0, matrix products: 2.78 us -> none  [body(): jnp.dot(vectors, known.T, precision=lax.Precision.HIGHEST, preferred_elem...]
    transpose x1, local copies, waits for them, and re-layouts: 0.45 us -> 2.75 us  [body(): vectors.reshape(-1, width, BLOCK).transpose(1, 0, 2).reshape(width, -1)]
    all_to_all x1, waiting for transfers between devices: 5.21 us -> 7.04 us  [body(): parts = lax.all_to_all(tied[5], 'row', 0, 0, tiled=True)]
    all_to_all x1, starting transfers between devices: 21.6 us -> 23.3 us  [body(): parts = lax.all_to_all(tied[5], 'row', 0, 0, tiled=True)]
    ppermute x7, waiting for transfers between devices: 0.14 us -> 1.6 us  [within(): lax.ppermute(block, 'row', [(i, (i // ring ^ flip) * ring + (i % ring + t...]
    pallas_call x3 -> x4, Pallas kernels: 11.1 us -> 12.3 us  [the longest x1 5.12 us: forward(): pl.pallas_call(functools.partial(forward_kernel, vecs), out_shape=(jax.Sh...]
  transfers between devices with their start and end apart: 12 -> 12, of which waited for: 3 -> 4; matrix products, arithmetic and copies ran while one was open for 12% -> 9% of each run, Pallas kernels for 17% -> 18%
where the time goes in v8:
time: 95.3 us; the launch traced here: 94.9 us
  starting transfers between devices  42.1 us (44%)
  Pallas kernels  23.3 us (24%)
  waiting for transfers between devices  17.4 us (18%)
  local copies, waits for them, and re-layouts  8.38 us (9%)
  other arithmetic  2.12 us (2%)
  between operations  1.55 us (2%)
    all_to_all x1, starting transfers between devices, body(): parts = lax.all_to_all(tied[5], 'row', 0, 0, tiled=True)  23.3 us
    ppermute x7, starting transfers between devices, within(): lax.ppermute(block, 'row', [(i, (i // ring ^ flip) * ring + (i % ring + t...  10.4 us
    all_to_all x1, waiting for transfers between devices, body(): gram = lax.all_to_all(gram, BOTH, 0, 0, tiled=True)  8.71 us
    all_to_all x1, waiting for transfers between devices, body(): parts = lax.all_to_all(tied[5], 'row', 0, 0, tiled=True)  7.04 us
    all_to_all x1, starting transfers between devices, body(): gram = lax.all_to_all(gram, BOTH, 0, 0, tiled=True)  6.21 us
    pallas_call x1, Pallas kernels, backward(): pl.pallas_call(functools.partial(backward_kernel, vecs), out_shape=jax.Sh...  5.15 us
    pallas_call x1, Pallas kernels, forward(): pl.pallas_call(functools.partial(forward_kernel, vecs), out_shape=(jax.Sh...  5.12 us
    pallas_call x2, Pallas kernels, spread(): pl.pallas_call(spread_kernel, grid=(blocks // WIDTH,), out_shape=jax.Shap...  3.72 us
  transfers between devices with their start and end apart: 12, of which 4 were waited for; matrix products, arithmetic and copies ran while one was open for 9% of the time, Pallas kernels for 18%

profile of v8, /device:TPU:1, one launch (start us, length us, event | category | flops | bytes accessed | tf_op | source)
XLA Modules:
  0.0 94.9 jit_solution(4852419670534255385)
XLA Ops:
  0.6 1.2 %fusion.3 = (bf16[4,16384]{1,0:T(4,128)(2,1)S(1)}, f32[4,16384]{1,0:T(4,128)S(1)}) fusion(f32[16384]{0:T(1024)} %param.17, f32[4,16384]{1,0:T(4,128)} %refs_3_.1, f32[4,16384]{1,0:T(4,128)} %refs_0_, f32[4]{0:T(128)} %param.16), kind=kLoop, calls=%fused_computation.9 | loop fusion | flops 262144 | bytes 983056 | tf_op jit(solution)/shard_map/convert_element_type | solution.py:420
  2.3 2.1 %collective-permute-start.2 = (bf16[256,256]{1,0:T(8,128)(2,1)S(1)}, bf16[256,256]{1,0:T(8,128)(2,1)S(1)}, u32[]{:S(2)}, u32[]{:S(2)}) collective-permute-start(bf16[256,256]{1,0:T(8,128)(2,1)S(1)} %bitcast.19), channel_id=1, source_target_pairs={{0,64},{16,80},{32,96},{48,112},{64,0},{80,16},{96,32},{112,48},{1... | collective-permute-start | bytes 393224 | tf_op jit(solution)/shard_map/ppermute | solution.py:416
  4.4 1.6 %collective-permute-start = (bf16[256,256]{1,0:T(8,128)(2,1)S(1)}, bf16[256,256]{1,0:T(8,128)(2,1)S(1)}, u32[]{:S(2)}, u32[]{:S(2)}) collective-permute-start(bf16[256,256]{1,0:T(8,128)(2,1)S(1)} %bitcast.20), channel_id=1, source_target_pairs={{0,16},{16,32},{32,48},{48,0},{64,80},{80,96},{96,112},{112,64},{1... | collective-permute-start | bytes 393224 | tf_op jit(solution)/shard_map/ppermute | solution.py:416
  6.0 2.1 %collective-permute-start.3 = (bf16[256,256]{1,0:T(8,128)(2,1)S(1)}, bf16[256,256]{1,0:T(8,128)(2,1)S(1)}, u32[]{:S(2)}, u32[]{:S(2)}) collective-permute-start(bf16[256,256]{1,0:T(8,128)(2,1)S(1)} %bitcast.21), channel_id=1, source_target_pairs={{0,48},{16,0},{32,16},{48,32},{64,112},{80,64},{96,80},{112,96},{1... | collective-permute-start | bytes 393224 | tf_op jit(solution)/shard_map/ppermute | solution.py:416
  8.2 1.3 %collective-permute-start.4 = (bf16[256,256]{1,0:T(8,128)(2,1)S(1)}, bf16[256,256]{1,0:T(8,128)(2,1)S(1)}, u32[]{:S(2)}, u32[]{:S(2)}) collective-permute-start(bf16[256,256]{1,0:T(8,128)(2,1)S(1)} %bitcast.22), channel_id=1, source_target_pairs={{0,32},{16,48},{32,0},{48,16},{64,96},{80,112},{96,64},{112,80},{1... | collective-permute-start | bytes 393224 | tf_op jit(solution)/shard_map/ppermute | solution.py:416
  10.1 0.8 collective-permute-start.5
  10.9 1.9 %collective-permute-start.6 = (bf16[256,256]{1,0:T(8,128)(2,1)S(1)}, bf16[256,256]{1,0:T(8,128)(2,1)S(1)}, u32[]{:S(2)}, u32[]{:S(2)}) collective-permute-start(bf16[256,256]{1,0:T(8,128)(2,1)S(1)} %collective-permute-done.2.refs_1_), channel_id=1, source_target_pairs={{0,48},{16,0},{32,16},{48,32},{64,112},{80,64},{96,80},{112,96},{1... | collective-permute-start | bytes 393224 | tf_op jit(solution)/shard_map/ppermute | solution.py:416
  12.9 0.5 collective-permute-start.7
  13.3 0.7 compare_select_fusion
  14.0 0.7 collective-permute-start.1
  14.8 0.3 collective-permute-done.4.refs_4_
  15.1 0.7 copy-done.6
  15.8 3.6 %early_pick.1 = (bf16[256,1024]{1,0:T(8,128)(2,1)S(1)}, bf16[512,4096]{1,0:T(8,128)(2,1)S(1)}) custom-call(s32[5]{0:T(128)S(1)} %bitcast.28, s32[1]{0:T(128)} %bitcast.16.count_ref, s32[1,1024]{1,0:T(1,128)S(1)} %bitcast.25, bf16[256,256]{1,0:T(8,128)(2,1)S(1)} %bitcast.23, bf16[256,256]{1,0:T(8,128)(2,1)S(1)} %collective-permute-done.2.refs_1_, ...), custom_call_target="tpu_custom_call" | custom-call | tf_op jit(solution)/shard_map/early_pick/pallas_call | solution.py:68
  19.4 1.3 %collective-permute-done.7.refs_7_.refs_2_ = bf16[256,256]{1,0:T(8,128)(2,1)S(1)} collective-permute-done((bf16[256,256]{1,0:T(8,128)(2,1)S(1)}, bf16[256,256]{1,0:T(8,128)(2,1)S(1)}, u32[]{:S(2)}, u32[]{:S(2)}) %collective-permute-start.7) | collective-permute-done | bytes 131104 | tf_op jit(solution)/shard_map/ppermute | solution.py:416
  20.7 1.8 %pick.1 = (bf16[256,1024]{1,0:T(8,128)(2,1)S(1)}, s32[1,1024]{1,0:T(1,128)S(1)}) custom-call(s32[8]{0:T(128)S(1)} %fusion.2.base_ref, s32[1,1024]{1,0:T(1,128)S(1)} %collective-permute-done.1.index_ref, bf16[256,256]{1,0:T(8,128)(2,1)S(1)} %bitcast.24, bf16[256,256]{1,0:T(8,128)(2,1)S(1)} %collective-permute-done.2.refs_1_, ...), custom_call_target="tpu_custom_call" | custom-call | tf_op jit(solution)/shard_map/pick/pallas_call | solution.py:92
  22.5 0.7 collective-permute-start.9
  23.3 5.1 %forward.1 = (bf16[1024,256]{1,0:T(8,128)(2,1)S(1)}, bf16[512,4096]{1,0:T(8,128)(2,1)S(1)}) custom-call(s32[3]{0:T(128)S(1)} %slice.6.base_ref, s32[1]{0:T(128)} %bitcast.17.count_ref, s32[1,1024]{1,0:T(1,128)S(1)} %bitcast.26, bf16[256,1024]{1,0:T(8,128)(2,1)S(1)} %get-tuple-element.22.before_ref, ...), custom_call_target="tpu_custom_call" | custom-call | tf_op jit(solution)/shard_map/forward/pallas_call | solution.py:184
  28.4 0.9 collective-permute-start.8
  29.3 5.1 %backward.1.part_ref = bf16[1024,256]{1,0:T(8,128)(2,1)S(1)} custom-call(bf16[256,1024]{1,0:T(8,128)(2,1)S(1)} %collective-permute-done.9.y_ref, bf16[4096,256]{1,0:T(8,128)(2,1)S(1)} %copy-done.1, bf16[512,4096]{1,0:T(8,128)(2,1)S(1)} %get-tuple-element.23.refs_4_.half_ref, bf16[512,4096]{1,0:T(8,128)(2,1)S(1)} %get-tuple-element.26.rest_ref), custom_call_target="tpu_custom_call" | custom-call | tf_op jit(solution)/shard_map/backward/pallas_call | solution.py:243
  34.5 1.5 %spread.2.refs_0_ = f32[2048,256]{1,0:T(8,128)S(1)} custom-call(s32[1]{0:T(128)} %bitcast.18.count_ref, s32[1,1024]{1,0:T(1,128)S(1)} %bitcast.27, bf16[1024,256]{1,0:T(8,128)(2,1)S(1)} %backward.1.part_ref), custom_call_target="tpu_custom_call" | custom-call | tf_op jit(solution)/shard_map/spread/pallas_call | solution.py:269
  35.9 2.3 %spread.3 = bf16[2048,256]{1,0:T(8,128)(2,1)} custom-call(s32[1]{0:T(128)} %constant.45.clone.1.count_ref, s32[1,1024]{1,0:T(1,128)S(1)} %get-tuple-element.21.index_ref, bf16[1024,256]{1,0:T(8,128)(2,1)S(1)} %collective-permute-done.8.part_ref, f32[2048,256]{1,0:T(8,128)S(1)} %spread.2.refs_0_), custom_call_target="tpu_custom_call" | custom-call | tf_op jit(solution)/shard_map/spread/pallas_call | solution.py:269
  38.2 23.3 %all-to-all-start = ((bf16[8,256,256]{2,1,0:T(8,128)(2,1)}), bf16[8,256,256]{2,1,0:T(8,128)(2,1)S(1)}, u32[]{:S(2)}, u32[]{:S(2)}) async-start(bf16[8,256,256]{2,1,0:T(8,128)(2,1)} %bitcast.7), calls=%async_computation | async-start | bytes 2097152 | tf_op jit(solution)/shard_map/all_to_all | solution.py:443
  61.7 1.8 %reshape.53 = f32[12,256,64]{2,1,0:T(8,128)} reshape(f32[12,16384]{1,0:T(8,128)S(1)} %pad_maximum_fusion) | data formatting | bytes 1572864 | tf_op jit(solution)/shard_map/reshape | solution.py:442
  63.5 2.7 %copy.19 = f32[256,12,64]{0,2,1:T(8,128)} copy(f32[256,12,64]{2,0,1:T(8,128)} %bitcast.31) | data formatting | bytes 1572864 | tf_op jit(solution)/shard_map/transpose | solution.py:442
  66.3 1.4 %copy.20.vector_ref = f32[256,768]{1,0:T(8,128)S(1)} copy(f32[256,768]{0,1:T(8,128)} %bitcast.32) | data formatting | bytes 1572864 | tf_op jit(solution)/shard_map/reshape | solution.py:442
  67.7 1.8 %early_gram.1.early_ref = f32[2,128]{1,0:T(2,128)S(1)} custom-call(f32[4,16384]{1,0:T(4,128)S(1)} %copy-done, f32[4,16384]{1,0:T(4,128)S(1)} %get-tuple-element.29.refs_1_, f32[4,16384]{1,0:T(4,128)S(1)} %copy-done.3, f32[4,16384]{1,0:T(4,128)S(1)} %copy-done.2, f32[4,16384]{1,0:T(4,128)S(1)} %copy-done.4), custom_call_target="tpu_custom_call" | custom-call | tf_op jit(solution)/shard_map/early_gram/pallas_call | solution.py:294
  69.5 7.0 %all-to-all-done.part_ref = bf16[8,256,256]{2,1,0:T(8,128)(2,1)S(1)} async-done(((bf16[8,256,256]{2,1,0:T(8,128)(2,1)}), bf16[8,256,256]{2,1,0:T(8,128)(2,1)S(1)}, u32[]{:S(2)}, u32[]{:S(2)}) %all-to-all-start) | async-done | bytes 1048608 | tf_op jit(solution)/shard_map/all_to_all | solution.py:443
  76.6 1.2 %totalled.1 = (f32[256,256]{1,0:T(8,128)S(1)}, f32[128,2,128]{2,1,0:T(2,128)}) custom-call(bf16[8,256,256]{2,1,0:T(8,128)(2,1)S(1)} %all-to-all-done.part_ref, f32[256,768]{1,0:T(8,128)S(1)} %copy.20.vector_ref, f32[2,128]{1,0:T(2,128)S(1)} %early_gram.1.early_ref), custom_call_target="tpu_custom_call" | custom-call | tf_op jit(solution)/shard_map/totalled/pallas_call | solution.py:334
  77.8 6.2 %all-to-all-start.1 = ((f32[128,2,128]{2,1,0:T(2,128)}), f32[128,2,128]{2,1,0:T(2,128)S(1)}, u32[]{:S(2)}, u32[]{:S(2)}) async-start(f32[128,2,128]{2,1,0:T(2,128)} %get-tuple-element.34), calls=%async_computation.1 | async-start | bytes 262144 | tf_op jit(solution)/shard_map/all_to_all | solution.py:446
  84.3 0.9 reshape.56
  85.2 8.7 %all-to-all-done.1.gram_ref = f32[128,2,128]{2,1,0:T(2,128)S(1)} async-done(((f32[128,2,128]{2,1,0:T(2,128)}), f32[128,2,128]{2,1,0:T(2,128)S(1)}, u32[]{:S(2)}, u32[]{:S(2)}) %all-to-all-start.1) | async-done | bytes 131104 | tf_op jit(solution)/shard_map/all_to_all | solution.py:446
  94.0 0.9 unpacked.1
  (28 shorter events, 1.0 us)
Async XLA Ops:
  2.3 7.8 %collective-permute-start.2 = (bf16[256,256]{1,0:T(8,128)(2,1)S(1)}, bf16[256,256]{1,0:T(8,128)(2,1)S(1)}, u32[]{:S(2)}, u32[]{:S(2)}) collective-permute-start(bf16[256,256]{1,0:T(8,128)(2,1)S(1)} %bitcast.19), channel_id=1, source_target_pairs={{0,64},{16,80},{32,96},{48,112},{64,0},{80,16},{96,32},{112,48},{1... | collective-permute-start | bytes 393224 | tf_op jit(solution)/shard_map/ppermute | solution.py:416
  4.4 8.5 %collective-permute-start = (bf16[256,256]{1,0:T(8,128)(2,1)S(1)}, bf16[256,256]{1,0:T(8,128)(2,1)S(1)}, u32[]{:S(2)}, u32[]{:S(2)}) collective-permute-start(bf16[256,256]{1,0:T(8,128)(2,1)S(1)} %bitcast.20), channel_id=1, source_target_pairs={{0,16},{16,32},{32,48},{48,0},{64,80},{80,96},{96,112},{112,64},{1... | collective-permute-start | bytes 393224 | tf_op jit(solution)/shard_map/ppermute | solution.py:416
  6.0 8.0 %collective-permute-start.3 = (bf16[256,256]{1,0:T(8,128)(2,1)S(1)}, bf16[256,256]{1,0:T(8,128)(2,1)S(1)}, u32[]{:S(2)}, u32[]{:S(2)}) collective-permute-start(bf16[256,256]{1,0:T(8,128)(2,1)S(1)} %bitcast.21), channel_id=1, source_target_pairs={{0,48},{16,0},{32,16},{48,32},{64,112},{80,64},{96,80},{112,96},{1... | collective-permute-start | bytes 393224 | tf_op jit(solution)/shard_map/ppermute | solution.py:416
  8.2 6.9 %collective-permute-start.4 = (bf16[256,256]{1,0:T(8,128)(2,1)S(1)}, bf16[256,256]{1,0:T(8,128)(2,1)S(1)}, u32[]{:S(2)}, u32[]{:S(2)}) collective-permute-start(bf16[256,256]{1,0:T(8,128)(2,1)S(1)} %bitcast.22), channel_id=1, source_target_pairs={{0,32},{16,48},{32,0},{48,16},{64,96},{80,112},{96,64},{112,80},{1... | collective-permute-start | bytes 393224 | tf_op jit(solution)/shard_map/ppermute | solution.py:416
  10.1 9.3 %collective-permute-start.5 = (bf16[256,256]{1,0:T(8,128)(2,1)S(1)}, bf16[256,256]{1,0:T(8,128)(2,1)S(1)}, u32[]{:S(2)}, u32[]{:S(2)}) collective-permute-start(bf16[256,256]{1,0:T(8,128)(2,1)S(1)} %collective-permute-done.2.refs_1_), channel_id=1, source_target_pairs={{0,16},{16,32},{32,48},{48,0},{64,80},{80,96},{96,112},{112,64},{1... | collective-permute-start | bytes 393224 | tf_op jit(solution)/shard_map/ppermute | solution.py:416
  10.9 8.5 %collective-permute-start.6 = (bf16[256,256]{1,0:T(8,128)(2,1)S(1)}, bf16[256,256]{1,0:T(8,128)(2,1)S(1)}, u32[]{:S(2)}, u32[]{:S(2)}) collective-permute-start(bf16[256,256]{1,0:T(8,128)(2,1)S(1)} %collective-permute-done.2.refs_1_), channel_id=1, source_target_pairs={{0,48},{16,0},{32,16},{48,32},{64,112},{80,64},{96,80},{112,96},{1... | collective-permute-start | bytes 393224 | tf_op jit(solution)/shard_map/ppermute | solution.py:416
  12.9 7.8 %collective-permute-start.7 = (bf16[256,256]{1,0:T(8,128)(2,1)S(1)}, bf16[256,256]{1,0:T(8,128)(2,1)S(1)}, u32[]{:S(2)}, u32[]{:S(2)}) collective-permute-start(bf16[256,256]{1,0:T(8,128)(2,1)S(1)} %collective-permute-done.2.refs_1_), channel_id=1, source_target_pairs={{0,32},{16,48},{32,0},{48,16},{64,96},{80,112},{96,64},{112,80},{1... | collective-permute-start | bytes 393224 | tf_op jit(solution)/shard_map/ppermute | solution.py:416
  14.0 5.4 %collective-permute-start.1 = (s32[1,1024]{1,0:T(1,128)S(1)}, s32[1,1024]{1,0:T(1,128)S(1)}, u32[]{:S(2)}, u32[]{:S(2)}) collective-permute-start(s32[1,1024]{1,0:T(1,128)S(1)} %compare_select_fusion), channel_id=1, source_target_pairs={{0,0},{1,1},{2,2},{3,3},{4,4},{5,5},{6,6},{7,7},{8,8},{9,9},{10,10... | collective-permute-start | bytes 12296 | tf_op jit(solution)/shard_map/ppermute | solution.py:413
  15.1 0.7 copy-start.6
  15.8 7.5 %copy-start.5 = (bf16[256,256]{1,0:T(8,128)(2,1)S(1)}, bf16[256,256]{1,0:T(8,128)(2,1)}, u32[]{:S(2)}) copy-start(bf16[256,256]{1,0:T(8,128)(2,1)} %constant.57.clone.refs_3_) | copy-start | bytes 393220
  22.5 6.7 %collective-permute-start.9 = (bf16[256,1024]{1,0:T(8,128)(2,1)S(1)}, bf16[256,1024]{1,0:T(8,128)(2,1)S(1)}, u32[]{:S(2)}, u32[]{:S(2)}) collective-permute-start(bf16[256,1024]{1,0:T(8,128)(2,1)S(1)} %get-tuple-element.25), channel_id=1, source_target_pairs={{0,0},{1,1},{2,2},{3,3},{4,4},{5,5},{6,6},{7,7},{8,8},{9,9},{10,10... | collective-permute-start | bytes 1572872 | tf_op jit(solution)/shard_map/ppermute | solution.py:413
  23.2 6.0 %copy-start.1 = (bf16[4096,256]{1,0:T(8,128)(2,1)S(1)}, bf16[4096,256]{1,0:T(8,128)(2,1)}, u32[]{:S(2)}) copy-start(bf16[4096,256]{1,0:T(8,128)(2,1)} %constant.58.clone.route_ref) | copy-start | bytes 6291460
  28.4 7.5 %collective-permute-start.8 = (bf16[1024,256]{1,0:T(8,128)(2,1)S(1)}, bf16[1024,256]{1,0:T(8,128)(2,1)S(1)}, u32[]{:S(2)}, u32[]{:S(2)}) collective-permute-start(bf16[1024,256]{1,0:T(8,128)(2,1)S(1)} %get-tuple-element.24), channel_id=1, source_target_pairs={{0,0},{1,1},{2,2},{3,3},{4,4},{5,5},{6,6},{7,7},{8,8},{9,9},{10,10... | collective-permute-start | bytes 1572872 | tf_op jit(solution)/shard_map/ppermute | solution.py:413
  34.4 27.1 %copy-start = (f32[4,16384]{1,0:T(4,128)S(1)}, f32[4,16384]{1,0:T(4,128)}, u32[]{:S(2)}) copy-start(f32[4,16384]{1,0:T(4,128)} %refs_0_) | copy-start | bytes 786436
  34.4 27.1 %copy-start.3 = (f32[4,16384]{1,0:T(4,128)S(1)}, f32[4,16384]{1,0:T(4,128)}, u32[]{:S(2)}) copy-start(f32[4,16384]{1,0:T(4,128)} %refs_2_) | copy-start | bytes 786436
  38.2 38.4 %all-to-all-start = ((bf16[8,256,256]{2,1,0:T(8,128)(2,1)}), bf16[8,256,256]{2,1,0:T(8,128)(2,1)S(1)}, u32[]{:S(2)}, u32[]{:S(2)}) async-start(bf16[8,256,256]{2,1,0:T(8,128)(2,1)} %bitcast.7), calls=%async_computation | async-start | bytes 2097152 | tf_op jit(solution)/shard_map/all_to_all | solution.py:443
  61.5 6.2 %copy-start.2 = (f32[4,16384]{1,0:T(4,128)S(1)}, f32[4,16384]{1,0:T(4,128)}, u32[]{:S(2)}) copy-start(f32[4,16384]{1,0:T(4,128)} %refs_3_.1) | copy-start | bytes 786436
  61.5 6.2 %copy-start.4 = (f32[4,16384]{1,0:T(4,128)S(1)}, f32[4,16384]{1,0:T(4,128)}, u32[]{:S(2)}) copy-start(f32[4,16384]{1,0:T(4,128)} %refs_4_) | copy-start | bytes 786436
  77.8 16.2 %all-to-all-start.1 = ((f32[128,2,128]{2,1,0:T(2,128)}), f32[128,2,128]{2,1,0:T(2,128)S(1)}, u32[]{:S(2)}, u32[]{:S(2)}) async-start(f32[128,2,128]{2,1,0:T(2,128)} %get-tuple-element.34), calls=%async_computation.1 | async-start | bytes 262144 | tf_op jit(solution)/shard_map/all_to_all | solution.py:446

commit v9 on v8

--- a/solution.py
+++ b/solution.py
@@ -403,8 +403,7 @@
     slots = tile_vals.shape[2]
     tile = tile_vals[0, 0]
     residue = (hx_vec - x_vec * theta[:, None]) / precond[None, :]
-    live = jnp.arange(slots, dtype=jnp.int32) < tile_count[0, 0]
-    row_index = jnp.where(live, tile_rows[0, 0], -1)[None]
+    row_index = tile_rows[0, 0][None]
     col_index = tile_cols[0, 0][None]
     used = tile_count.reshape(1)
 

time: 95.3 us -> 95.4 us (level)
  transfers between devices with their start and end apart: 12 -> 12, of which waited for: 4 -> 4; matrix products, arithmetic and copies ran while one was open for 9% -> 8% of each run, Pallas kernels for 18% -> 18%
where the time goes in v9:
time: 95.4 us; the launch traced here: 95 us
  starting transfers between devices  43 us (45%)
  Pallas kernels  23.3 us (24%)
  waiting for transfers between devices  17.4 us (18%)
  local copies, waits for them, and re-layouts  8.39 us (9%)
  between operations  1.53 us (2%)
  other arithmetic  1.43 us (1%)
    all_to_all x1, starting transfers between devices, body(): parts = lax.all_to_all(tied[5], 'row', 0, 0, tiled=True)  23.4 us
    ppermute x7, starting transfers between devices, within(): lax.ppermute(block, 'row', [(i, (i // ring ^ flip) * ring + (i % ring + t...  10.3 us
    all_to_all x1, waiting for transfers between devices, body(): gram = lax.all_to_all(gram, BOTH, 0, 0, tiled=True)  8.71 us
    all_to_all x1, waiting for transfers between devices, body(): parts = lax.all_to_all(tied[5], 'row', 0, 0, tiled=True)  7.03 us
    all_to_all x1, starting transfers between devices, body(): gram = lax.all_to_all(gram, BOTH, 0, 0, tiled=True)  6.32 us
    pallas_call x1, Pallas kernels, backward(): pl.pallas_call(functools.partial(backward_kernel, vecs), out_shape=jax.Sh...  5.15 us
    pallas_call x1, Pallas kernels, forward(): pl.pallas_call(functools.partial(forward_kernel, vecs), out_shape=(jax.Sh...  5.12 us
    pallas_call x2, Pallas kernels, spread(): pl.pallas_call(spread_kernel, grid=(blocks // WIDTH,), out_shape=jax.Shap...  3.72 us
  transfers between devices with their start and end apart: 12, of which 4 were waited for; matrix products, arithmetic and copies ran while one was open for 8% of the time, Pallas kernels for 18%

profile of v9, /device:TPU:1, one launch (start us, length us, event | category | flops | bytes accessed | tf_op | source)
XLA Modules:
  0.0 95.0 jit_solution(7942341163403664287)
XLA Ops:
  0.6 1.2 %fusion.3 = (bf16[4,16384]{1,0:T(4,128)(2,1)S(1)}, f32[4,16384]{1,0:T(4,128)S(1)}) fusion(f32[16384]{0:T(1024)} %param.17, f32[4,16384]{1,0:T(4,128)} %refs_3_.1, f32[4,16384]{1,0:T(4,128)} %refs_0_, f32[4]{0:T(128)} %param.16), kind=kLoop, calls=%fused_computation.8 | loop fusion | flops 262144 | bytes 983056 | tf_op jit(solution)/shard_map/convert_element_type | solution.py:419
  1.9 0.3 reshape.32
  2.3 2.1 %collective-permute-start.2 = (bf16[256,256]{1,0:T(8,128)(2,1)S(1)}, bf16[256,256]{1,0:T(8,128)(2,1)S(1)}, u32[]{:S(2)}, u32[]{:S(2)}) collective-permute-start(bf16[256,256]{1,0:T(8,128)(2,1)S(1)} %bitcast.16), channel_id=1, source_target_pairs={{0,64},{16,80},{32,96},{48,112},{64,0},{80,16},{96,32},{112,48},{1... | collective-permute-start | bytes 393224 | tf_op jit(solution)/shard_map/ppermute | solution.py:415
  4.4 1.6 %collective-permute-start = (bf16[256,256]{1,0:T(8,128)(2,1)S(1)}, bf16[256,256]{1,0:T(8,128)(2,1)S(1)}, u32[]{:S(2)}, u32[]{:S(2)}) collective-permute-start(bf16[256,256]{1,0:T(8,128)(2,1)S(1)} %bitcast.17), channel_id=1, source_target_pairs={{0,16},{16,32},{32,48},{48,0},{64,80},{80,96},{96,112},{112,64},{1... | collective-permute-start | bytes 393224 | tf_op jit(solution)/shard_map/ppermute | solution.py:415
  6.0 2.1 %collective-permute-start.3 = (bf16[256,256]{1,0:T(8,128)(2,1)S(1)}, bf16[256,256]{1,0:T(8,128)(2,1)S(1)}, u32[]{:S(2)}, u32[]{:S(2)}) collective-permute-start(bf16[256,256]{1,0:T(8,128)(2,1)S(1)} %bitcast.18), channel_id=1, source_target_pairs={{0,48},{16,0},{32,16},{48,32},{64,112},{80,64},{96,80},{112,96},{1... | collective-permute-start | bytes 393224 | tf_op jit(solution)/shard_map/ppermute | solution.py:415
  8.2 1.3 %collective-permute-start.4 = (bf16[256,256]{1,0:T(8,128)(2,1)S(1)}, bf16[256,256]{1,0:T(8,128)(2,1)S(1)}, u32[]{:S(2)}, u32[]{:S(2)}) collective-permute-start(bf16[256,256]{1,0:T(8,128)(2,1)S(1)} %bitcast.19), channel_id=1, source_target_pairs={{0,32},{16,48},{32,0},{48,16},{64,96},{80,112},{96,64},{112,80},{1... | collective-permute-start | bytes 393224 | tf_op jit(solution)/shard_map/ppermute | solution.py:415
  9.5 0.7 collective-permute-start.5
  10.2 1.9 %collective-permute-start.6 = (bf16[256,256]{1,0:T(8,128)(2,1)S(1)}, bf16[256,256]{1,0:T(8,128)(2,1)S(1)}, u32[]{:S(2)}, u32[]{:S(2)}) collective-permute-start(bf16[256,256]{1,0:T(8,128)(2,1)S(1)} %collective-permute-done.2.refs_1_), channel_id=1, source_target_pairs={{0,48},{16,0},{32,16},{48,32},{64,112},{80,64},{96,80},{112,96},{1... | collective-permute-start | bytes 393224 | tf_op jit(solution)/shard_map/ppermute | solution.py:415
  12.1 0.5 collective-permute-start.7
  12.6 1.3 %collective-permute-start.1 = (s32[1,1024]{1,0:T(1,128)}, s32[1,1024]{1,0:T(1,128)S(1)}, u32[]{:S(2)}, u32[]{:S(2)}) collective-permute-start(s32[1,1024]{1,0:T(1,128)} %bitcast.32), channel_id=1, source_target_pairs={{0,0},{1,1},{2,2},{3,3},{4,4},{5,5},{6,6},{7,7},{8,8},{9,9},{10,10... | collective-permute-start | bytes 12296 | tf_op jit(solution)/shard_map/ppermute | solution.py:412
  14.7 0.4 collective-permute-done.4.refs_4_
  15.1 0.7 copy-done.6
  15.8 3.6 %early_pick.1 = (bf16[256,1024]{1,0:T(8,128)(2,1)S(1)}, bf16[512,4096]{1,0:T(8,128)(2,1)S(1)}) custom-call(s32[5]{0:T(128)S(1)} %bitcast.25, s32[1]{0:T(128)} %bitcast.13.count_ref, s32[1,1024]{1,0:T(1,128)S(1)} %bitcast.22, bf16[256,256]{1,0:T(8,128)(2,1)S(1)} %bitcast.20, bf16[256,256]{1,0:T(8,128)(2,1)S(1)} %collective-permute-done.2.refs_1_, ...), custom_call_target="tpu_custom_call" | custom-call | tf_op jit(solution)/shard_map/early_pick/pallas_call | solution.py:68
  19.4 1.3 %collective-permute-done.7.refs_7_.refs_2_ = bf16[256,256]{1,0:T(8,128)(2,1)S(1)} collective-permute-done((bf16[256,256]{1,0:T(8,128)(2,1)S(1)}, bf16[256,256]{1,0:T(8,128)(2,1)S(1)}, u32[]{:S(2)}, u32[]{:S(2)}) %collective-permute-start.7) | collective-permute-done | bytes 131104 | tf_op jit(solution)/shard_map/ppermute | solution.py:415
  20.7 1.8 %pick.1 = (bf16[256,1024]{1,0:T(8,128)(2,1)S(1)}, s32[1,1024]{1,0:T(1,128)S(1)}) custom-call(s32[8]{0:T(128)S(1)} %fusion.2.base_ref, s32[1,1024]{1,0:T(1,128)S(1)} %collective-permute-done.1.index_ref, bf16[256,256]{1,0:T(8,128)(2,1)S(1)} %bitcast.21, bf16[256,256]{1,0:T(8,128)(2,1)S(1)} %collective-permute-done.2.refs_1_, ...), custom_call_target="tpu_custom_call" | custom-call | tf_op jit(solution)/shard_map/pick/pallas_call | solution.py:92
  22.5 0.7 collective-permute-start.9
  23.3 5.1 %forward.1 = (bf16[1024,256]{1,0:T(8,128)(2,1)S(1)}, bf16[512,4096]{1,0:T(8,128)(2,1)S(1)}) custom-call(s32[3]{0:T(128)S(1)} %slice.6.base_ref, s32[1]{0:T(128)} %bitcast.14.count_ref, s32[1,1024]{1,0:T(1,128)S(1)} %bitcast.23, bf16[256,1024]{1,0:T(8,128)(2,1)S(1)} %get-tuple-element.22.before_ref, ...), custom_call_target="tpu_custom_call" | custom-call | tf_op jit(solution)/shard_map/forward/pallas_call | solution.py:184
  28.4 0.9 collective-permute-start.8
  29.3 5.1 %backward.1.part_ref = bf16[1024,256]{1,0:T(8,128)(2,1)S(1)} custom-call(bf16[256,1024]{1,0:T(8,128)(2,1)S(1)} %collective-permute-done.9.y_ref, bf16[4096,256]{1,0:T(8,128)(2,1)S(1)} %copy-done.1, bf16[512,4096]{1,0:T(8,128)(2,1)S(1)} %get-tuple-element.23.refs_4_.half_ref, bf16[512,4096]{1,0:T(8,128)(2,1)S(1)} %get-tuple-element.26.rest_ref), custom_call_target="tpu_custom_call" | custom-call | tf_op jit(solution)/shard_map/backward/pallas_call | solution.py:243
  34.5 1.5 %spread.2.refs_0_ = f32[2048,256]{1,0:T(8,128)S(1)} custom-call(s32[1]{0:T(128)} %bitcast.15.count_ref, s32[1,1024]{1,0:T(1,128)S(1)} %bitcast.24, bf16[1024,256]{1,0:T(8,128)(2,1)S(1)} %backward.1.part_ref), custom_call_target="tpu_custom_call" | custom-call | tf_op jit(solution)/shard_map/spread/pallas_call | solution.py:269
  35.9 2.3 %spread.3 = bf16[2048,256]{1,0:T(8,128)(2,1)} custom-call(s32[1]{0:T(128)} %constant.44.clone.1.count_ref, s32[1,1024]{1,0:T(1,128)S(1)} %get-tuple-element.21.index_ref, bf16[1024,256]{1,0:T(8,128)(2,1)S(1)} %collective-permute-done.8.part_ref, f32[2048,256]{1,0:T(8,128)S(1)} %spread.2.refs_0_), custom_call_target="tpu_custom_call" | custom-call | tf_op jit(solution)/shard_map/spread/pallas_call | solution.py:269
  38.2 23.4 %all-to-all-start = ((bf16[8,256,256]{2,1,0:T(8,128)(2,1)}), bf16[8,256,256]{2,1,0:T(8,128)(2,1)S(1)}, u32[]{:S(2)}, u32[]{:S(2)}) async-start(bf16[8,256,256]{2,1,0:T(8,128)(2,1)} %bitcast.6), calls=%async_computation | async-start | bytes 2097152 | tf_op jit(solution)/shard_map/all_to_all | solution.py:442
  61.8 1.8 %reshape.36 = f32[12,256,64]{2,1,0:T(8,128)} reshape(f32[12,16384]{1,0:T(8,128)S(1)} %pad_maximum_fusion) | data formatting | bytes 1572864 | tf_op jit(solution)/shard_map/reshape | solution.py:441
  63.6 2.7 %copy.19 = f32[256,12,64]{0,2,1:T(8,128)} copy(f32[256,12,64]{2,0,1:T(8,128)} %bitcast.28) | data formatting | bytes 1572864 | tf_op jit(solution)/shard_map/transpose | solution.py:441
  66.4 1.4 %copy.20.vector_ref = f32[256,768]{1,0:T(8,128)S(1)} copy(f32[256,768]{0,1:T(8,128)} %bitcast.29) | data formatting | bytes 1572864 | tf_op jit(solution)/shard_map/reshape | solution.py:441
  67.8 1.8 %early_gram.1.early_ref = f32[2,128]{1,0:T(2,128)S(1)} custom-call(f32[4,16384]{1,0:T(4,128)S(1)} %copy-done, f32[4,16384]{1,0:T(4,128)S(1)} %get-tuple-element.29.refs_1_, f32[4,16384]{1,0:T(4,128)S(1)} %copy-done.3, f32[4,16384]{1,0:T(4,128)S(1)} %copy-done.2, f32[4,16384]{1,0:T(4,128)S(1)} %copy-done.4), custom_call_target="tpu_custom_call" | custom-call | tf_op jit(solution)/shard_map/early_gram/pallas_call | solution.py:294
  69.6 7.0 %all-to-all-done.part_ref = bf16[8,256,256]{2,1,0:T(8,128)(2,1)S(1)} async-done(((bf16[8,256,256]{2,1,0:T(8,128)(2,1)}), bf16[8,256,256]{2,1,0:T(8,128)(2,1)S(1)}, u32[]{:S(2)}, u32[]{:S(2)}) %all-to-all-start) | async-done | bytes 1048608 | tf_op jit(solution)/shard_map/all_to_all | solution.py:442
  76.6 1.2 %totalled.1 = (f32[256,256]{1,0:T(8,128)S(1)}, f32[128,2,128]{2,1,0:T(2,128)}) custom-call(bf16[8,256,256]{2,1,0:T(8,128)(2,1)S(1)} %all-to-all-done.part_ref, f32[256,768]{1,0:T(8,128)S(1)} %copy.20.vector_ref, f32[2,128]{1,0:T(2,128)S(1)} %early_gram.1.early_ref), custom_call_target="tpu_custom_call" | custom-call | tf_op jit(solution)/shard_map/totalled/pallas_call | solution.py:334
  77.8 6.3 %all-to-all-start.1 = ((f32[128,2,128]{2,1,0:T(2,128)}), f32[128,2,128]{2,1,0:T(2,128)S(1)}, u32[]{:S(2)}, u32[]{:S(2)}) async-start(f32[128,2,128]{2,1,0:T(2,128)} %get-tuple-element.34), calls=%async_computation.1 | async-start | bytes 262144 | tf_op jit(solution)/shard_map/all_to_all | solution.py:445
  84.5 0.9 reshape.39
  85.4 8.7 %all-to-all-done.1.gram_ref = f32[128,2,128]{2,1,0:T(2,128)S(1)} async-done(((f32[128,2,128]{2,1,0:T(2,128)}), f32[128,2,128]{2,1,0:T(2,128)S(1)}, u32[]{:S(2)}, u32[]{:S(2)}) %all-to-all-start.1) | async-done | bytes 131104 | tf_op jit(solution)/shard_map/all_to_all | solution.py:445
  94.1 0.9 unpacked.1
  (27 shorter events, 0.8 us)
Async XLA Ops:
  2.3 7.2 %collective-permute-start.2 = (bf16[256,256]{1,0:T(8,128)(2,1)S(1)}, bf16[256,256]{1,0:T(8,128)(2,1)S(1)}, u32[]{:S(2)}, u32[]{:S(2)}) collective-permute-start(bf16[256,256]{1,0:T(8,128)(2,1)S(1)} %bitcast.16), channel_id=1, source_target_pairs={{0,64},{16,80},{32,96},{48,112},{64,0},{80,16},{96,32},{112,48},{1... | collective-permute-start | bytes 393224 | tf_op jit(solution)/shard_map/ppermute | solution.py:415
  4.4 7.7 %collective-permute-start = (bf16[256,256]{1,0:T(8,128)(2,1)S(1)}, bf16[256,256]{1,0:T(8,128)(2,1)S(1)}, u32[]{:S(2)}, u32[]{:S(2)}) collective-permute-start(bf16[256,256]{1,0:T(8,128)(2,1)S(1)} %bitcast.17), channel_id=1, source_target_pairs={{0,16},{16,32},{32,48},{48,0},{64,80},{80,96},{96,112},{112,64},{1... | collective-permute-start | bytes 393224 | tf_op jit(solution)/shard_map/ppermute | solution.py:415
  6.0 6.6 %collective-permute-start.3 = (bf16[256,256]{1,0:T(8,128)(2,1)S(1)}, bf16[256,256]{1,0:T(8,128)(2,1)S(1)}, u32[]{:S(2)}, u32[]{:S(2)}) collective-permute-start(bf16[256,256]{1,0:T(8,128)(2,1)S(1)} %bitcast.18), channel_id=1, source_target_pairs={{0,48},{16,0},{32,16},{48,32},{64,112},{80,64},{96,80},{112,96},{1... | collective-permute-start | bytes 393224 | tf_op jit(solution)/shard_map/ppermute | solution.py:415
  8.2 6.9 %collective-permute-start.4 = (bf16[256,256]{1,0:T(8,128)(2,1)S(1)}, bf16[256,256]{1,0:T(8,128)(2,1)S(1)}, u32[]{:S(2)}, u32[]{:S(2)}) collective-permute-start(bf16[256,256]{1,0:T(8,128)(2,1)S(1)} %bitcast.19), channel_id=1, source_target_pairs={{0,32},{16,48},{32,0},{48,16},{64,96},{80,112},{96,64},{112,80},{1... | collective-permute-start | bytes 393224 | tf_op jit(solution)/shard_map/ppermute | solution.py:415
  9.5 9.9 %collective-permute-start.5 = (bf16[256,256]{1,0:T(8,128)(2,1)S(1)}, bf16[256,256]{1,0:T(8,128)(2,1)S(1)}, u32[]{:S(2)}, u32[]{:S(2)}) collective-permute-start(bf16[256,256]{1,0:T(8,128)(2,1)S(1)} %collective-permute-done.2.refs_1_), channel_id=1, source_target_pairs={{0,16},{16,32},{32,48},{48,0},{64,80},{80,96},{96,112},{112,64},{1... | collective-permute-start | bytes 393224 | tf_op jit(solution)/shard_map/ppermute | solution.py:415
  10.2 9.2 %collective-permute-start.6 = (bf16[256,256]{1,0:T(8,128)(2,1)S(1)}, bf16[256,256]{1,0:T(8,128)(2,1)S(1)}, u32[]{:S(2)}, u32[]{:S(2)}) collective-permute-start(bf16[256,256]{1,0:T(8,128)(2,1)S(1)} %collective-permute-done.2.refs_1_), channel_id=1, source_target_pairs={{0,48},{16,0},{32,16},{48,32},{64,112},{80,64},{96,80},{112,96},{1... | collective-permute-start | bytes 393224 | tf_op jit(solution)/shard_map/ppermute | solution.py:415
  12.1 8.6 %collective-permute-start.7 = (bf16[256,256]{1,0:T(8,128)(2,1)S(1)}, bf16[256,256]{1,0:T(8,128)(2,1)S(1)}, u32[]{:S(2)}, u32[]{:S(2)}) collective-permute-start(bf16[256,256]{1,0:T(8,128)(2,1)S(1)} %collective-permute-done.2.refs_1_), channel_id=1, source_target_pairs={{0,32},{16,48},{32,0},{48,16},{64,96},{80,112},{96,64},{112,80},{1... | collective-permute-start | bytes 393224 | tf_op jit(solution)/shard_map/ppermute | solution.py:415
  12.6 6.8 %collective-permute-start.1 = (s32[1,1024]{1,0:T(1,128)}, s32[1,1024]{1,0:T(1,128)S(1)}, u32[]{:S(2)}, u32[]{:S(2)}) collective-permute-start(s32[1,1024]{1,0:T(1,128)} %bitcast.32), channel_id=1, source_target_pairs={{0,0},{1,1},{2,2},{3,3},{4,4},{5,5},{6,6},{7,7},{8,8},{9,9},{10,10... | collective-permute-start | bytes 12296 | tf_op jit(solution)/shard_map/ppermute | solution.py:412
  15.1 0.7 copy-start.6
  15.8 7.5 %copy-start.5 = (bf16[256,256]{1,0:T(8,128)(2,1)S(1)}, bf16[256,256]{1,0:T(8,128)(2,1)}, u32[]{:S(2)}) copy-start(bf16[256,256]{1,0:T(8,128)(2,1)} %constant.56.clone.refs_3_) | copy-start | bytes 393220
  22.5 6.7 %collective-permute-start.9 = (bf16[256,1024]{1,0:T(8,128)(2,1)S(1)}, bf16[256,1024]{1,0:T(8,128)(2,1)S(1)}, u32[]{:S(2)}, u32[]{:S(2)}) collective-permute-start(bf16[256,1024]{1,0:T(8,128)(2,1)S(1)} %get-tuple-element.25), channel_id=1, source_target_pairs={{0,0},{1,1},{2,2},{3,3},{4,4},{5,5},{6,6},{7,7},{8,8},{9,9},{10,10... | collective-permute-start | bytes 1572872 | tf_op jit(solution)/shard_map/ppermute | solution.py:412
  23.2 6.0 %copy-start.1 = (bf16[4096,256]{1,0:T(8,128)(2,1)S(1)}, bf16[4096,256]{1,0:T(8,128)(2,1)}, u32[]{:S(2)}) copy-start(bf16[4096,256]{1,0:T(8,128)(2,1)} %constant.57.clone.route_ref) | copy-start | bytes 6291460
  28.4 7.5 %collective-permute-start.8 = (bf16[1024,256]{1,0:T(8,128)(2,1)S(1)}, bf16[1024,256]{1,0:T(8,128)(2,1)S(1)}, u32[]{:S(2)}, u32[]{:S(2)}) collective-permute-start(bf16[1024,256]{1,0:T(8,128)(2,1)S(1)} %get-tuple-element.24), channel_id=1, source_target_pairs={{0,0},{1,1},{2,2},{3,3},{4,4},{5,5},{6,6},{7,7},{8,8},{9,9},{10,10... | collective-permute-start | bytes 1572872 | tf_op jit(solution)/shard_map/ppermute | solution.py:412
  34.4 27.2 %copy-start = (f32[4,16384]{1,0:T(4,128)S(1)}, f32[4,16384]{1,0:T(4,128)}, u32[]{:S(2)}) copy-start(f32[4,16384]{1,0:T(4,128)} %refs_0_) | copy-start | bytes 786436
  34.4 27.2 %copy-start.3 = (f32[4,16384]{1,0:T(4,128)S(1)}, f32[4,16384]{1,0:T(4,128)}, u32[]{:S(2)}) copy-start(f32[4,16384]{1,0:T(4,128)} %refs_2_) | copy-start | bytes 786436
  38.2 38.4 %all-to-all-start = ((bf16[8,256,256]{2,1,0:T(8,128)(2,1)}), bf16[8,256,256]{2,1,0:T(8,128)(2,1)S(1)}, u32[]{:S(2)}, u32[]{:S(2)}) async-start(bf16[8,256,256]{2,1,0:T(8,128)(2,1)} %bitcast.6), calls=%async_computation | async-start | bytes 2097152 | tf_op jit(solution)/shard_map/all_to_all | solution.py:442
  61.6 6.2 %copy-start.2 = (f32[4,16384]{1,0:T(4,128)S(1)}, f32[4,16384]{1,0:T(4,128)}, u32[]{:S(2)}) copy-start(f32[4,16384]{1,0:T(4,128)} %refs_3_.1) | copy-start | bytes 786436
  61.6 6.2 %copy-start.4 = (f32[4,16384]{1,0:T(4,128)S(1)}, f32[4,16384]{1,0:T(4,128)}, u32[]{:S(2)}) copy-start(f32[4,16384]{1,0:T(4,128)} %refs_4_) | copy-start | bytes 786436
  77.8 16.3 %all-to-all-start.1 = ((f32[128,2,128]{2,1,0:T(2,128)}), f32[128,2,128]{2,1,0:T(2,128)S(1)}, u32[]{:S(2)}, u32[]{:S(2)}) async-start(f32[128,2,128]{2,1,0:T(2,128)} %get-tuple-element.34), calls=%async_computation.1 | async-start | bytes 262144 | tf_op jit(solution)/shard_map/all_to_all | solution.py:445
